TPU v7x, 256 devices: a whole 4x4x8 slice. The times are simulated.
256 devices in a mesh: fsdp: 8 (over z), expert: 32 (over x, y, core).
Axes of the slice: x: 4, y: 4, z: 8, core: 2. Of those that a mesh axis runs over, the one named last changes fastest.
Arguments:
- x_quant: bfloat16 [32768, 6144], P(('fsdp', 'expert')), may hold values from -6 to 6
- x_scale: float32 [32768, 48], P(('fsdp', 'expert')), may hold values from 0.3 to 3
- grad_out: bfloat16 [32768, 6144], P(('fsdp', 'expert')), may hold values from -6 to 6
- route_mask: int32 [32768], P(('fsdp', 'expert')), may hold values from 0 to 1, as said below
- route_prob: bfloat16 [32768], P(('fsdp', 'expert')), may hold values from 0.19921875 to 0.8984375
- gate_quant: bfloat16 [6144, 8192], P('fsdp', 'expert'), may hold values from -0.078125 to 0.078125
- gate_scale: float32 [48, 64], P('fsdp', 'expert'), may hold values from 0.5 to 2
- up_quant: bfloat16 [6144, 8192], P('fsdp', 'expert'), may hold values from -0.078125 to 0.078125
- up_scale: float32 [48, 64], P('fsdp', 'expert'), may hold values from 0.5 to 2
- down_quant: bfloat16 [8192, 6144], P('expert', 'fsdp'), may hold values from -0.0625 to 0.0625
- down_scale: float32 [64, 48], P('expert', 'fsdp'), may hold values from 0.5 to 2
Outputs:
- grad_x: bfloat16 [32768, 6144], P(('fsdp', 'expert'))
- grad_prob: float32 [32768], P(('fsdp', 'expert'))
- grad_gate: float32 [6144, 8192], P('fsdp', 'expert')
- grad_up: float32 [6144, 8192], P('fsdp', 'expert')
- grad_down: float32 [8192, 6144], P('expert', 'fsdp')
Inputs may be any that keep to these rules, and one draw needn't show every extreme that they name: `route_mask`: each block of 128 consecutive tokens (the tokens of one device) has 1 to 8 routed tokens; in every draw there is a run of 32 consecutive blocks (one index of fsdp) in which every block has exactly 8.
All inputs are finite; a program needn't handle non-finite values.
Results may differ from a plain program's by a relative error of at most 0.015.
Values may be sent and summed in bfloat16 or wider, within the bound.
No kernel may reach another device: no remote copies, remote signals or barrier semaphores. Data moves between devices by JAX's collectives and lax.ppermute only.
A program may use at most 128 MiB of HBM per device.

v0:
```python
import jax
import jax.numpy as jnp
from jax import lax
from jax.experimental import pallas as pl
from jax.experimental.pallas import tpu as pltpu
from jax.sharding import Mesh
from jax.sharding import PartitionSpec as P

CAP = 8
PLANE = ("x", "y")
EXPERT = ("x", "y", "core")
CORE_FIRST = ("core", "x", "y")
LANES = 128
BLOCK = 128
BF16 = jnp.bfloat16
F32 = jnp.float32


def contract(left, right, left_dim, right_dim):
    return lax.dot_general(
        left, right, (((left_dim,), (right_dim,)), ((), ())), preferred_element_type=F32
    )


def kernel_call(body, outs, limit, scalars=0, **specs):
    grid_spec = pltpu.PrefetchScalarGridSpec(num_scalar_prefetch=scalars, grid=(1,), **specs)
    return pl.pallas_call(
        body,
        out_shape=outs,
        grid_spec=grid_spec,
        compiler_params=pltpu.CompilerParams(vmem_limit_bytes=limit << 20),
    )


def whole(shape):
    return pl.BlockSpec(shape, lambda *_: (0,) * len(shape), pipeline_mode=pl.Buffered(1))


def block_at(shape, where):
    return pl.BlockSpec(shape, lambda *_: where, pipeline_mode=pl.Buffered(1))


def two_lanes(column):
    high = column.astype(BF16).astype(F32)
    lane = lax.broadcasted_iota(jnp.int32, (column.shape[0], LANES), 1)
    spread = jnp.where(lane == 0, high, jnp.where(lane == 1, column - high, 0.0))
    return spread.astype(BF16)


def scaled_weights(gate_quant, gate_scale, up_quant, up_scale, down_quant, down_scale):
    part, units = gate_quant.shape

    def put(out, quant, scale, shift):
        tall, broad = quant.shape[0] // BLOCK, quant.shape[1] // BLOCK
        for i in range(tall):
            for j in range(broad):
                rows, cols = slice(i * BLOCK, (i + 1) * BLOCK), slice(j * BLOCK, (j + 1) * BLOCK)
                out[rows, shift + j * BLOCK : shift + (j + 1) * BLOCK] = (
                    quant[rows, cols].astype(F32) * scale[i, j]
                ).astype(BF16)

    def body(gate, up, down, gate_s, up_s, down_s, gate_up_out, down_out):
        put(gate_up_out, gate, gate_s, 0)
        put(gate_up_out, up, up_s, units)
        put(down_out, down, down_s, 0)

    quants, scales = [gate_quant, up_quant, down_quant], [gate_scale, up_scale, down_scale]
    shapes = ((part, 2 * units), down_quant.shape)
    return kernel_call(
        body,
        tuple(jax.ShapeDtypeStruct(v, BF16) for v in shapes),
        16,
        in_specs=[whole(v.shape) for v in quants]
        + [pl.BlockSpec(memory_space=pltpu.SMEM)] * 3,
        out_specs=tuple(whole(v) for v in shapes),
    )(*quants, *scales)


def pre_sums(rows, gate_up_parts, down_parts):
    count = len(gate_up_parts)
    part, both = gate_up_parts[0][3].shape
    units = both // 2
    width = (rows.shape[1] - LANES) // 2
    places = [r for r, _, _, _ in gate_up_parts]
    assert places == [r for r, _, _, _ in down_parts]

    def body(rows_ref, *refs):
        out = refs[-1]
        pre = back = None
        for i, r in enumerate(places):
            x = rows_ref[:, r * part : (r + 1) * part]
            dy = rows_ref[:, width + r * part : width + (r + 1) * part]
            one = contract(x, refs[i][...], 1, 0)
            two = contract(dy, refs[count + i][...], 1, 1)
            pre = one if pre is None else pre + one
            back = two if back is None else back + two
        out[:, :both] = pre
        out[:, both:] = back

    weights = [p[3] for p in gate_up_parts] + [p[3] for p in down_parts]
    shape = (rows.shape[0], both + units)
    return kernel_call(
        body,
        jax.ShapeDtypeStruct(shape, F32),
        40,
        in_specs=[whole(v.shape) for v in [rows] + weights],
        out_specs=whole(shape),
    )(rows, *weights)


def activations(rows, sums, gate_up_parts, down_parts):
    count = rows.shape[0]
    both = gate_up_parts[0][3].shape[1]
    units = both // 2
    far = gate_up_parts[0][0]
    part = sum(b - a for _, a, b, _ in gate_up_parts)
    width = (rows.shape[1] - LANES) // 2

    def body(x_ref, dy_ref, prob_ref, sums_ref, wa, wb, da, db, acts_ref, prob_out):
        half = part // 2
        pre = sums_ref[:, :both]
        pre = pre + contract(x_ref[:, :half], wa[...], 1, 0)
        pre = pre + contract(x_ref[:, half:], wb[...], 1, 0)
        back = jnp.concatenate(
            [contract(dy_ref[...], da[...], 1, 1), contract(dy_ref[...], db[...], 1, 1)], axis=1
        )
        back = sums_ref[:, both:] + back
        gate_pre, up_pre = pre[:, :units], pre[:, units:]
        sigmoid_gate = jax.nn.sigmoid(gate_pre)
        hidden = (gate_pre * sigmoid_gate * up_pre).astype(BF16)
        prob_part = jnp.sum(hidden.astype(F32) * back, axis=1, keepdims=True)
        grad_hidden = prob_ref[:, :1].astype(F32) * back
        acts_ref[:, :units] = (
            grad_hidden * up_pre * sigmoid_gate * (1.0 + gate_pre * (1.0 - sigmoid_gate))
        ).astype(BF16)
        acts_ref[:, units:both] = (grad_hidden * gate_pre * sigmoid_gate).astype(BF16)
        acts_ref[:, both:] = hidden
        prob_out[...] = two_lanes(prob_part)

    weights = [p[3] for p in gate_up_parts] + [p[3] for p in down_parts]
    acts_shape, prob_shape = (count, both + units), (count, LANES)
    return kernel_call(
        body,
        (jax.ShapeDtypeStruct(acts_shape, BF16), jax.ShapeDtypeStruct(prob_shape, BF16)),
        32,
        in_specs=[
            block_at((count, part), (0, far)),
            block_at((count, part), (0, width // part + far)),
            block_at((count, LANES), (0, 2 * width // LANES)),
            whole(sums.shape),
        ]
        + [whole(v.shape) for v in weights],
        out_specs=(whole(acts_shape), whole(prob_shape)),
    )(rows, rows, rows, sums, *weights)


def slot_sums(core, acts, prob_lanes, gate_up_parts):
    half = acts.shape[0] // 2
    both = gate_up_parts[0][3].shape[1]
    part = gate_up_parts[0][2]
    width = sum(b - a for _, a, b, _ in gate_up_parts)
    places = [r * part + a for r, a, _, _ in gate_up_parts]

    def body(core_ref, acts_ref, prob_ref, *refs):
        for which, out in ((1 - core_ref[0], refs[-2]), (core_ref[0], refs[-1])):
            rows = pl.ds(pl.multiple_of(which * half, half), half)
            acts = acts_ref[rows, :both]
            for place, weight in zip(places, refs):
                out[:, place : place + weight.shape[0]] = contract(acts, weight[...], 1, 1).astype(
                    BF16
                )
            out[:, width:] = prob_ref[rows, :]

    weights = [p[3] for p in gate_up_parts]
    shape = (half, width + LANES)
    return kernel_call(
        body,
        (jax.ShapeDtypeStruct(shape, BF16),) * 2,
        40,
        scalars=1,
        in_specs=[whole(v.shape) for v in [acts, prob_lanes] + weights],
        out_specs=(whole(shape),) * 2,
    )(core, acts, prob_lanes, *weights)


def pair_sum(mine, other):
    width = mine.shape[1] - LANES

    def body(a_ref, b_ref, out):
        for at in range(0, width, 768):
            cols = slice(at, at + 768)
            out[:, cols] = (a_ref[:, cols].astype(F32) + b_ref[:, cols].astype(F32)).astype(BF16)
        lanes = a_ref[:, width:].astype(F32) + b_ref[:, width:].astype(F32)
        out[:, width:] = two_lanes(lanes[:, 0:1] + lanes[:, 1:2])

    return kernel_call(
        body,
        jax.ShapeDtypeStruct(mine.shape, BF16),
        16,
        in_specs=[whole(mine.shape)] * 2,
        out_specs=whole(mine.shape),
    )(mine, other)


def weight_sums(columns, act_parts):
    _, count, twice = columns.shape
    part = twice // 2
    wide = act_parts[0][3].shape[1]
    units = wide // 3
    places = [r for r, _, _, _ in act_parts]

    def body(cols_ref, *refs):
        gate_up = down = None
        for r, acts in zip(places, refs):
            one = contract(cols_ref[r, :, :part], acts[:, : 2 * units], 0, 0)
            two = contract(acts[:, 2 * units :], cols_ref[r, :, part:], 0, 0)
            gate_up = one if gate_up is None else gate_up + one
            down = two if down is None else down + two
        refs[-2][...] = gate_up
        refs[-1][...] = down

    shapes = ((part, 2 * units), (units, part))
    acts = [p[3] for p in act_parts]
    return kernel_call(
        body,
        tuple(jax.ShapeDtypeStruct(v, F32) for v in shapes),
        40,
        in_specs=[whole(v.shape) for v in [columns] + acts],
        out_specs=tuple(whole(v) for v in shapes),
    )(columns, *acts)


def last_weight_sums(columns, gate_up, down, act_parts):
    _, count, twice = columns.shape
    part = twice // 2
    units = down.shape[0]
    far = act_parts[0][0]

    def body(cols_ref, gate_up_ref, down_ref, aa, ab, gate_out, up_out, down_out):
        half = count // 2
        one, two = gate_up_ref[...], down_ref[...]
        for acts, rows in ((aa, slice(0, half)), (ab, slice(half, count))):
            one = one + contract(cols_ref[0, rows, :part], acts[:, : 2 * units], 0, 0)
            two = two + contract(acts[:, 2 * units :], cols_ref[0, rows, part:], 0, 0)
        gate_out[...] = one[:, :units]
        up_out[...] = one[:, units:]
        down_out[...] = two

    acts = [p[3] for p in act_parts]
    shapes = ((part, units), (part, units), (units, part))
    return kernel_call(
        body,
        tuple(jax.ShapeDtypeStruct(v, F32) for v in shapes),
        32,
        in_specs=[block_at((1, count, twice), (far, 0, 0))]
        + [whole(v.shape) for v in [gate_up, down] + acts],
        out_specs=tuple(whole(v) for v in shapes),
    )(columns, gate_up, down, *acts)


def turn(values, axis, place, size):
    flipped = jnp.flip(values, axis)
    twice = jnp.concatenate([flipped, flipped], axis)
    return lax.dynamic_slice_in_dim(twice, size - 1 - place, size, axis)


def ring_gather(block, axis, size):
    up = [(i, (i + 1) % size) for i in range(size)]
    down = [(i, (i - 1) % size) for i in range(size)]
    far = size // 2
    length = block.shape[0]
    near = [(0, 0, length, block)]
    ahead, behind = block, block
    for step in range(1, far):
        ahead = lax.ppermute(ahead, axis, up)
        behind = lax.ppermute(behind, axis, down)
        near.append((step, 0, length, ahead))
        near.append((size - step, 0, length, behind))
    half = length // 2
    ahead = lax.ppermute(ahead[:half], axis, up)
    behind = lax.ppermute(behind[half:], axis, down)
    return near, [(far, 0, half, ahead), (far, half, length, behind)]


def make_on_device(mesh):
    ring = mesh.shape["fsdp"]

    def on_device(
        x_quant,
        x_scale,
        grad_out,
        route_mask,
        route_prob,
        gate_quant,
        gate_scale,
        up_quant,
        up_scale,
        down_quant,
        down_scale,
    ):
        place = lax.axis_index("fsdp")
        core = lax.axis_index("core")
        width = x_quant.shape[1]
        part = width // ring

        w_gate_up, w_down = scaled_weights(
            gate_quant, gate_scale, up_quant, up_scale, down_quant, down_scale
        )
        down_near, down_far = ring_gather(w_down, "fsdp", ring)
        gate_up_near, gate_up_far = ring_gather(w_gate_up, "fsdp", ring)

        slot_rank = jnp.cumsum(route_mask) - 1
        slot_ids = jnp.arange(CAP, dtype=jnp.int32)
        table = ((slot_rank[None, :] == slot_ids[:, None]) & (route_mask[None, :] == 1)).astype(BF16)
        table_wide = table.astype(F32)
        blocks = x_scale.shape[1]
        slot_quant = jnp.dot(table, x_quant, preferred_element_type=F32)
        slot_scale = jnp.dot(
            table_wide, x_scale, precision=lax.Precision.HIGHEST, preferred_element_type=F32
        )
        slot_x = (
            (slot_quant.reshape(CAP, blocks, width // blocks) * slot_scale[:, :, None])
            .reshape(CAP, width)
            .astype(BF16)
        )
        slot_dy = jnp.dot(table, grad_out, preferred_element_type=F32).astype(BF16)
        slot_prob = jnp.sum(table_wide * route_prob.astype(F32)[None, :], axis=1)
        weighted = (slot_prob[:, None] * slot_dy.astype(F32)).astype(BF16)

        sides = jnp.concatenate(
            [slot_x.reshape(CAP, ring, part), weighted.reshape(CAP, ring, part)], axis=-1
        ).transpose(1, 0, 2)
        turned = turn(
            jnp.stack([slot_x, slot_dy]).reshape(2, CAP, ring, part), 2, place, ring
        ).reshape(2, CAP, width)
        packed = jnp.concatenate(
            [turned[0], turned[1], jnp.broadcast_to(slot_prob.astype(BF16)[:, None], (CAP, 128))],
            axis=1,
        )
        rows = lax.all_gather(packed, CORE_FIRST, axis=0, tiled=True)

        sides = lax.all_to_all(sides, "fsdp", split_axis=0, concat_axis=0, tiled=True)
        sides = turn(sides, 0, place, ring)
        columns = lax.all_gather(sides, CORE_FIRST, axis=1, tiled=True)

        sums = pre_sums(rows, gate_up_near, down_near)
        acts, prob_lanes = activations(rows, sums, gate_up_far, down_far)
        acts_near, acts_far = ring_gather(acts, "fsdp", ring)

        give, keep = slot_sums(core[None], acts, prob_lanes, gate_up_near + gate_up_far)
        got = lax.ppermute(give, "core", [(0, 1), (1, 0)])
        got, *_ = lax.optimization_barrier((got, acts_near[1][3], acts_near[2][3]))
        both = pair_sum(keep, got).reshape(-1, CAP, width + LANES)
        shares = lax.all_to_all(both, PLANE, split_axis=0, concat_axis=0, tiled=True)
        mine = jnp.sum(shares.astype(F32), axis=0)
        mine_grad = mine[:, :width].astype(BF16).reshape(CAP, ring, part)
        mine_grad = turn(mine_grad, 1, place, ring).reshape(CAP, width)
        mine_prob = mine[:, width] + mine[:, width + 1]
        grad_x = contract(table, mine_grad, 0, 0).astype(BF16)
        grad_prob = jnp.sum(table_wide * mine_prob[:, None], axis=0)

        gate_up, down = weight_sums(columns, acts_near)
        grad_gate, grad_up, grad_down = last_weight_sums(columns, gate_up, down, acts_far)
        return (grad_x, grad_prob, grad_gate, grad_up, grad_down)

    return on_device


def solution(mesh):
    devices = mesh.devices
    mesh = Mesh(devices.reshape(devices.shape[0], 4, 4, 2), ("fsdp", "x", "y", "core"))
    tokens = ("fsdp", "x", "y", "core")
    placed = (
        P(tokens, None),
        P(tokens, None),
        P(tokens, None),
        P(tokens),
        P(tokens),
        P("fsdp", EXPERT),
        P("fsdp", EXPERT),
        P("fsdp", EXPERT),
        P("fsdp", EXPERT),
        P(EXPERT, "fsdp"),
        P(EXPERT, "fsdp"),
    )
    return jax.shard_map(
        make_on_device(mesh),
        mesh=mesh,
        in_specs=placed,
        out_specs=(
            P(tokens, None),
            P(tokens),
            P("fsdp", EXPERT),
            P("fsdp", EXPERT),
            P(EXPERT, "fsdp"),
        ),
        check_vma=False,
    )
```

profile of v0, /device:TPU:1, one launch (start us, length us, event | category | flops | bytes accessed | tf_op | source)
XLA Modules:
  0.0 218.3 jit_solution(9935058963573242669)
XLA Ops:
  11.9 17.7 %all_to_all.10 = bf16[8,8,1536]{2,1,0:T(8,128)(2,1)S(1)} all-to-all(bf16[8,8,1536]{2,1,0:T(8,128)(2,1)S(1)} %maximum_bitcast_fusion), channel_id=1, replica_groups=mesh['fsdp'=8,'x'=4,'y'=4,'core'=2] {'fsdp'}, dimensions={0} | all-to-all | bytes 393216 | tf_op jit(solution)/shard_map/all_to_all | solution.py:342
  31.6 2.6 %collective-permute-start.1 = (bf16[768,512]{1,0:T(8,128)(2,1)S(1)}, bf16[768,512]{1,0:T(8,128)(2,1)S(1)}, u32[]{:S(2)}, u32[]{:S(2)}) collective-permute-start(bf16[768,512]{1,0:T(8,128)(2,1)S(1)} %get-tuple-element.17.refs_0_), channel_id=1, source_target_pairs={{0,224},{32,0},{64,32},{96,64},{128,96},{160,128},{192,160},{224,1... | collective-permute-start | bytes 2359304 | tf_op jit(solution)/shard_map/ppermute | solution.py:276
  34.3 15.0 %collective-permute-done.refs_1_ = bf16[768,512]{1,0:T(8,128)(2,1)S(1)} collective-permute-done((bf16[768,512]{1,0:T(8,128)(2,1)S(1)}, bf16[768,512]{1,0:T(8,128)(2,1)S(1)}, u32[]{:S(2)}, u32[]{:S(2)}) %collective-permute-start) | collective-permute-done | bytes 786464 | tf_op jit(solution)/shard_map/ppermute | solution.py:275
  50.1 2.7 %collective-permute-start.3 = (bf16[768,512]{1,0:T(8,128)(2,1)S(1)}, bf16[768,512]{1,0:T(8,128)(2,1)S(1)}, u32[]{:S(2)}, u32[]{:S(2)}) collective-permute-start(bf16[768,512]{1,0:T(8,128)(2,1)S(1)} %collective-permute-done.1.refs_2_), channel_id=1, source_target_pairs={{0,224},{32,0},{64,32},{96,64},{128,96},{160,128},{192,160},{224,1... | collective-permute-start | bytes 2359304 | tf_op jit(solution)/shard_map/ppermute | solution.py:276
  53.7 2.7 %collective-permute-start.7 = (bf16[256,768]{1,0:T(8,128)(2,1)S(1)}, bf16[256,768]{1,0:T(8,128)(2,1)S(1)}, u32[]{:S(2)}, u32[]{:S(2)}) collective-permute-start(bf16[256,768]{1,0:T(8,128)(2,1)S(1)} %get-tuple-element.18.refs_7_), channel_id=1, source_target_pairs={{0,224},{32,0},{64,32},{96,64},{128,96},{160,128},{192,160},{224,1... | collective-permute-start | bytes 1179656 | tf_op jit(solution)/shard_map/ppermute | solution.py:276
  57.1 9.0 %collective-permute-done.2.refs_3_ = bf16[768,512]{1,0:T(8,128)(2,1)S(1)} collective-permute-done((bf16[768,512]{1,0:T(8,128)(2,1)S(1)}, bf16[768,512]{1,0:T(8,128)(2,1)S(1)}, u32[]{:S(2)}, u32[]{:S(2)}) %collective-permute-start.2) | collective-permute-done | bytes 786464 | tf_op jit(solution)/shard_map/ppermute | solution.py:275
  66.9 2.7 %collective-permute-start.5 = (bf16[768,512]{1,0:T(8,128)(2,1)S(1)}, bf16[768,512]{1,0:T(8,128)(2,1)S(1)}, u32[]{:S(2)}, u32[]{:S(2)}) collective-permute-start(bf16[768,512]{1,0:T(8,128)(2,1)S(1)} %collective-permute-done.3.refs_4_), channel_id=1, source_target_pairs={{0,224},{32,0},{64,32},{96,64},{128,96},{160,128},{192,160},{224,1... | collective-permute-start | bytes 2359304 | tf_op jit(solution)/shard_map/ppermute | solution.py:276
  69.6 4.8 %collective-permute-done.6.refs_8_ = bf16[256,768]{1,0:T(8,128)(2,1)S(1)} collective-permute-done((bf16[256,768]{1,0:T(8,128)(2,1)S(1)}, bf16[256,768]{1,0:T(8,128)(2,1)S(1)}, u32[]{:S(2)}, u32[]{:S(2)}) %collective-permute-start.6) | collective-permute-done | bytes 393248 | tf_op jit(solution)/shard_map/ppermute | solution.py:275
  74.4 3.3 %collective-permute-start.9 = (bf16[256,768]{1,0:T(8,128)(2,1)S(1)}, bf16[256,768]{1,0:T(8,128)(2,1)S(1)}, u32[]{:S(2)}, u32[]{:S(2)}) collective-permute-start(bf16[256,768]{1,0:T(8,128)(2,1)S(1)} %collective-permute-done.7.refs_9_), channel_id=1, source_target_pairs={{0,224},{32,0},{64,32},{96,64},{128,96},{160,128},{192,160},{224,1... | collective-permute-start | bytes 1179656 | tf_op jit(solution)/shard_map/ppermute | solution.py:276
  78.4 21.2 %collective-permute-done.8.refs_10_ = bf16[256,768]{1,0:T(8,128)(2,1)S(1)} collective-permute-done((bf16[256,768]{1,0:T(8,128)(2,1)S(1)}, bf16[256,768]{1,0:T(8,128)(2,1)S(1)}, u32[]{:S(2)}, u32[]{:S(2)}) %collective-permute-start.8) | collective-permute-done | bytes 393248 | tf_op jit(solution)/shard_map/ppermute | solution.py:275
  100.4 2.7 %collective-permute-start.11 = (bf16[256,768]{1,0:T(8,128)(2,1)S(1)}, bf16[256,768]{1,0:T(8,128)(2,1)S(1)}, u32[]{:S(2)}, u32[]{:S(2)}) collective-permute-start(bf16[256,768]{1,0:T(8,128)(2,1)S(1)} %collective-permute-done.9.refs_11_), channel_id=1, source_target_pairs={{0,224},{32,0},{64,32},{96,64},{128,96},{160,128},{192,160},{224,1... | collective-permute-start | bytes 1179656 | tf_op jit(solution)/shard_map/ppermute | solution.py:276
  105.4 2.7 %collective-permute-start.13 = (bf16[384,512]{1,0:T(8,128)(2,1)}, bf16[384,512]{1,0:T(8,128)(2,1)}, u32[]{:S(2)}, u32[]{:S(2)}) collective-permute-start(bf16[384,512]{1,0:T(8,128)(2,1)} %slice.50), channel_id=1, source_target_pairs={{0,224},{32,0},{64,32},{96,64},{128,96},{160,128},{192,160},{224,1... | collective-permute-start | bytes 1179656 | tf_op jit(solution)/shard_map/ppermute | solution.py:281
  111.0 2.7 %collective-permute-start.15 = (bf16[128,768]{1,0:T(8,128)(2,1)}, bf16[128,768]{1,0:T(8,128)(2,1)}, u32[]{:S(2)}, u32[]{:S(2)}) collective-permute-start(bf16[128,768]{1,0:T(8,128)(2,1)} %slice.52), channel_id=1, source_target_pairs={{0,224},{32,0},{64,32},{96,64},{128,96},{160,128},{192,160},{224,1... | collective-permute-start | bytes 589832 | tf_op jit(solution)/shard_map/ppermute | solution.py:281
  126.5 5.2 %shard_map.147.sums_ref = f32[256,768]{1,0:T(8,128)S(1)} custom-call(bf16[256,12416]{1,0:T(8,128)(2,1)} %all-gather.3.cloned.1.call-done.rows_ref.x_ref.dy_ref.prob_ref, bf16[768,512]{1,0:T(8,128)(2,1)S(1)} %copy-done.5, bf16[768,512]{1,0:T(8,128)(2,1)S(1)} %copy-done.8, bf16[768,512]{1,0:T(8,128)(2,1)S(1)} %copy-done.11, bf16[768,512]{1,0:T(8,128)(2,1)S(1)} %copy-done.14, ...), custom_call_target="tpu_custom_call" | custom-call | tf_op jit(solution)/shard_map/pallas_call | solution.py:102
  132.6 1.5 copy-done.20
  134.0 2.0 shard_map.148
  136.1 5.1 %shard_map.149 = (bf16[128,6272]{1,0:T(8,128)(2,1)S(1)}, bf16[128,6272]{1,0:T(8,128)(2,1)S(1)}) custom-call(s32[1]{0:T(128)} %bitcast.1.core_ref, bf16[256,768]{1,0:T(8,128)(2,1)S(1)} %get-tuple-element.19.acts_ref.refs_0_, bf16[256,128]{1,0:T(8,128)(2,1)S(1)} %get-tuple-element.20.prob_ref, bf16[768,512]{1,0:T(8,128)(2,1)S(1)} %copy-done.6, ...), custom_call_target="tpu_custom_call" | custom-call | tf_op jit(solution)/shard_map/pallas_call | solution.py:176
  141.2 9.6 %collective-permute-start.16 = (bf16[128,6272]{1,0:T(8,128)(2,1)S(1)}, bf16[128,6272]{1,0:T(8,128)(2,1)S(1)}, u32[]{:S(2)}, u32[]{:S(2)}) collective-permute-start(bf16[128,6272]{1,0:T(8,128)(2,1)S(1)} %get-tuple-element.22), channel_id=1, source_target_pairs={{0,1},{1,0},{2,3},{3,2},{4,5},{5,4},{6,7},{7,6},{8,9},{9,8},{10,11... | collective-permute-start | bytes 4816904 | tf_op jit(solution)/shard_map/ppermute | solution.py:351
  150.8 2.7 %collective-permute-start.18 = (bf16[256,768]{1,0:T(8,128)(2,1)S(1)}, bf16[256,768]{1,0:T(8,128)(2,1)S(1)}, u32[]{:S(2)}, u32[]{:S(2)}) collective-permute-start(bf16[256,768]{1,0:T(8,128)(2,1)S(1)} %get-tuple-element.19.acts_ref.refs_0_), channel_id=1, source_target_pairs={{0,224},{32,0},{64,32},{96,64},{128,96},{160,128},{192,160},{224,1... | collective-permute-start | bytes 1179656 | tf_op jit(solution)/shard_map/ppermute | solution.py:276
  153.5 9.2 %collective-permute-done.17.refs_1_ = bf16[256,768]{1,0:T(8,128)(2,1)S(1)} collective-permute-done((bf16[256,768]{1,0:T(8,128)(2,1)S(1)}, bf16[256,768]{1,0:T(8,128)(2,1)S(1)}, u32[]{:S(2)}, u32[]{:S(2)}) %collective-permute-start.17) | collective-permute-done | bytes 393248 | tf_op jit(solution)/shard_map/ppermute | solution.py:275
  162.7 1.9 shard_map.150
  164.5 6.8 %all-to-all-start = ((bf16[16,8,6272]{2,1,0:T(8,128)(2,1)}), bf16[16,8,6272]{2,1,0:T(8,128)(2,1)}, u32[]{:S(2)}, u32[]{:S(2)}) async-start(bf16[16,8,6272]{2,1,0:T(8,128)(2,1)} %bitcast.7), calls=%async_computation | async-start | bytes 3211264 | tf_op jit(solution)/shard_map/all_to_all | solution.py:354
  171.5 2.7 %collective-permute-start.20 = (bf16[256,768]{1,0:T(8,128)(2,1)S(1)}, bf16[256,768]{1,0:T(8,128)(2,1)S(1)}, u32[]{:S(2)}, u32[]{:S(2)}) collective-permute-start(bf16[256,768]{1,0:T(8,128)(2,1)S(1)} %collective-permute-done.18.refs_2_), channel_id=1, source_target_pairs={{0,224},{32,0},{64,32},{96,64},{128,96},{160,128},{192,160},{224,1... | collective-permute-start | bytes 1179656 | tf_op jit(solution)/shard_map/ppermute | solution.py:276
  174.1 8.1 %collective-permute-done.19.refs_3_ = bf16[256,768]{1,0:T(8,128)(2,1)S(1)} collective-permute-done((bf16[256,768]{1,0:T(8,128)(2,1)S(1)}, bf16[256,768]{1,0:T(8,128)(2,1)S(1)}, u32[]{:S(2)}, u32[]{:S(2)}) %collective-permute-start.19) | collective-permute-done | bytes 393248 | tf_op jit(solution)/shard_map/ppermute | solution.py:275
  183.0 2.7 %collective-permute-start.22 = (bf16[256,768]{1,0:T(8,128)(2,1)S(1)}, bf16[256,768]{1,0:T(8,128)(2,1)S(1)}, u32[]{:S(2)}, u32[]{:S(2)}) collective-permute-start(bf16[256,768]{1,0:T(8,128)(2,1)S(1)} %collective-permute-done.20.refs_4_), channel_id=1, source_target_pairs={{0,224},{32,0},{64,32},{96,64},{128,96},{160,128},{192,160},{224,1... | collective-permute-start | bytes 1179656 | tf_op jit(solution)/shard_map/ppermute | solution.py:276
  185.7 6.5 %collective-permute-done.21.refs_5_ = bf16[256,768]{1,0:T(8,128)(2,1)S(1)} collective-permute-done((bf16[256,768]{1,0:T(8,128)(2,1)S(1)}, bf16[256,768]{1,0:T(8,128)(2,1)S(1)}, u32[]{:S(2)}, u32[]{:S(2)}) %collective-permute-start.21) | collective-permute-done | bytes 393248 | tf_op jit(solution)/shard_map/ppermute | solution.py:275
  193.6 2.7 %collective-permute-start.24 = (bf16[128,768]{1,0:T(8,128)(2,1)}, bf16[128,768]{1,0:T(8,128)(2,1)}, u32[]{:S(2)}, u32[]{:S(2)}) collective-permute-start(bf16[128,768]{1,0:T(8,128)(2,1)} %slice.57), channel_id=1, source_target_pairs={{0,224},{32,0},{64,32},{96,64},{128,96},{160,128},{192,160},{224,1... | collective-permute-start | bytes 589832 | tf_op jit(solution)/shard_map/ppermute | solution.py:281
  196.3 2.8 %copy-done.2 = bf16[8,256,1536]{2,1,0:T(8,128)(2,1)S(1)} copy-done((bf16[8,256,1536]{2,1,0:T(8,128)(2,1)S(1)}, bf16[8,256,1536]{2,1,0:T(8,128)(2,1)}, u32[]{:S(2)}) %copy-start.2) | copy-done | bytes 6291480
  201.0 2.4 %shard_map.151 = (f32[768,512]{1,0:T(8,128)S(1)}, f32[256,768]{1,0:T(8,128)S(1)}) custom-call(bf16[8,256,1536]{2,1,0:T(8,128)(2,1)S(1)} %copy-done.2, bf16[256,768]{1,0:T(8,128)(2,1)S(1)} %get-tuple-element.19.acts_ref.refs_0_, bf16[256,768]{1,0:T(8,128)(2,1)S(1)} %collective-permute-done.17.refs_1_, bf16[256,768]{1,0:T(8,128)(2,1)S(1)} %collective-permute-done.18.refs_2_, ...), custom_call_target="tpu_custom_call" | custom-call | tf_op jit(solution)/shard_map/pallas_call | solution.py:224
  203.8 3.1 %shard_map.152 = (f32[768,256]{1,0:T(8,128)}, f32[768,256]{1,0:T(8,128)}, f32[256,768]{1,0:T(8,128)}) custom-call(bf16[8,256,1536]{2,1,0:T(8,128)(2,1)S(1)} %copy-done.3, f32[768,512]{1,0:T(8,128)S(1)} %get-tuple-element.24.gate_up_ref, f32[256,768]{1,0:T(8,128)S(1)} %get-tuple-element.25.down_ref, bf16[128,768]{1,0:T(8,128)(2,1)} %collective-permute-done.23.aa, ...), custom_call_target="tpu_custom_call" | custom-call | tf_op jit(solution)/shard_map/pallas_call | solution.py:251
  206.9 1.7 convert_reduce_fusion
  209.1 1.8 convolution_convert_fusion
  (166 shorter events, 36.1 us)
Async XLA Ops:
  7.2 106.5 %all-gather.3.cloned.1.call-start = ((), (), s32[]{:S(2)}) async-start(), calls=%async_computation.2 | async-start | bytes 6555648 | tf_op jit(solution)/shard_map/all_gather | solution.py:340
  10.9 19.7 %copy-start.30 = (bf16[768,256]{1,0:T(8,128)(2,1)S(1)}, bf16[768,256]{1,0:T(8,128)(2,1)}, u32[]{:S(2)}) copy-start(bf16[768,256]{1,0:T(8,128)(2,1)} %gate.1) | copy-start | bytes 1179652
  11.8 184.4 %all-gather.5.cloned.1.call-start = ((), (), s32[]{:S(2)}) async-start(), calls=%async_computation.3 | async-start | bytes 6488064 | tf_op jit(solution)/shard_map/all_gather | solution.py:344
  31.5 73.1 %copy-start.4 = (bf16[768,512]{1,0:T(8,128)(2,1)}, bf16[768,512]{1,0:T(8,128)(2,1)S(1)}, u32[]{:S(2)}) copy-start(bf16[768,512]{1,0:T(8,128)(2,1)S(1)} %get-tuple-element.17.refs_0_) | copy-start | bytes 2359300
  31.5 17.7 %collective-permute-start = (bf16[768,512]{1,0:T(8,128)(2,1)S(1)}, bf16[768,512]{1,0:T(8,128)(2,1)S(1)}, u32[]{:S(2)}, u32[]{:S(2)}) collective-permute-start(bf16[768,512]{1,0:T(8,128)(2,1)S(1)} %get-tuple-element.17.refs_0_), channel_id=1, source_target_pairs={{0,32},{32,64},{64,96},{96,128},{128,160},{160,192},{192,224},{224... | collective-permute-start | bytes 2359304 | tf_op jit(solution)/shard_map/ppermute | solution.py:275
  31.6 18.5 %collective-permute-start.1 = (bf16[768,512]{1,0:T(8,128)(2,1)S(1)}, bf16[768,512]{1,0:T(8,128)(2,1)S(1)}, u32[]{:S(2)}, u32[]{:S(2)}) collective-permute-start(bf16[768,512]{1,0:T(8,128)(2,1)S(1)} %get-tuple-element.17.refs_0_), channel_id=1, source_target_pairs={{0,224},{32,0},{64,32},{96,64},{128,96},{160,128},{192,160},{224,1... | collective-permute-start | bytes 2359304 | tf_op jit(solution)/shard_map/ppermute | solution.py:276
  49.2 16.8 %collective-permute-start.2 = (bf16[768,512]{1,0:T(8,128)(2,1)S(1)}, bf16[768,512]{1,0:T(8,128)(2,1)S(1)}, u32[]{:S(2)}, u32[]{:S(2)}) collective-permute-start(bf16[768,512]{1,0:T(8,128)(2,1)S(1)} %collective-permute-done.refs_1_), channel_id=1, source_target_pairs={{0,32},{32,64},{64,96},{96,128},{128,160},{160,192},{192,224},{224... | collective-permute-start | bytes 2359304 | tf_op jit(solution)/shard_map/ppermute | solution.py:275
  50.1 16.8 %collective-permute-start.3 = (bf16[768,512]{1,0:T(8,128)(2,1)S(1)}, bf16[768,512]{1,0:T(8,128)(2,1)S(1)}, u32[]{:S(2)}, u32[]{:S(2)}) collective-permute-start(bf16[768,512]{1,0:T(8,128)(2,1)S(1)} %collective-permute-done.1.refs_2_), channel_id=1, source_target_pairs={{0,224},{32,0},{64,32},{96,64},{128,96},{160,128},{192,160},{224,1... | collective-permute-start | bytes 2359304 | tf_op jit(solution)/shard_map/ppermute | solution.py:276
  53.7 20.7 %collective-permute-start.6 = (bf16[256,768]{1,0:T(8,128)(2,1)S(1)}, bf16[256,768]{1,0:T(8,128)(2,1)S(1)}, u32[]{:S(2)}, u32[]{:S(2)}) collective-permute-start(bf16[256,768]{1,0:T(8,128)(2,1)S(1)} %get-tuple-element.18.refs_7_), channel_id=1, source_target_pairs={{0,32},{32,64},{64,96},{96,128},{128,160},{160,192},{192,224},{224... | collective-permute-start | bytes 1179656 | tf_op jit(solution)/shard_map/ppermute | solution.py:275
  53.7 20.7 %collective-permute-start.7 = (bf16[256,768]{1,0:T(8,128)(2,1)S(1)}, bf16[256,768]{1,0:T(8,128)(2,1)S(1)}, u32[]{:S(2)}, u32[]{:S(2)}) collective-permute-start(bf16[256,768]{1,0:T(8,128)(2,1)S(1)} %get-tuple-element.18.refs_7_), channel_id=1, source_target_pairs={{0,224},{32,0},{64,32},{96,64},{128,96},{160,128},{192,160},{224,1... | collective-permute-start | bytes 1179656 | tf_op jit(solution)/shard_map/ppermute | solution.py:276
  66.1 37.8 %collective-permute-start.4 = (bf16[768,512]{1,0:T(8,128)(2,1)S(1)}, bf16[768,512]{1,0:T(8,128)(2,1)S(1)}, u32[]{:S(2)}, u32[]{:S(2)}) collective-permute-start(bf16[768,512]{1,0:T(8,128)(2,1)S(1)} %collective-permute-done.2.refs_3_), channel_id=1, source_target_pairs={{0,32},{32,64},{64,96},{96,128},{128,160},{160,192},{192,224},{224... | collective-permute-start | bytes 2359304 | tf_op jit(solution)/shard_map/ppermute | solution.py:275
  66.9 38.5 %copy-start.16 = (bf16[768,512]{1,0:T(8,128)(2,1)}, bf16[768,512]{1,0:T(8,128)(2,1)S(1)}, u32[]{:S(2)}) copy-start(bf16[768,512]{1,0:T(8,128)(2,1)S(1)} %collective-permute-done.3.refs_4_) | copy-start | bytes 2359300
  66.9 37.7 %collective-permute-start.5 = (bf16[768,512]{1,0:T(8,128)(2,1)S(1)}, bf16[768,512]{1,0:T(8,128)(2,1)S(1)}, u32[]{:S(2)}, u32[]{:S(2)}) collective-permute-start(bf16[768,512]{1,0:T(8,128)(2,1)S(1)} %collective-permute-done.3.refs_4_), channel_id=1, source_target_pairs={{0,224},{32,0},{64,32},{96,64},{128,96},{160,128},{192,160},{224,1... | collective-permute-start | bytes 2359304 | tf_op jit(solution)/shard_map/ppermute | solution.py:276
  74.4 35.8 %copy-start.35 = (bf16[256,768]{1,0:T(8,128)(2,1)}, bf16[256,768]{1,0:T(8,128)(2,1)S(1)}, u32[]{:S(2)}) copy-start(bf16[256,768]{1,0:T(8,128)(2,1)S(1)} %collective-permute-done.6.refs_8_) | copy-start | bytes 1179652
  74.4 25.3 %collective-permute-start.8 = (bf16[256,768]{1,0:T(8,128)(2,1)S(1)}, bf16[256,768]{1,0:T(8,128)(2,1)S(1)}, u32[]{:S(2)}, u32[]{:S(2)}) collective-permute-start(bf16[256,768]{1,0:T(8,128)(2,1)S(1)} %collective-permute-done.6.refs_8_), channel_id=1, source_target_pairs={{0,32},{32,64},{64,96},{96,128},{128,160},{160,192},{192,224},{224... | collective-permute-start | bytes 1179656 | tf_op jit(solution)/shard_map/ppermute | solution.py:275
  74.4 26.0 %collective-permute-start.9 = (bf16[256,768]{1,0:T(8,128)(2,1)S(1)}, bf16[256,768]{1,0:T(8,128)(2,1)S(1)}, u32[]{:S(2)}, u32[]{:S(2)}) collective-permute-start(bf16[256,768]{1,0:T(8,128)(2,1)S(1)} %collective-permute-done.7.refs_9_), channel_id=1, source_target_pairs={{0,224},{32,0},{64,32},{96,64},{128,96},{160,128},{192,160},{224,1... | collective-permute-start | bytes 1179656 | tf_op jit(solution)/shard_map/ppermute | solution.py:276
  99.7 8.4 %collective-permute-start.10 = (bf16[256,768]{1,0:T(8,128)(2,1)S(1)}, bf16[256,768]{1,0:T(8,128)(2,1)S(1)}, u32[]{:S(2)}, u32[]{:S(2)}) collective-permute-start(bf16[256,768]{1,0:T(8,128)(2,1)S(1)} %collective-permute-done.8.refs_10_), channel_id=1, source_target_pairs={{0,32},{32,64},{64,96},{96,128},{128,160},{160,192},{192,224},{224... | collective-permute-start | bytes 1179656 | tf_op jit(solution)/shard_map/ppermute | solution.py:275
  100.4 9.1 %collective-permute-start.11 = (bf16[256,768]{1,0:T(8,128)(2,1)S(1)}, bf16[256,768]{1,0:T(8,128)(2,1)S(1)}, u32[]{:S(2)}, u32[]{:S(2)}) collective-permute-start(bf16[256,768]{1,0:T(8,128)(2,1)S(1)} %collective-permute-done.9.refs_11_), channel_id=1, source_target_pairs={{0,224},{32,0},{64,32},{96,64},{128,96},{160,128},{192,160},{224,1... | collective-permute-start | bytes 1179656 | tf_op jit(solution)/shard_map/ppermute | solution.py:276
  104.6 27.2 %collective-permute-start.12 = (bf16[384,512]{1,0:T(8,128)(2,1)}, bf16[384,512]{1,0:T(8,128)(2,1)S(1)}, u32[]{:S(2)}, u32[]{:S(2)}) collective-permute-start(bf16[384,512]{1,0:T(8,128)(2,1)} %slice.49), channel_id=1, source_target_pairs={{0,32},{32,64},{64,96},{96,128},{128,160},{160,192},{192,224},{224... | collective-permute-start | bytes 1179656 | tf_op jit(solution)/shard_map/ppermute | solution.py:280
  105.4 27.2 %collective-permute-start.13 = (bf16[384,512]{1,0:T(8,128)(2,1)}, bf16[384,512]{1,0:T(8,128)(2,1)}, u32[]{:S(2)}, u32[]{:S(2)}) collective-permute-start(bf16[384,512]{1,0:T(8,128)(2,1)} %slice.50), channel_id=1, source_target_pairs={{0,224},{32,0},{64,32},{96,64},{128,96},{160,128},{192,160},{224,1... | collective-permute-start | bytes 1179656 | tf_op jit(solution)/shard_map/ppermute | solution.py:281
  109.5 22.3 %collective-permute-start.14 = (bf16[128,768]{1,0:T(8,128)(2,1)}, bf16[128,768]{1,0:T(8,128)(2,1)}, u32[]{:S(2)}, u32[]{:S(2)}) collective-permute-start(bf16[128,768]{1,0:T(8,128)(2,1)} %slice.51), channel_id=1, source_target_pairs={{0,32},{32,64},{64,96},{96,128},{128,160},{160,192},{192,224},{224... | collective-permute-start | bytes 589832 | tf_op jit(solution)/shard_map/ppermute | solution.py:280
  111.0 20.8 %collective-permute-start.15 = (bf16[128,768]{1,0:T(8,128)(2,1)}, bf16[128,768]{1,0:T(8,128)(2,1)}, u32[]{:S(2)}, u32[]{:S(2)}) collective-permute-start(bf16[128,768]{1,0:T(8,128)(2,1)} %slice.52), channel_id=1, source_target_pairs={{0,224},{32,0},{64,32},{96,64},{128,96},{160,128},{192,160},{224,1... | collective-permute-start | bytes 589832 | tf_op jit(solution)/shard_map/ppermute | solution.py:281
  141.2 21.5 %collective-permute-start.16 = (bf16[128,6272]{1,0:T(8,128)(2,1)S(1)}, bf16[128,6272]{1,0:T(8,128)(2,1)S(1)}, u32[]{:S(2)}, u32[]{:S(2)}) collective-permute-start(bf16[128,6272]{1,0:T(8,128)(2,1)S(1)} %get-tuple-element.22), channel_id=1, source_target_pairs={{0,1},{1,0},{2,3},{3,2},{4,5},{5,4},{6,7},{7,6},{8,9},{9,8},{10,11... | collective-permute-start | bytes 4816904 | tf_op jit(solution)/shard_map/ppermute | solution.py:351
  150.8 11.9 %collective-permute-start.17 = (bf16[256,768]{1,0:T(8,128)(2,1)S(1)}, bf16[256,768]{1,0:T(8,128)(2,1)S(1)}, u32[]{:S(2)}, u32[]{:S(2)}) collective-permute-start(bf16[256,768]{1,0:T(8,128)(2,1)S(1)} %get-tuple-element.19.acts_ref.refs_0_), channel_id=1, source_target_pairs={{0,32},{32,64},{64,96},{96,128},{128,160},{160,192},{192,224},{224... | collective-permute-start | bytes 1179656 | tf_op jit(solution)/shard_map/ppermute | solution.py:275
  150.8 11.9 %collective-permute-start.18 = (bf16[256,768]{1,0:T(8,128)(2,1)S(1)}, bf16[256,768]{1,0:T(8,128)(2,1)S(1)}, u32[]{:S(2)}, u32[]{:S(2)}) collective-permute-start(bf16[256,768]{1,0:T(8,128)(2,1)S(1)} %get-tuple-element.19.acts_ref.refs_0_), channel_id=1, source_target_pairs={{0,224},{32,0},{64,32},{96,64},{128,96},{160,128},{192,160},{224,1... | collective-permute-start | bytes 1179656 | tf_op jit(solution)/shard_map/ppermute | solution.py:276
  164.5 42.4 %all-to-all-start = ((bf16[16,8,6272]{2,1,0:T(8,128)(2,1)}), bf16[16,8,6272]{2,1,0:T(8,128)(2,1)}, u32[]{:S(2)}, u32[]{:S(2)}) async-start(bf16[16,8,6272]{2,1,0:T(8,128)(2,1)} %bitcast.7), calls=%async_computation | async-start | bytes 3211264 | tf_op jit(solution)/shard_map/all_to_all | solution.py:354
  171.4 10.9 %collective-permute-start.19 = (bf16[256,768]{1,0:T(8,128)(2,1)S(1)}, bf16[256,768]{1,0:T(8,128)(2,1)S(1)}, u32[]{:S(2)}, u32[]{:S(2)}) collective-permute-start(bf16[256,768]{1,0:T(8,128)(2,1)S(1)} %collective-permute-done.17.refs_1_), channel_id=1, source_target_pairs={{0,32},{32,64},{64,96},{96,128},{128,160},{160,192},{192,224},{224... | collective-permute-start | bytes 1179656 | tf_op jit(solution)/shard_map/ppermute | solution.py:275
  171.5 11.5 %collective-permute-start.20 = (bf16[256,768]{1,0:T(8,128)(2,1)S(1)}, bf16[256,768]{1,0:T(8,128)(2,1)S(1)}, u32[]{:S(2)}, u32[]{:S(2)}) collective-permute-start(bf16[256,768]{1,0:T(8,128)(2,1)S(1)} %collective-permute-done.18.refs_2_), channel_id=1, source_target_pairs={{0,224},{32,0},{64,32},{96,64},{128,96},{160,128},{192,160},{224,1... | collective-permute-start | bytes 1179656 | tf_op jit(solution)/shard_map/ppermute | solution.py:276
  182.2 10.0 %collective-permute-start.21 = (bf16[256,768]{1,0:T(8,128)(2,1)S(1)}, bf16[256,768]{1,0:T(8,128)(2,1)S(1)}, u32[]{:S(2)}, u32[]{:S(2)}) collective-permute-start(bf16[256,768]{1,0:T(8,128)(2,1)S(1)} %collective-permute-done.19.refs_3_), channel_id=1, source_target_pairs={{0,32},{32,64},{64,96},{96,128},{128,160},{160,192},{192,224},{224... | collective-permute-start | bytes 1179656 | tf_op jit(solution)/shard_map/ppermute | solution.py:275
  183.0 9.9 %collective-permute-start.22 = (bf16[256,768]{1,0:T(8,128)(2,1)S(1)}, bf16[256,768]{1,0:T(8,128)(2,1)S(1)}, u32[]{:S(2)}, u32[]{:S(2)}) collective-permute-start(bf16[256,768]{1,0:T(8,128)(2,1)S(1)} %collective-permute-done.20.refs_4_), channel_id=1, source_target_pairs={{0,224},{32,0},{64,32},{96,64},{128,96},{160,128},{192,160},{224,1... | collective-permute-start | bytes 1179656 | tf_op jit(solution)/shard_map/ppermute | solution.py:276
  192.9 10.5 %collective-permute-start.23 = (bf16[128,768]{1,0:T(8,128)(2,1)}, bf16[128,768]{1,0:T(8,128)(2,1)}, u32[]{:S(2)}, u32[]{:S(2)}) collective-permute-start(bf16[128,768]{1,0:T(8,128)(2,1)} %slice.56), channel_id=1, source_target_pairs={{0,32},{32,64},{64,96},{96,128},{128,160},{160,192},{192,224},{224... | collective-permute-start | bytes 589832 | tf_op jit(solution)/shard_map/ppermute | solution.py:280
  193.6 9.8 %collective-permute-start.24 = (bf16[128,768]{1,0:T(8,128)(2,1)}, bf16[128,768]{1,0:T(8,128)(2,1)}, u32[]{:S(2)}, u32[]{:S(2)}) collective-permute-start(bf16[128,768]{1,0:T(8,128)(2,1)} %slice.57), channel_id=1, source_target_pairs={{0,224},{32,0},{64,32},{96,64},{128,96},{160,128},{192,160},{224,1... | collective-permute-start | bytes 589832 | tf_op jit(solution)/shard_map/ppermute | solution.py:281
  (44 other events, 177.4 us)
Sparse Core Ops, SparseCore 0:
  11.9 58.4 all-gather.2
  73.0 53.1 all-gather.4
where the time goes:
time: 221 us; the launch traced here: 218 us
  waiting for transfers between devices  73.8 us (33%)
  starting transfers between devices  49.3 us (22%)
  local copies, waits for them, and re-layouts  33.8 us (15%)
  Pallas kernels  20.6 us (9%)
  blocking collectives  17.7 us (8%)
  between operations  14.5 us (7%)
  other arithmetic  6.05 us (3%)
  matrix products  2.53 us (1%)
    ppermute x9, waiting for transfers between devices, ring_gather(): ahead = lax.ppermute(ahead, axis, up)  73.8 us
    unnamed x99, local copies, waits for them, and re-layouts  28.4 us
    ppermute x9, starting transfers between devices, ring_gather(): behind = lax.ppermute(behind, axis, down)  24.6 us
    all_to_all x1, blocking collectives, on_device(): lax.all_to_all(sides, 'fsdp', split_axis=0, concat_axis=0, tiled=True)  17.7 us
    ppermute x1, starting transfers between devices, on_device(): got = lax.ppermute(give, 'core', [(0, 1), (1, 0)])  9.57 us
    ppermute x3, starting transfers between devices, ring_gather(): behind = lax.ppermute(behind[half:], axis, down)  8.02 us
    all_to_all x1, starting transfers between devices, on_device(): lax.all_to_all(both, PLANE, split_axis=0, concat_axis=0, tiled=True)  6.82 us
    pallas_call x1, Pallas kernels, pre_sums(): kernel_call(body, jax.ShapeDtypeStruct(shape, F32), 40, in_specs=[whole(v...  5.25 us
  transfers between devices with their start and end apart: 28, of which 7 were waited for; matrix products, arithmetic and copies ran while one was open for 2% of the time, Pallas kernels for 9%

commit v1 on v0

v1 whole, which is shorter than its diff:
```python
import jax
import jax.numpy as jnp
from jax import lax
from jax.experimental import pallas as pl
from jax.experimental.pallas import tpu as pltpu
from jax.sharding import Mesh
from jax.sharding import PartitionSpec as P

CAP = 8
PLANE = ("x", "y")
EXPERT = ("x", "y", "core")
CORE_FIRST = ("core", "x", "y")
LANES = 128
BLOCK = 128
BF16 = jnp.bfloat16
F32 = jnp.float32


def contract(left, right, left_dim, right_dim):
    return lax.dot_general(
        left, right, (((left_dim,), (right_dim,)), ((), ())), preferred_element_type=F32
    )


def kernel_call(body, outs, limit, scalars=0, grid=(1,), **specs):
    grid_spec = pltpu.PrefetchScalarGridSpec(num_scalar_prefetch=scalars, grid=grid, **specs)
    return pl.pallas_call(
        body,
        out_shape=outs,
        grid_spec=grid_spec,
        compiler_params=pltpu.CompilerParams(vmem_limit_bytes=limit << 20),
    )


def far_memory():
    return pl.BlockSpec(memory_space=pl.ANY)


def whole(shape):
    return pl.BlockSpec(shape, lambda *_: (0,) * len(shape), pipeline_mode=pl.Buffered(1))


def block_at(shape, where):
    return pl.BlockSpec(shape, lambda *_: where, pipeline_mode=pl.Buffered(1))


def two_lanes(column):
    high = column.astype(BF16).astype(F32)
    lane = lax.broadcasted_iota(jnp.int32, (column.shape[0], LANES), 1)
    spread = jnp.where(lane == 0, high, jnp.where(lane == 1, column - high, 0.0))
    return spread.astype(BF16)


def scaled_weights(gate_quant, gate_scale, up_quant, up_scale, down_quant, down_scale):
    part, units = gate_quant.shape

    def put(out, quant, scale, shift):
        tall, broad = quant.shape[0] // BLOCK, quant.shape[1] // BLOCK
        for i in range(tall):
            for j in range(broad):
                rows, cols = slice(i * BLOCK, (i + 1) * BLOCK), slice(j * BLOCK, (j + 1) * BLOCK)
                out[rows, shift + j * BLOCK : shift + (j + 1) * BLOCK] = (
                    quant[rows, cols].astype(F32) * scale[i, j]
                ).astype(BF16)

    def body(gate, up, down, gate_s, up_s, down_s, gate_up_out, down_out):
        put(gate_up_out, gate, gate_s, 0)
        put(gate_up_out, up, up_s, units)
        put(down_out, down, down_s, 0)

    quants, scales = [gate_quant, up_quant, down_quant], [gate_scale, up_scale, down_scale]
    shapes = ((part, 2 * units), down_quant.shape)
    return kernel_call(
        body,
        tuple(jax.ShapeDtypeStruct(v, BF16) for v in shapes),
        60,
        in_specs=[whole(v.shape) for v in quants]
        + [pl.BlockSpec(memory_space=pltpu.SMEM)] * 3,
        out_specs=tuple(whole(v) for v in shapes),
    )(*quants, *scales)


def pre_sums(rows, gate_up_parts, down_parts):
    count = len(gate_up_parts)
    part, both = gate_up_parts[0][1].shape
    units = both // 2
    slots = rows.shape[0]
    width = (rows.shape[1] - LANES) // 2
    places = [r for r, _ in gate_up_parts]
    assert places == [r for r, _ in down_parts]

    def body(rows_ref, *refs):
        weights, out = refs[: 2 * count], refs[2 * count]
        x_in, dy_in, gate_up_in, down_in, sems = refs[2 * count + 1 :]
        copies = []
        for i, r in enumerate(places):
            copies.append(
                [
                    pltpu.make_async_copy(source, into.at[i], sems.at[k, i])
                    for k, (source, into) in enumerate(
                        (
                            (rows_ref.at[:, pl.ds(r * part, part)], x_in),
                            (rows_ref.at[:, pl.ds(width + r * part, part)], dy_in),
                            (weights[i], gate_up_in),
                            (weights[count + i], down_in),
                        )
                    )
                ]
            )
            for copy in copies[-1]:
                copy.start()
        pre = back = None
        for i in range(count):
            for copy in copies[i]:
                copy.wait()
            one = contract(x_in[i], gate_up_in[i], 1, 0)
            two = contract(dy_in[i], down_in[i], 1, 1)
            pre = one if pre is None else pre + one
            back = two if back is None else back + two
        out[:, :both] = pre
        out[:, both:] = back

    weights = [w for _, w in gate_up_parts] + [w for _, w in down_parts]
    shape = (slots, both + units)
    return kernel_call(
        body,
        jax.ShapeDtypeStruct(shape, F32),
        60,
        in_specs=[far_memory()] * (1 + 2 * count),
        out_specs=whole(shape),
        scratch_shapes=[
            pltpu.VMEM((count, slots, part), BF16),
            pltpu.VMEM((count, slots, part), BF16),
            pltpu.VMEM((count, part, both), BF16),
            pltpu.VMEM((count, units, part), BF16),
            pltpu.SemaphoreType.DMA((4, count)),
        ],
    )(rows, *weights)


def activations(rows, sums, gate_up_part, down_part):
    count = rows.shape[0]
    far, w_gate_up = gate_up_part
    w_down = down_part[1]
    part, both = w_gate_up.shape
    units = both // 2
    width = (rows.shape[1] - LANES) // 2

    def body(x_ref, dy_ref, prob_ref, sums_ref, gate_up_ref, down_ref, acts_ref, prob_out):
        pre = sums_ref[:, :both] + contract(x_ref[...], gate_up_ref[...], 1, 0)
        back = sums_ref[:, both:] + contract(dy_ref[...], down_ref[...], 1, 1)
        gate_pre, up_pre = pre[:, :units], pre[:, units:]
        sigmoid_gate = jax.nn.sigmoid(gate_pre)
        hidden = (gate_pre * sigmoid_gate * up_pre).astype(BF16)
        prob_part = jnp.sum(hidden.astype(F32) * back, axis=1, keepdims=True)
        grad_hidden = prob_ref[:, :1].astype(F32) * back
        acts_ref[:, :units] = (
            grad_hidden * up_pre * sigmoid_gate * (1.0 + gate_pre * (1.0 - sigmoid_gate))
        ).astype(BF16)
        acts_ref[:, units:both] = (grad_hidden * gate_pre * sigmoid_gate).astype(BF16)
        acts_ref[:, both:] = hidden
        prob_out[...] = two_lanes(prob_part)

    acts_shape, prob_shape = (count, both + units), (count, LANES)
    return kernel_call(
        body,
        (jax.ShapeDtypeStruct(acts_shape, BF16), jax.ShapeDtypeStruct(prob_shape, BF16)),
        60,
        in_specs=[
            block_at((count, part), (0, far)),
            block_at((count, part), (0, width // part + far)),
            block_at((count, LANES), (0, 2 * width // LANES)),
            whole(sums.shape),
            whole(w_gate_up.shape),
            whole(w_down.shape),
        ],
        out_specs=(whole(acts_shape), whole(prob_shape)),
    )(rows, rows, rows, sums, w_gate_up, w_down)


def slot_sums(core, acts, prob_lanes, gate_up_parts):
    half = acts.shape[0] // 2
    count = len(gate_up_parts)
    part, both = gate_up_parts[0][1].shape
    width = count * part
    places = [r for r, _ in gate_up_parts]

    def body(core_ref, acts_ref, prob_ref, *refs):
        weights, give, keep, weights_in, sems = refs[:count], *refs[count:]
        copies = [
            pltpu.make_async_copy(weights[i], weights_in.at[i], sems.at[i]) for i in range(count)
        ]
        for copy in copies:
            copy.start()
        theirs = pl.ds(pl.multiple_of((1 - core_ref[0]) * half, half), half)
        mine = pl.ds(pl.multiple_of(core_ref[0] * half, half), half)
        acts = jnp.concatenate([acts_ref[theirs, :both], acts_ref[mine, :both]], axis=0)
        for i, r in enumerate(places):
            copies[i].wait()
            sums = contract(acts, weights_in[i], 1, 1).astype(BF16)
            give[:, r * part : (r + 1) * part] = sums[:half]
            keep[:, r * part : (r + 1) * part] = sums[half:]
        give[:, width:] = prob_ref[theirs, :]
        keep[:, width:] = prob_ref[mine, :]

    weights = [w for _, w in gate_up_parts]
    shape = (half, width + LANES)
    return kernel_call(
        body,
        (jax.ShapeDtypeStruct(shape, BF16),) * 2,
        60,
        scalars=1,
        in_specs=[whole(acts.shape), whole(prob_lanes.shape)] + [far_memory()] * count,
        out_specs=(whole(shape),) * 2,
        scratch_shapes=[
            pltpu.VMEM((count, part, both), BF16),
            pltpu.SemaphoreType.DMA((count,)),
        ],
    )(core, acts, prob_lanes, *weights)


def pair_sum(mine, other):
    width = mine.shape[1] - LANES

    def body(a_ref, b_ref, out):
        for at in range(0, width, 768):
            cols = slice(at, at + 768)
            out[:, cols] = (a_ref[:, cols].astype(F32) + b_ref[:, cols].astype(F32)).astype(BF16)
        lanes = a_ref[:, width:].astype(F32) + b_ref[:, width:].astype(F32)
        out[:, width:] = two_lanes(lanes[:, 0:1] + lanes[:, 1:2])

    return kernel_call(
        body,
        jax.ShapeDtypeStruct(mine.shape, BF16),
        16,
        in_specs=[whole(mine.shape)] * 2,
        out_specs=whole(mine.shape),
    )(mine, other)


def weight_sums(columns, acts):
    slots, twice = columns.shape
    part, units = twice // 2, acts.shape[1] // 3
    tile = 256
    steps = part // tile

    def body(x_ref, weighted_ref, acts_ref, gate_out, up_out, down_out):
        both = contract(x_ref[...], acts_ref[:, : 2 * units], 0, 0)
        gate_out[...] = both[:, :units]
        up_out[...] = both[:, units:]
        down_out[...] = contract(acts_ref[:, 2 * units :], weighted_ref[...], 0, 0)

    return kernel_call(
        body,
        (
            jax.ShapeDtypeStruct((part, units), F32),
            jax.ShapeDtypeStruct((part, units), F32),
            jax.ShapeDtypeStruct((units, part), F32),
        ),
        60,
        grid=(steps,),
        in_specs=[
            pl.BlockSpec((slots, tile), lambda i: (0, i)),
            pl.BlockSpec((slots, tile), lambda i: (0, steps + i)),
            whole(acts.shape),
        ],
        out_specs=(
            pl.BlockSpec((tile, units), lambda i: (i, 0)),
            pl.BlockSpec((tile, units), lambda i: (i, 0)),
            pl.BlockSpec((units, tile), lambda i: (0, i)),
        ),
    )(columns, columns, acts)


def turn(values, axis, place, size):
    flipped = jnp.flip(values, axis)
    twice = jnp.concatenate([flipped, flipped], axis)
    return lax.dynamic_slice_in_dim(twice, size - 1 - place, size, axis)


def ring_gather(block, axis, size, last_up):
    up = [(i, (i + 1) % size) for i in range(size)]
    down = [(i, (i - 1) % size) for i in range(size)]
    far = size // 2
    parts = [(0, block)]
    ahead, behind = block, block
    for step in range(1, far):
        ahead = lax.ppermute(ahead, axis, up)
        behind = lax.ppermute(behind, axis, down)
        parts += [(step, ahead), (size - step, behind)]
    last = lax.ppermute(ahead, axis, up) if last_up else lax.ppermute(behind, axis, down)
    return parts, (far, last)


def make_on_device(mesh):
    ring = mesh.shape["fsdp"]

    def on_device(
        x_quant,
        x_scale,
        grad_out,
        route_mask,
        route_prob,
        gate_quant,
        gate_scale,
        up_quant,
        up_scale,
        down_quant,
        down_scale,
    ):
        place = lax.axis_index("fsdp")
        core = lax.axis_index("core")
        width = x_quant.shape[1]
        part = width // ring

        w_gate_up, w_down = scaled_weights(
            gate_quant, gate_scale, up_quant, up_scale, down_quant, down_scale
        )
        down_near, down_far = ring_gather(w_down, "fsdp", ring, False)
        gate_up_near, gate_up_far = ring_gather(w_gate_up, "fsdp", ring, True)

        slot_rank = jnp.cumsum(route_mask) - 1
        slot_ids = jnp.arange(CAP, dtype=jnp.int32)
        table = ((slot_rank[None, :] == slot_ids[:, None]) & (route_mask[None, :] == 1)).astype(BF16)
        table_wide = table.astype(F32)
        blocks = x_scale.shape[1]
        slot_quant = jnp.dot(table, x_quant, preferred_element_type=F32)
        slot_scale = jnp.dot(
            table_wide, x_scale, precision=lax.Precision.HIGHEST, preferred_element_type=F32
        )
        slot_x = (
            (slot_quant.reshape(CAP, blocks, width // blocks) * slot_scale[:, :, None])
            .reshape(CAP, width)
            .astype(BF16)
        )
        slot_dy = jnp.dot(table, grad_out, preferred_element_type=F32).astype(BF16)
        slot_prob = jnp.sum(table_wide * route_prob.astype(F32)[None, :], axis=1)
        weighted = (slot_prob[:, None] * slot_dy.astype(F32)).astype(BF16)

        sides = jnp.concatenate(
            [slot_x.reshape(CAP, ring, part), weighted.reshape(CAP, ring, part)], axis=-1
        ).transpose(1, 0, 2)
        turned = turn(
            jnp.stack([slot_x, slot_dy]).reshape(2, CAP, ring, part), 2, place, ring
        ).reshape(2, CAP, width)
        packed = jnp.concatenate(
            [turned[0], turned[1], jnp.broadcast_to(slot_prob.astype(BF16)[:, None], (CAP, 128))],
            axis=1,
        )
        rows = lax.all_gather(packed, CORE_FIRST, axis=0, tiled=True)

        sides = lax.all_to_all(sides, "fsdp", split_axis=0, concat_axis=0, tiled=True)
        columns = lax.all_gather(sides, CORE_FIRST, axis=1, tiled=True).reshape(-1, 2 * part)

        sums = pre_sums(rows, gate_up_near, down_near)
        acts, prob_lanes = activations(rows, sums, gate_up_far, down_far)
        all_acts = lax.all_gather(acts, "fsdp", axis=0, tiled=True)

        give, keep = slot_sums(core[None], acts, prob_lanes, [*gate_up_near, gate_up_far])
        got = lax.ppermute(give, "core", [(0, 1), (1, 0)])
        both = pair_sum(keep, got).reshape(-1, CAP, width + LANES)
        shares = lax.all_to_all(both, PLANE, split_axis=0, concat_axis=0, tiled=True)
        mine = jnp.sum(shares.astype(F32), axis=0)
        mine_grad = mine[:, :width].astype(BF16).reshape(CAP, ring, part)
        mine_grad = turn(mine_grad, 1, place, ring).reshape(CAP, width)
        mine_prob = mine[:, width] + mine[:, width + 1]
        grad_x = contract(table, mine_grad, 0, 0).astype(BF16)
        grad_prob = jnp.sum(table_wide * mine_prob[:, None], axis=0)

        grad_gate, grad_up, grad_down = weight_sums(columns, all_acts)
        return (grad_x, grad_prob, grad_gate, grad_up, grad_down)

    return on_device


def solution(mesh):
    devices = mesh.devices
    mesh = Mesh(devices.reshape(devices.shape[0], 4, 4, 2), ("fsdp", "x", "y", "core"))
    tokens = ("fsdp", "x", "y", "core")
    placed = (
        P(tokens, None),
        P(tokens, None),
        P(tokens, None),
        P(tokens),
        P(tokens),
        P("fsdp", EXPERT),
        P("fsdp", EXPERT),
        P("fsdp", EXPERT),
        P("fsdp", EXPERT),
        P(EXPERT, "fsdp"),
        P(EXPERT, "fsdp"),
    )
    return jax.shard_map(
        make_on_device(mesh),
        mesh=mesh,
        in_specs=placed,
        out_specs=(
            P(tokens, None),
            P(tokens),
            P("fsdp", EXPERT),
            P("fsdp", EXPERT),
            P(EXPERT, "fsdp"),
        ),
        check_vma=False,
    )
```

time: 221 us -> 203 us (0.919); the launches traced: 218 us -> 203 us
  blocking collectives: 17.7 us -> 47 us
  local copies, waits for them, and re-layouts: 33.8 us -> 6.43 us
  starting transfers between devices: 49.3 us -> 22.6 us
  Pallas kernels: 20.6 us -> 28 us
  waiting for transfers between devices: 73.8 us -> 78.8 us
  other arithmetic: 6.05 us -> 3.81 us
    all_to_all x0 -> x1, blocking collectives: none -> 29.2 us  [on_device(): lax.all_to_all(both, PLANE, split_axis=0, concat_axis=0, tiled=True)]
    unnamed x99 -> x37, local copies, waits for them, and re-layouts: 28.4 us -> 5.26 us
    ppermute x9 -> x6, waiting for transfers between devices: 0.02 us -> 20.5 us  [ring_gather(): behind = lax.ppermute(behind, axis, down)]
    ppermute x9 -> x6, waiting for transfers between devices: 73.8 us -> 54.9 us  [ring_gather(): ahead = lax.ppermute(ahead, axis, up)]
    ppermute x9 -> x6, starting transfers between devices: 24.6 us -> 11.4 us  [ring_gather(): behind = lax.ppermute(behind, axis, down)]
    all_to_all x1 -> x0, starting transfers between devices: 6.82 us -> none  [on_device(): lax.all_to_all(both, PLANE, split_axis=0, concat_axis=0, tiled=True)]
    pallas_call x4 -> x3, Pallas kernels: 15.8 us -> 21.7 us  [the longest x1 7.67 us: slot_sums(): kernel_call(body, (jax.ShapeDtypeStruct(shape, BF16),) * 2, 60, scalars=1...]
    slice x6 -> x0, local copies, waits for them, and re-layouts: 4.31 us -> none  [the longest x3 2.16 us: ring_gather(): ahead = lax.ppermute(ahead[:half], axis, up)]
  transfers between devices with their start and end apart: 28 -> 18, of which waited for: 7 -> 8; matrix products, arithmetic and copies ran while one was open for 2% -> 2% of each run, Pallas kernels for 9% -> 10%
where the time goes in v1:
time: 203 us
  waiting for transfers between devices  78.8 us (39%)
  blocking collectives  47 us (23%)
  Pallas kernels  28 us (14%)
  starting transfers between devices  22.6 us (11%)
  between operations  14 us (7%)
  local copies, waits for them, and re-layouts  6.43 us (3%)
  other arithmetic  3.81 us (2%)
  matrix products  2.52 us (1%)
    ppermute x6, waiting for transfers between devices, ring_gather(): ahead = lax.ppermute(ahead, axis, up)  54.9 us
    all_to_all x1, blocking collectives, on_device(): lax.all_to_all(both, PLANE, split_axis=0, concat_axis=0, tiled=True)  29.2 us
    ppermute x6, waiting for transfers between devices, ring_gather(): behind = lax.ppermute(behind, axis, down)  20.5 us
    all_to_all x1, blocking collectives, on_device(): lax.all_to_all(sides, 'fsdp', split_axis=0, concat_axis=0, tiled=True)  17.8 us
    ppermute x6, starting transfers between devices, ring_gather(): behind = lax.ppermute(behind, axis, down)  11.4 us
    pallas_call x1, Pallas kernels, slot_sums(): kernel_call(body, (jax.ShapeDtypeStruct(shape, BF16),) * 2, 60, scalars=1...  7.67 us
    pallas_call x1, Pallas kernels, weight_sums(): kernel_call(body, (jax.ShapeDtypeStruct((part, units), F32), jax.ShapeDty...  7.23 us
    pallas_call x1, Pallas kernels, pre_sums(): kernel_call(body, jax.ShapeDtypeStruct(shape, F32), 60, in_specs=[far_mem...  6.82 us
  transfers between devices with their start and end apart: 18, of which 8 were waited for; matrix products, arithmetic and copies ran while one was open for 2% of the time, Pallas kernels for 10%

profile of v1, /device:TPU:1, one launch (start us, length us, event | category | flops | bytes accessed | tf_op | source)
XLA Modules:
  0.0 203.2 jit_solution(4621674446807024850)
XLA Ops:
  7.3 0.8 broadcast_compare_fusion
  8.1 0.8 copy.34
  11.0 0.7 pad_maximum_fusion
  11.8 17.8 %all_to_all.10 = bf16[8,8,1536]{2,1,0:T(8,128)(2,1)} all-to-all(bf16[8,8,1536]{2,1,0:T(8,128)(2,1)S(1)} %maximum_bitcast_fusion), channel_id=1, replica_groups=mesh['fsdp'=8,'x'=4,'y'=4,'core'=2] {'fsdp'}, dimensions={0} | all-to-all | bytes 393216 | tf_op jit(solution)/shard_map/all_to_all | solution.py:352
  29.7 0.7 copy.36.gate_s
  31.1 2.4 %shard_map.146 = (bf16[768,512]{1,0:T(8,128)(2,1)}, bf16[256,768]{1,0:T(8,128)(2,1)}) custom-call(bf16[768,256]{1,0:T(8,128)(2,1)} %gate.1, bf16[768,256]{1,0:T(8,128)(2,1)} %up.1, bf16[256,768]{1,0:T(8,128)(2,1)} %down.1, f32[6,2]{1,0:T(8,128)} %copy.36.gate_s, f32[6,2]{1,0:T(8,128)} %copy.37.up_s, f32[2,6]{1,0:T(2,128)} %down_s.1), custom_call_target="tpu_custom_call" | custom-call | tf_op jit(solution)/shard_map/pallas_call | solution.py:73
  33.5 2.6 %collective-permute-start.1 = (bf16[768,512]{1,0:T(8,128)(2,1)}, bf16[768,512]{1,0:T(8,128)(2,1)S(1)}, u32[]{:S(2)}, u32[]{:S(2)}) collective-permute-start(bf16[768,512]{1,0:T(8,128)(2,1)} %get-tuple-element.14.refs_0_), channel_id=1, source_target_pairs={{0,224},{32,0},{64,32},{96,64},{128,96},{160,128},{192,160},{224,1... | collective-permute-start | bytes 2359304 | tf_op jit(solution)/shard_map/ppermute | solution.py:289
  36.1 15.2 %collective-permute-done.refs_1_ = bf16[768,512]{1,0:T(8,128)(2,1)S(1)} collective-permute-done((bf16[768,512]{1,0:T(8,128)(2,1)}, bf16[768,512]{1,0:T(8,128)(2,1)S(1)}, u32[]{:S(2)}, u32[]{:S(2)}) %collective-permute-start) | collective-permute-done | bytes 786464 | tf_op jit(solution)/shard_map/ppermute | solution.py:288
  51.3 2.7 %collective-permute-start.3 = (bf16[768,512]{1,0:T(8,128)(2,1)S(1)}, bf16[768,512]{1,0:T(8,128)(2,1)S(1)}, u32[]{:S(2)}, u32[]{:S(2)}) collective-permute-start(bf16[768,512]{1,0:T(8,128)(2,1)S(1)} %collective-permute-done.1.refs_2_), channel_id=1, source_target_pairs={{0,224},{32,0},{64,32},{96,64},{128,96},{160,128},{192,160},{224,1... | collective-permute-start | bytes 2359304 | tf_op jit(solution)/shard_map/ppermute | solution.py:289
  54.0 14.0 %collective-permute-done.2.refs_3_ = bf16[768,512]{1,0:T(8,128)(2,1)S(1)} collective-permute-done((bf16[768,512]{1,0:T(8,128)(2,1)S(1)}, bf16[768,512]{1,0:T(8,128)(2,1)S(1)}, u32[]{:S(2)}, u32[]{:S(2)}) %collective-permute-start.2) | collective-permute-done | bytes 786464 | tf_op jit(solution)/shard_map/ppermute | solution.py:288
  68.1 7.4 %collective-permute-done.7.refs_9_ = bf16[256,768]{1,0:T(8,128)(2,1)S(1)} collective-permute-done((bf16[256,768]{1,0:T(8,128)(2,1)}, bf16[256,768]{1,0:T(8,128)(2,1)S(1)}, u32[]{:S(2)}, u32[]{:S(2)}) %collective-permute-start.7) | collective-permute-done | bytes 393248 | tf_op jit(solution)/shard_map/ppermute | solution.py:289
  75.5 3.3 %collective-permute-start.9 = (bf16[256,768]{1,0:T(8,128)(2,1)S(1)}, bf16[256,768]{1,0:T(8,128)(2,1)S(1)}, u32[]{:S(2)}, u32[]{:S(2)}) collective-permute-start(bf16[256,768]{1,0:T(8,128)(2,1)S(1)} %collective-permute-done.7.refs_9_), channel_id=1, source_target_pairs={{0,224},{32,0},{64,32},{96,64},{128,96},{160,128},{192,160},{224,1... | collective-permute-start | bytes 1179656 | tf_op jit(solution)/shard_map/ppermute | solution.py:289
  78.8 13.8 %collective-permute-done.6.refs_8_ = bf16[256,768]{1,0:T(8,128)(2,1)S(1)} collective-permute-done((bf16[256,768]{1,0:T(8,128)(2,1)}, bf16[256,768]{1,0:T(8,128)(2,1)S(1)}, u32[]{:S(2)}, u32[]{:S(2)}) %collective-permute-start.6) | collective-permute-done | bytes 393248 | tf_op jit(solution)/shard_map/ppermute | solution.py:288
  92.6 2.7 %collective-permute-start.5 = (bf16[768,512]{1,0:T(8,128)(2,1)S(1)}, bf16[768,512]{1,0:T(8,128)(2,1)}, u32[]{:S(2)}, u32[]{:S(2)}) collective-permute-start(bf16[768,512]{1,0:T(8,128)(2,1)S(1)} %collective-permute-done.3.refs_4_), channel_id=1, source_target_pairs={{0,224},{32,0},{64,32},{96,64},{128,96},{160,128},{192,160},{224,1... | collective-permute-start | bytes 2359304 | tf_op jit(solution)/shard_map/ppermute | solution.py:289
  95.4 1.4 collective-permute-start.12
  96.8 4.4 %collective-permute-done.8.refs_10_ = bf16[256,768]{1,0:T(8,128)(2,1)S(1)} collective-permute-done((bf16[256,768]{1,0:T(8,128)(2,1)S(1)}, bf16[256,768]{1,0:T(8,128)(2,1)S(1)}, u32[]{:S(2)}, u32[]{:S(2)}) %collective-permute-start.8) | collective-permute-done | bytes 393248 | tf_op jit(solution)/shard_map/ppermute | solution.py:288
  101.3 13.1 %collective-permute-done.11.refs_13_ = bf16[256,768]{1,0:T(8,128)(2,1)} collective-permute-done((bf16[256,768]{1,0:T(8,128)(2,1)S(1)}, bf16[256,768]{1,0:T(8,128)(2,1)}, u32[]{:S(2)}, u32[]{:S(2)}) %collective-permute-start.11) | collective-permute-done | bytes 393248 | tf_op jit(solution)/shard_map/ppermute | solution.py:289
  114.4 3.5 %collective-permute-start.13 = (bf16[256,768]{1,0:T(8,128)(2,1)}, bf16[256,768]{1,0:T(8,128)(2,1)S(1)}, u32[]{:S(2)}, u32[]{:S(2)}) collective-permute-start(bf16[256,768]{1,0:T(8,128)(2,1)} %collective-permute-done.11.refs_13_), channel_id=1, source_target_pairs={{0,224},{32,0},{64,32},{96,64},{128,96},{160,128},{192,160},{224,1... | collective-permute-start | bytes 1179656 | tf_op jit(solution)/shard_map/ppermute | solution.py:291
  117.9 7.5 %collective-permute-done.10.refs_12_ = bf16[256,768]{1,0:T(8,128)(2,1)S(1)} collective-permute-done((bf16[256,768]{1,0:T(8,128)(2,1)S(1)}, bf16[256,768]{1,0:T(8,128)(2,1)S(1)}, u32[]{:S(2)}, u32[]{:S(2)}) %collective-permute-start.10) | collective-permute-done | bytes 393248 | tf_op jit(solution)/shard_map/ppermute | solution.py:288
  125.5 0.7 copy-done.13
  126.2 6.8 %shard_map.147.sums_ref = f32[256,768]{1,0:T(8,128)} custom-call(bf16[256,12416]{1,0:T(8,128)(2,1)} %all-gather.4.cloned.1.call-done.rows_ref.x_ref.dy_ref.prob_ref, bf16[768,512]{1,0:T(8,128)(2,1)} %get-tuple-element.14.refs_0_, bf16[768,512]{1,0:T(8,128)(2,1)} %copy-done.3, bf16[768,512]{1,0:T(8,128)(2,1)} %copy-done.4, bf16[768,512]{1,0:T(8,128)(2,1)} %copy-done.5, ...), custom_call_target="tpu_custom_call" | custom-call | tf_op jit(solution)/shard_map/pallas_call | solution.py:125
  133.1 0.7 copy-done.8
  133.8 0.9 copy-done.2
  134.7 3.1 %shard_map.148 = (bf16[256,768]{1,0:T(8,128)(2,1)}, bf16[256,128]{1,0:T(8,128)(2,1)}) custom-call(bf16[256,12416]{1,0:T(8,128)(2,1)} %all-gather.4.cloned.1.call-done.rows_ref.x_ref.dy_ref.prob_ref, bf16[256,12416]{1,0:T(8,128)(2,1)} %all-gather.4.cloned.1.call-done.rows_ref.x_ref.dy_ref.prob_ref, ...), custom_call_target="tpu_custom_call" | custom-call | tf_op jit(solution)/shard_map/pallas_call | solution.py:165
  137.9 7.7 %shard_map.149 = (bf16[128,6272]{1,0:T(8,128)(2,1)}, bf16[128,6272]{1,0:T(8,128)(2,1)}) custom-call(s32[1]{0:T(128)} %bitcast.1.core_ref, bf16[256,768]{1,0:T(8,128)(2,1)} %get-tuple-element.16.acts_ref, bf16[256,128]{1,0:T(8,128)(2,1)} %get-tuple-element.17.prob_ref, bf16[768,512]{1,0:T(8,128)(2,1)} %get-tuple-element.14.refs_0_, ...), custom_call_target="tpu_custom_call" | custom-call | tf_op jit(solution)/shard_map/pallas_call | solution.py:208
  145.5 6.1 %collective-permute-start.14 = (bf16[128,6272]{1,0:T(8,128)(2,1)}, bf16[128,6272]{1,0:T(8,128)(2,1)S(1)}, u32[]{:S(2)}, u32[]{:S(2)}) collective-permute-start(bf16[128,6272]{1,0:T(8,128)(2,1)} %get-tuple-element.19), channel_id=1, source_target_pairs={{0,1},{1,0},{2,3},{3,2},{4,5},{5,4},{6,7},{7,6},{8,9},{9,8},{10,11... | collective-permute-start | bytes 4816904 | tf_op jit(solution)/shard_map/ppermute | solution.py:360
  151.6 3.3 %collective-permute-done.14.b_ref = bf16[128,6272]{1,0:T(8,128)(2,1)S(1)} collective-permute-done((bf16[128,6272]{1,0:T(8,128)(2,1)}, bf16[128,6272]{1,0:T(8,128)(2,1)S(1)}, u32[]{:S(2)}, u32[]{:S(2)}) %collective-permute-start.14) | collective-permute-done | bytes 1605664 | tf_op jit(solution)/shard_map/ppermute | solution.py:360
  154.9 1.4 copy-done.1
  156.4 0.7 shard_map.150
  157.0 29.2 %all_to_all.11 = bf16[16,8,6272]{2,1,0:T(8,128)(2,1)S(1)} all-to-all(bf16[16,8,6272]{2,1,0:T(8,128)(2,1)S(1)} %bitcast.22), channel_id=1, replica_groups=mesh['fsdp'=8,'x'=4,'y'=4,'core'=2] {'x','y'}, dimensions={0} | all-to-all | bytes 3211264 | tf_op jit(solution)/shard_map/all_to_all | solution.py:362
  187.6 1.8 convolution_convert_fusion
  189.4 7.2 %shard_map.151 = (f32[768,256]{1,0:T(8,128)}, f32[768,256]{1,0:T(8,128)}, f32[256,768]{1,0:T(8,128)}) custom-call(bf16[2048,1536]{1,0:T(8,128)(2,1)} %bitcast.23, bf16[2048,1536]{1,0:T(8,128)(2,1)} %bitcast.24, bf16[2048,768]{1,0:T(8,128)(2,1)} %all-gather.8.cloned.1.call-done.acts_ref), custom_call_target="tpu_custom_call" | custom-call | tf_op jit(solution)/shard_map/pallas_call | solution.py:253
  (77 shorter events, 4.6 us)
Async XLA Ops:
  7.2 2.8 %copy-start = (bf16[128,6144]{1,0:T(8,128)(2,1)S(1)}, bf16[128,6144]{1,0:T(8,128)(2,1)}, u32[]{:S(2)}) copy-start(bf16[128,6144]{1,0:T(8,128)(2,1)} %param.13) | copy-start | bytes 4718596
  7.2 3.1 %copy-start.14 = (f32[128,48]{0,1:T(8,128)S(1)}, f32[128,48]{0,1:T(8,128)}, u32[]{:S(2)}) copy-start(f32[128,48]{0,1:T(8,128)} %param.12) | copy-start | bytes 73732
  7.2 3.3 %copy-start.7 = (bf16[128,6144]{1,0:T(8,128)(2,1)S(1)}, bf16[128,6144]{1,0:T(8,128)(2,1)}, u32[]{:S(2)}) copy-start(bf16[128,6144]{1,0:T(8,128)(2,1)} %param.11) | copy-start | bytes 4718596
  7.2 119.0 %all-gather.4.cloned.1.call-start = ((), (), s32[]{:S(2)}) async-start(), calls=%async_computation.2 | async-start | bytes 6555648 | tf_op jit(solution)/shard_map/all_gather | solution.py:350
  10.8 18.9 %copy-start.15 = (f32[6,2]{0,1:T(2,128)S(1)}, f32[6,2]{0,1:T(2,128)}, u32[]{:S(2)}) copy-start(f32[6,2]{0,1:T(2,128)} %param.17) | copy-start | bytes 148
  10.8 19.6 %copy-start.16 = (f32[6,2]{0,1:T(2,128)S(1)}, f32[6,2]{0,1:T(2,128)}, u32[]{:S(2)}) copy-start(f32[6,2]{0,1:T(2,128)} %param.19) | copy-start | bytes 148
  11.8 177.6 %all-gather.6.cloned.1.call-start = ((), (), s32[]{:S(2)}) async-start(), calls=%async_computation.3 | async-start | bytes 6488064 | tf_op jit(solution)/shard_map/all_gather | solution.py:353
  29.6 159.8 %all-gather.8.cloned.1.call-start = ((), (), s32[]{:S(2)}) async-start(), calls=%async_computation.4 | async-start | bytes 3538944 | tf_op jit(solution)/shard_map/all_gather | solution.py:357
  33.5 17.8 %collective-permute-start = (bf16[768,512]{1,0:T(8,128)(2,1)}, bf16[768,512]{1,0:T(8,128)(2,1)S(1)}, u32[]{:S(2)}, u32[]{:S(2)}) collective-permute-start(bf16[768,512]{1,0:T(8,128)(2,1)} %get-tuple-element.14.refs_0_), channel_id=1, source_target_pairs={{0,32},{32,64},{64,96},{96,128},{128,160},{160,192},{192,224},{224... | collective-permute-start | bytes 2359304 | tf_op jit(solution)/shard_map/ppermute | solution.py:288
  33.5 17.8 %collective-permute-start.1 = (bf16[768,512]{1,0:T(8,128)(2,1)}, bf16[768,512]{1,0:T(8,128)(2,1)S(1)}, u32[]{:S(2)}, u32[]{:S(2)}) collective-permute-start(bf16[768,512]{1,0:T(8,128)(2,1)} %get-tuple-element.14.refs_0_), channel_id=1, source_target_pairs={{0,224},{32,0},{64,32},{96,64},{128,96},{160,128},{192,160},{224,1... | collective-permute-start | bytes 2359304 | tf_op jit(solution)/shard_map/ppermute | solution.py:289
  51.3 74.9 %copy-start.3 = (bf16[768,512]{1,0:T(8,128)(2,1)}, bf16[768,512]{1,0:T(8,128)(2,1)S(1)}, u32[]{:S(2)}) copy-start(bf16[768,512]{1,0:T(8,128)(2,1)S(1)} %collective-permute-done.refs_1_) | copy-start | bytes 2359300
  51.3 16.8 %collective-permute-start.2 = (bf16[768,512]{1,0:T(8,128)(2,1)S(1)}, bf16[768,512]{1,0:T(8,128)(2,1)S(1)}, u32[]{:S(2)}, u32[]{:S(2)}) collective-permute-start(bf16[768,512]{1,0:T(8,128)(2,1)S(1)} %collective-permute-done.refs_1_), channel_id=1, source_target_pairs={{0,32},{32,64},{64,96},{96,128},{128,160},{160,192},{192,224},{224... | collective-permute-start | bytes 2359304 | tf_op jit(solution)/shard_map/ppermute | solution.py:288
  51.3 44.1 %copy-start.4 = (bf16[768,512]{1,0:T(8,128)(2,1)}, bf16[768,512]{1,0:T(8,128)(2,1)S(1)}, u32[]{:S(2)}) copy-start(bf16[768,512]{1,0:T(8,128)(2,1)S(1)} %collective-permute-done.1.refs_2_) | copy-start | bytes 2359300
  51.3 41.3 %collective-permute-start.3 = (bf16[768,512]{1,0:T(8,128)(2,1)S(1)}, bf16[768,512]{1,0:T(8,128)(2,1)S(1)}, u32[]{:S(2)}, u32[]{:S(2)}) collective-permute-start(bf16[768,512]{1,0:T(8,128)(2,1)S(1)} %collective-permute-done.1.refs_2_), channel_id=1, source_target_pairs={{0,224},{32,0},{64,32},{96,64},{128,96},{160,128},{192,160},{224,1... | collective-permute-start | bytes 2359304 | tf_op jit(solution)/shard_map/ppermute | solution.py:289
  54.0 21.5 %collective-permute-start.7 = (bf16[256,768]{1,0:T(8,128)(2,1)}, bf16[256,768]{1,0:T(8,128)(2,1)S(1)}, u32[]{:S(2)}, u32[]{:S(2)}) collective-permute-start(bf16[256,768]{1,0:T(8,128)(2,1)} %get-tuple-element.15.refs_7_), channel_id=1, source_target_pairs={{0,224},{32,0},{64,32},{96,64},{128,96},{160,128},{192,160},{224,1... | collective-permute-start | bytes 1179656 | tf_op jit(solution)/shard_map/ppermute | solution.py:289
  68.1 27.3 %copy-start.5 = (bf16[768,512]{1,0:T(8,128)(2,1)}, bf16[768,512]{1,0:T(8,128)(2,1)S(1)}, u32[]{:S(2)}) copy-start(bf16[768,512]{1,0:T(8,128)(2,1)S(1)} %collective-permute-done.2.refs_3_) | copy-start | bytes 2359300
  68.1 27.3 %collective-permute-start.4 = (bf16[768,512]{1,0:T(8,128)(2,1)S(1)}, bf16[768,512]{1,0:T(8,128)(2,1)}, u32[]{:S(2)}, u32[]{:S(2)}) collective-permute-start(bf16[768,512]{1,0:T(8,128)(2,1)S(1)} %collective-permute-done.2.refs_3_), channel_id=1, source_target_pairs={{0,32},{32,64},{64,96},{96,128},{128,160},{160,192},{192,224},{224... | collective-permute-start | bytes 2359304 | tf_op jit(solution)/shard_map/ppermute | solution.py:288
  68.1 24.5 %collective-permute-start.6 = (bf16[256,768]{1,0:T(8,128)(2,1)}, bf16[256,768]{1,0:T(8,128)(2,1)S(1)}, u32[]{:S(2)}, u32[]{:S(2)}) collective-permute-start(bf16[256,768]{1,0:T(8,128)(2,1)} %get-tuple-element.15.refs_7_), channel_id=1, source_target_pairs={{0,32},{32,64},{64,96},{96,128},{128,160},{160,192},{192,224},{224... | collective-permute-start | bytes 1179656 | tf_op jit(solution)/shard_map/ppermute | solution.py:288
  75.5 25.8 %copy-start.9 = (bf16[256,768]{1,0:T(8,128)(2,1)}, bf16[256,768]{1,0:T(8,128)(2,1)S(1)}, u32[]{:S(2)}) copy-start(bf16[256,768]{1,0:T(8,128)(2,1)S(1)} %collective-permute-done.7.refs_9_) | copy-start | bytes 1179652
  75.5 19.8 %collective-permute-start.9 = (bf16[256,768]{1,0:T(8,128)(2,1)S(1)}, bf16[256,768]{1,0:T(8,128)(2,1)S(1)}, u32[]{:S(2)}, u32[]{:S(2)}) collective-permute-start(bf16[256,768]{1,0:T(8,128)(2,1)S(1)} %collective-permute-done.7.refs_9_), channel_id=1, source_target_pairs={{0,224},{32,0},{64,32},{96,64},{128,96},{160,128},{192,160},{224,1... | collective-permute-start | bytes 1179656 | tf_op jit(solution)/shard_map/ppermute | solution.py:289
  92.6 21.8 %copy-start.10 = (bf16[256,768]{1,0:T(8,128)(2,1)}, bf16[256,768]{1,0:T(8,128)(2,1)S(1)}, u32[]{:S(2)}) copy-start(bf16[256,768]{1,0:T(8,128)(2,1)S(1)} %collective-permute-done.6.refs_8_) | copy-start | bytes 1179652
  92.6 8.7 %collective-permute-start.8 = (bf16[256,768]{1,0:T(8,128)(2,1)S(1)}, bf16[256,768]{1,0:T(8,128)(2,1)S(1)}, u32[]{:S(2)}, u32[]{:S(2)}) collective-permute-start(bf16[256,768]{1,0:T(8,128)(2,1)S(1)} %collective-permute-done.6.refs_8_), channel_id=1, source_target_pairs={{0,32},{32,64},{64,96},{96,128},{128,160},{160,192},{192,224},{224... | collective-permute-start | bytes 1179656 | tf_op jit(solution)/shard_map/ppermute | solution.py:288
  92.6 4.2 %copy-start.6 = (bf16[768,512]{1,0:T(8,128)(2,1)}, bf16[768,512]{1,0:T(8,128)(2,1)S(1)}, u32[]{:S(2)}) copy-start(bf16[768,512]{1,0:T(8,128)(2,1)S(1)} %collective-permute-done.3.refs_4_) | copy-start | bytes 2359300
  92.6 33.6 %collective-permute-start.5 = (bf16[768,512]{1,0:T(8,128)(2,1)S(1)}, bf16[768,512]{1,0:T(8,128)(2,1)}, u32[]{:S(2)}, u32[]{:S(2)}) collective-permute-start(bf16[768,512]{1,0:T(8,128)(2,1)S(1)} %collective-permute-done.3.refs_4_), channel_id=1, source_target_pairs={{0,224},{32,0},{64,32},{96,64},{128,96},{160,128},{192,160},{224,1... | collective-permute-start | bytes 2359304 | tf_op jit(solution)/shard_map/ppermute | solution.py:289
  95.3 22.6 %copy-start.11 = (bf16[256,768]{1,0:T(8,128)(2,1)}, bf16[256,768]{1,0:T(8,128)(2,1)S(1)}, u32[]{:S(2)}) copy-start(bf16[256,768]{1,0:T(8,128)(2,1)S(1)} %collective-permute-done.9.refs_11_) | copy-start | bytes 1179652
  95.3 19.1 %collective-permute-start.11 = (bf16[256,768]{1,0:T(8,128)(2,1)S(1)}, bf16[256,768]{1,0:T(8,128)(2,1)}, u32[]{:S(2)}, u32[]{:S(2)}) collective-permute-start(bf16[256,768]{1,0:T(8,128)(2,1)S(1)} %collective-permute-done.9.refs_11_), channel_id=1, source_target_pairs={{0,224},{32,0},{64,32},{96,64},{128,96},{160,128},{192,160},{224,1... | collective-permute-start | bytes 1179656 | tf_op jit(solution)/shard_map/ppermute | solution.py:289
  95.4 37.7 %collective-permute-start.12 = (bf16[768,512]{1,0:T(8,128)(2,1)}, bf16[768,512]{1,0:T(8,128)(2,1)S(1)}, u32[]{:S(2)}, u32[]{:S(2)}) collective-permute-start(bf16[768,512]{1,0:T(8,128)(2,1)} %collective-permute-done.4.refs_5_), channel_id=1, source_target_pairs={{0,32},{32,64},{64,96},{96,128},{128,160},{160,192},{192,224},{224... | collective-permute-start | bytes 2359304 | tf_op jit(solution)/shard_map/ppermute | solution.py:291
  101.3 24.2 %copy-start.12 = (bf16[256,768]{1,0:T(8,128)(2,1)}, bf16[256,768]{1,0:T(8,128)(2,1)S(1)}, u32[]{:S(2)}) copy-start(bf16[256,768]{1,0:T(8,128)(2,1)S(1)} %collective-permute-done.8.refs_10_) | copy-start | bytes 1179652
  101.3 24.2 %collective-permute-start.10 = (bf16[256,768]{1,0:T(8,128)(2,1)S(1)}, bf16[256,768]{1,0:T(8,128)(2,1)S(1)}, u32[]{:S(2)}, u32[]{:S(2)}) collective-permute-start(bf16[256,768]{1,0:T(8,128)(2,1)S(1)} %collective-permute-done.8.refs_10_), channel_id=1, source_target_pairs={{0,32},{32,64},{64,96},{96,128},{128,160},{160,192},{192,224},{224... | collective-permute-start | bytes 1179656 | tf_op jit(solution)/shard_map/ppermute | solution.py:288
  114.4 18.6 %collective-permute-start.13 = (bf16[256,768]{1,0:T(8,128)(2,1)}, bf16[256,768]{1,0:T(8,128)(2,1)S(1)}, u32[]{:S(2)}, u32[]{:S(2)}) collective-permute-start(bf16[256,768]{1,0:T(8,128)(2,1)} %collective-permute-done.11.refs_13_), channel_id=1, source_target_pairs={{0,224},{32,0},{64,32},{96,64},{128,96},{160,128},{192,160},{224,1... | collective-permute-start | bytes 1179656 | tf_op jit(solution)/shard_map/ppermute | solution.py:291
  145.5 9.4 %collective-permute-start.14 = (bf16[128,6272]{1,0:T(8,128)(2,1)}, bf16[128,6272]{1,0:T(8,128)(2,1)S(1)}, u32[]{:S(2)}, u32[]{:S(2)}) collective-permute-start(bf16[128,6272]{1,0:T(8,128)(2,1)} %get-tuple-element.19), channel_id=1, source_target_pairs={{0,1},{1,0},{2,3},{3,2},{4,5},{5,4},{6,7},{7,6},{8,9},{9,8},{10,11... | collective-permute-start | bytes 4816904 | tf_op jit(solution)/shard_map/ppermute | solution.py:360
  154.9 1.4 copy-start.1
  (3 other events, 2.4 us)
Sparse Core Ops, SparseCore 0:
  11.9 58.4 all-gather.3
  73.0 53.1 all-gather.5
  138.0 51.3 all-gather.7

commit v2 on v1

--- a/solution.py
+++ b/solution.py
@@ -53,58 +53,58 @@
 
 def scaled_weights(gate_quant, gate_scale, up_quant, up_scale, down_quant, down_scale):
     part, units = gate_quant.shape
-
-    def put(out, quant, scale, shift):
-        tall, broad = quant.shape[0] // BLOCK, quant.shape[1] // BLOCK
-        for i in range(tall):
-            for j in range(broad):
-                rows, cols = slice(i * BLOCK, (i + 1) * BLOCK), slice(j * BLOCK, (j + 1) * BLOCK)
-                out[rows, shift + j * BLOCK : shift + (j + 1) * BLOCK] = (
-                    quant[rows, cols].astype(F32) * scale[i, j]
-                ).astype(BF16)
-
-    def body(gate, up, down, gate_s, up_s, down_s, gate_up_out, down_out):
-        put(gate_up_out, gate, gate_s, 0)
-        put(gate_up_out, up, up_s, units)
-        put(down_out, down, down_s, 0)
+    half = part // 2
+
+    def body(gate, up, down, gate_s, up_s, down_s, first, second):
+        for i in range(part // BLOCK):
+            rows = slice(i * BLOCK, (i + 1) * BLOCK)
+            out, at = (first, i * BLOCK) if i * BLOCK < half else (second, i * BLOCK - half)
+            for j in range(units // BLOCK):
+                cols = slice(j * BLOCK, (j + 1) * BLOCK)
+                tiles = (
+                    gate[rows, cols].astype(F32) * gate_s[i, j],
+                    up[rows, cols].astype(F32) * up_s[i, j],
+                    (down[cols, rows].astype(F32) * down_s[j, i]).T,
+                )
+                for k, tile in enumerate(tiles):
+                    to = k * units + j * BLOCK
+                    out[at : at + BLOCK, to : to + BLOCK] = tile.astype(BF16)
 
     quants, scales = [gate_quant, up_quant, down_quant], [gate_scale, up_scale, down_scale]
-    shapes = ((part, 2 * units), down_quant.shape)
-    return kernel_call(
-        body,
-        tuple(jax.ShapeDtypeStruct(v, BF16) for v in shapes),
-        60,
-        in_specs=[whole(v.shape) for v in quants]
-        + [pl.BlockSpec(memory_space=pltpu.SMEM)] * 3,
-        out_specs=tuple(whole(v) for v in shapes),
+    shape = (half, 3 * units)
+    return kernel_call(
+        body,
+        (jax.ShapeDtypeStruct(shape, BF16),) * 2,
+        16,
+        in_specs=[whole(v.shape) for v in quants] + [pl.BlockSpec(memory_space=pltpu.SMEM)] * 3,
+        out_specs=(whole(shape),) * 2,
     )(*quants, *scales)
 
 
-def pre_sums(rows, gate_up_parts, down_parts):
-    count = len(gate_up_parts)
-    part, both = gate_up_parts[0][1].shape
-    units = both // 2
+def pre_sums(rows, first_parts, second_parts):
+    count = len(first_parts)
+    half, wide = first_parts[0][1].shape
+    part, both = 2 * half, wide // 3 * 2
     slots = rows.shape[0]
     width = (rows.shape[1] - LANES) // 2
-    places = [r for r, _ in gate_up_parts]
-    assert places == [r for r, _ in down_parts]
+    places = [r for r, _ in first_parts]
+    assert places == [r for r, _ in second_parts]
 
     def body(rows_ref, *refs):
         weights, out = refs[: 2 * count], refs[2 * count]
-        x_in, dy_in, gate_up_in, down_in, sems = refs[2 * count + 1 :]
+        x_in, dy_in, weights_in, sems = refs[2 * count + 1 :]
         copies = []
         for i, r in enumerate(places):
+            pairs = (
+                (rows_ref.at[:, pl.ds(r * part, part)], x_in.at[i]),
+                (rows_ref.at[:, pl.ds(width + r * part, part)], dy_in.at[i]),
+                (weights[i], weights_in.at[i, pl.ds(0, half)]),
+                (weights[count + i], weights_in.at[i, pl.ds(half, half)]),
+            )
             copies.append(
                 [
-                    pltpu.make_async_copy(source, into.at[i], sems.at[k, i])
-                    for k, (source, into) in enumerate(
-                        (
-                            (rows_ref.at[:, pl.ds(r * part, part)], x_in),
-                            (rows_ref.at[:, pl.ds(width + r * part, part)], dy_in),
-                            (weights[i], gate_up_in),
-                            (weights[count + i], down_in),
-                        )
-                    )
+                    pltpu.make_async_copy(source, into, sems.at[k, i])
+                    for k, (source, into) in enumerate(pairs)
                 ]
             )
             for copy in copies[-1]:
@@ -113,15 +113,15 @@
         for i in range(count):
             for copy in copies[i]:
                 copy.wait()
-            one = contract(x_in[i], gate_up_in[i], 1, 0)
-            two = contract(dy_in[i], down_in[i], 1, 1)
+            one = contract(x_in[i], weights_in[i, :, :both], 1, 0)
+            two = contract(dy_in[i], weights_in[i, :, both:], 1, 0)
             pre = one if pre is None else pre + one
             back = two if back is None else back + two
         out[:, :both] = pre
         out[:, both:] = back
 
-    weights = [w for _, w in gate_up_parts] + [w for _, w in down_parts]
-    shape = (slots, both + units)
+    weights = [w for _, w in first_parts] + [w for _, w in second_parts]
+    shape = (slots, wide)
     return kernel_call(
         body,
         jax.ShapeDtypeStruct(shape, F32),
@@ -131,24 +131,26 @@
         scratch_shapes=[
             pltpu.VMEM((count, slots, part), BF16),
             pltpu.VMEM((count, slots, part), BF16),
-            pltpu.VMEM((count, part, both), BF16),
-            pltpu.VMEM((count, units, part), BF16),
+            pltpu.VMEM((count, part, wide), BF16),
             pltpu.SemaphoreType.DMA((4, count)),
         ],
     )(rows, *weights)
 
 
-def activations(rows, sums, gate_up_part, down_part):
+def activations(rows, sums, first_part, second_part):
     count = rows.shape[0]
-    far, w_gate_up = gate_up_part
-    w_down = down_part[1]
-    part, both = w_gate_up.shape
-    units = both // 2
+    far, first = first_part
+    second = second_part[1]
+    half, wide = first.shape
+    part, units = 2 * half, wide // 3
+    both = 2 * units
     width = (rows.shape[1] - LANES) // 2
 
-    def body(x_ref, dy_ref, prob_ref, sums_ref, gate_up_ref, down_ref, acts_ref, prob_out):
-        pre = sums_ref[:, :both] + contract(x_ref[...], gate_up_ref[...], 1, 0)
-        back = sums_ref[:, both:] + contract(dy_ref[...], down_ref[...], 1, 1)
+    def body(x_ref, dy_ref, prob_ref, sums_ref, first_ref, second_ref, acts_ref, prob_out):
+        pre = sums_ref[:, :both] + contract(x_ref[:, :half], first_ref[:, :both], 1, 0)
+        pre = pre + contract(x_ref[:, half:], second_ref[:, :both], 1, 0)
+        back = sums_ref[:, both:] + contract(dy_ref[:, :half], first_ref[:, both:], 1, 0)
+        back = back + contract(dy_ref[:, half:], second_ref[:, both:], 1, 0)
         gate_pre, up_pre = pre[:, :units], pre[:, units:]
         sigmoid_gate = jax.nn.sigmoid(gate_pre)
         hidden = (gate_pre * sigmoid_gate * up_pre).astype(BF16)
@@ -171,50 +173,58 @@
             block_at((count, part), (0, width // part + far)),
             block_at((count, LANES), (0, 2 * width // LANES)),
             whole(sums.shape),
-            whole(w_gate_up.shape),
-            whole(w_down.shape),
+            whole(first.shape),
+            whole(second.shape),
         ],
         out_specs=(whole(acts_shape), whole(prob_shape)),
-    )(rows, rows, rows, sums, w_gate_up, w_down)
-
-
-def slot_sums(core, acts, prob_lanes, gate_up_parts):
-    half = acts.shape[0] // 2
-    count = len(gate_up_parts)
-    part, both = gate_up_parts[0][1].shape
+    )(rows, rows, rows, sums, first, second)
+
+
+def slot_sums(core, acts, prob_lanes, first_parts, second_parts):
+    rows_half = acts.shape[0] // 2
+    count = len(first_parts)
+    half, wide = first_parts[0][1].shape
+    part, both = 2 * half, wide // 3 * 2
     width = count * part
-    places = [r for r, _ in gate_up_parts]
+    places = [r for r, _ in first_parts]
+    assert places == [r for r, _ in second_parts]
 
     def body(core_ref, acts_ref, prob_ref, *refs):
-        weights, give, keep, weights_in, sems = refs[:count], *refs[count:]
-        copies = [
-            pltpu.make_async_copy(weights[i], weights_in.at[i], sems.at[i]) for i in range(count)
-        ]
-        for copy in copies:
-            copy.start()
-        theirs = pl.ds(pl.multiple_of((1 - core_ref[0]) * half, half), half)
-        mine = pl.ds(pl.multiple_of(core_ref[0] * half, half), half)
+        weights, give, keep, weights_in, sems = refs[: 2 * count], *refs[2 * count :]
+        copies = []
+        for i in range(count):
+            for k in range(2):
+                copy = pltpu.make_async_copy(
+                    weights[k * count + i].at[:, pl.ds(0, both)],
+                    weights_in.at[i, pl.ds(k * half, half)],
+                    sems.at[k, i],
+                )
+                copy.start()
+                copies.append(copy)
+        theirs = pl.ds(pl.multiple_of((1 - core_ref[0]) * rows_half, rows_half), rows_half)
+        mine = pl.ds(pl.multiple_of(core_ref[0] * rows_half, rows_half), rows_half)
         acts = jnp.concatenate([acts_ref[theirs, :both], acts_ref[mine, :both]], axis=0)
         for i, r in enumerate(places):
-            copies[i].wait()
+            copies[2 * i].wait()
+            copies[2 * i + 1].wait()
             sums = contract(acts, weights_in[i], 1, 1).astype(BF16)
-            give[:, r * part : (r + 1) * part] = sums[:half]
-            keep[:, r * part : (r + 1) * part] = sums[half:]
+            give[:, r * part : (r + 1) * part] = sums[:rows_half]
+            keep[:, r * part : (r + 1) * part] = sums[rows_half:]
         give[:, width:] = prob_ref[theirs, :]
         keep[:, width:] = prob_ref[mine, :]
 
-    weights = [w for _, w in gate_up_parts]
-    shape = (half, width + LANES)
+    weights = [w for _, w in first_parts] + [w for _, w in second_parts]
+    shape = (rows_half, width + LANES)
     return kernel_call(
         body,
         (jax.ShapeDtypeStruct(shape, BF16),) * 2,
         60,
         scalars=1,
-        in_specs=[whole(acts.shape), whole(prob_lanes.shape)] + [far_memory()] * count,
+        in_specs=[whole(acts.shape), whole(prob_lanes.shape)] + [far_memory()] * (2 * count),
         out_specs=(whole(shape),) * 2,
         scratch_shapes=[
             pltpu.VMEM((count, part, both), BF16),
-            pltpu.SemaphoreType.DMA((count,)),
+            pltpu.SemaphoreType.DMA((2, count)),
         ],
     )(core, acts, prob_lanes, *weights)
 
@@ -313,11 +323,11 @@
         width = x_quant.shape[1]
         part = width // ring
 
-        w_gate_up, w_down = scaled_weights(
+        first, second = scaled_weights(
             gate_quant, gate_scale, up_quant, up_scale, down_quant, down_scale
         )
-        down_near, down_far = ring_gather(w_down, "fsdp", ring, False)
-        gate_up_near, gate_up_far = ring_gather(w_gate_up, "fsdp", ring, True)
+        first_near, first_far = ring_gather(first, "fsdp", ring, True)
+        second_near, second_far = ring_gather(second, "fsdp", ring, False)
 
         slot_rank = jnp.cumsum(route_mask) - 1
         slot_ids = jnp.arange(CAP, dtype=jnp.int32)
@@ -350,13 +360,18 @@
         rows = lax.all_gather(packed, CORE_FIRST, axis=0, tiled=True)
 
         sides = lax.all_to_all(sides, "fsdp", split_axis=0, concat_axis=0, tiled=True)
+        sides, *_ = lax.optimization_barrier(
+            (sides, *(w for _, w in first_near[1:3] + second_near[1:3]))
+        )
         columns = lax.all_gather(sides, CORE_FIRST, axis=1, tiled=True).reshape(-1, 2 * part)
 
-        sums = pre_sums(rows, gate_up_near, down_near)
-        acts, prob_lanes = activations(rows, sums, gate_up_far, down_far)
+        sums = pre_sums(rows, first_near, second_near)
+        acts, prob_lanes = activations(rows, sums, first_far, second_far)
         all_acts = lax.all_gather(acts, "fsdp", axis=0, tiled=True)
 
-        give, keep = slot_sums(core[None], acts, prob_lanes, [*gate_up_near, gate_up_far])
+        give, keep = slot_sums(
+            core[None], acts, prob_lanes, [*first_near, first_far], [*second_near, second_far]
+        )
         got = lax.ppermute(give, "core", [(0, 1), (1, 0)])
         both = pair_sum(keep, got).reshape(-1, CAP, width + LANES)
         shares = lax.all_to_all(both, PLANE, split_axis=0, concat_axis=0, tiled=True)

time: 203 us -> 187 us (0.921)
  waiting for transfers between devices: 78.8 us -> 50.5 us
  blocking collectives: 47 us -> 55.3 us
  starting transfers between devices: 22.6 us -> 25.6 us
    ppermute x6, waiting for transfers between devices: 54.9 us -> 20.7 us  [ring_gather(): ahead = lax.ppermute(ahead, axis, up)]
    all_to_all x1, blocking collectives: 17.8 us -> 26 us  [on_device(): lax.all_to_all(sides, 'fsdp', split_axis=0, concat_axis=0, tiled=True)]
    ppermute x6, starting transfers between devices: 0.08 us -> 5.74 us  [ring_gather(): ahead = lax.ppermute(ahead, axis, up)]
    ppermute x1, waiting for transfers between devices: 0.01 us -> 5.56 us  [ring_gather(): lax.ppermute(ahead, axis, up)]
    all_gather x1, waiting for transfers between devices: 0.01 us -> 2.57 us  [on_device(): all_acts = lax.all_gather(acts, 'fsdp', axis=0, tiled=True)]
    ppermute x6, waiting for transfers between devices: 20.5 us -> 18.4 us  [ring_gather(): behind = lax.ppermute(behind, axis, down)]
    ppermute x1, starting transfers between devices: 6.07 us -> 3.92 us  [on_device(): got = lax.ppermute(give, 'core', [(0, 1), (1, 0)])]
    unnamed x37 -> x47, local copies, waits for them, and re-layouts: 5.26 us -> 5.03 us
  transfers between devices with their start and end apart: 18 -> 18, of which waited for: 8 -> 7; matrix products, arithmetic and copies ran while one was open for 2% -> 2% of each run, Pallas kernels for 10% -> 11%
where the time goes in v2:
time: 187 us; the launch traced here: 186 us
  blocking collectives  55.3 us (30%)
  waiting for transfers between devices  50.5 us (27%)
  Pallas kernels  26.9 us (14%)
  starting transfers between devices  25.6 us (14%)
  between operations  14.1 us (8%)
  local copies, waits for them, and re-layouts  6.12 us (3%)
  other arithmetic  4.68 us (3%)
  matrix products  3.16 us (2%)
    all_to_all x1, blocking collectives, on_device(): lax.all_to_all(both, PLANE, split_axis=0, concat_axis=0, tiled=True)  29.2 us
    all_to_all x1, blocking collectives, on_device(): lax.all_to_all(sides, 'fsdp', split_axis=0, concat_axis=0, tiled=True)  26 us
    ppermute x6, waiting for transfers between devices, ring_gather(): ahead = lax.ppermute(ahead, axis, up)  20.7 us
    ppermute x6, waiting for transfers between devices, ring_gather(): behind = lax.ppermute(behind, axis, down)  18.4 us
    ppermute x6, starting transfers between devices, ring_gather(): behind = lax.ppermute(behind, axis, down)  12.9 us
    pallas_call x1, Pallas kernels, slot_sums(): kernel_call(body, (jax.ShapeDtypeStruct(shape, BF16),) * 2, 60, scalars=1...  7.79 us
    pallas_call x1, Pallas kernels, weight_sums(): kernel_call(body, (jax.ShapeDtypeStruct((part, units), F32), jax.ShapeDty...  7.22 us
    pallas_call x1, Pallas kernels, pre_sums(): kernel_call(body, jax.ShapeDtypeStruct(shape, F32), 60, in_specs=[far_mem...  6.83 us
  transfers between devices with their start and end apart: 18, of which 7 were waited for; matrix products, arithmetic and copies ran while one was open for 2% of the time, Pallas kernels for 11%

profile of v2, /device:TPU:1, one launch (start us, length us, event | category | flops | bytes accessed | tf_op | source)
XLA Modules:
  0.0 186.3 jit_solution(6610689647357060449)
XLA Ops:
  7.2 0.8 convert_element_type.39
  8.7 0.8 copy.34
  9.9 1.0 multiply_convert_fusion
  13.2 1.0 copy-done.6
  14.2 1.0 shard_map.146
  15.2 2.5 %collective-permute-start = (bf16[384,768]{1,0:T(8,128)(2,1)S(1)}, bf16[384,768]{1,0:T(8,128)(2,1)S(1)}, u32[]{:S(2)}, u32[]{:S(2)}) collective-permute-start(bf16[384,768]{1,0:T(8,128)(2,1)S(1)} %get-tuple-element.15.refs_0_), channel_id=1, source_target_pairs={{0,32},{32,64},{64,96},{96,128},{128,160},{160,192},{192,224},{224... | collective-permute-start | bytes 1769480 | tf_op jit(solution)/shard_map/ppermute | solution.py:298
  17.8 4.0 %collective-permute-start.1 = (bf16[384,768]{1,0:T(8,128)(2,1)S(1)}, bf16[384,768]{1,0:T(8,128)(2,1)}, u32[]{:S(2)}, u32[]{:S(2)}) collective-permute-start(bf16[384,768]{1,0:T(8,128)(2,1)S(1)} %get-tuple-element.15.refs_0_), channel_id=1, source_target_pairs={{0,224},{32,0},{64,32},{96,64},{128,96},{160,128},{192,160},{224,1... | collective-permute-start | bytes 1769480 | tf_op jit(solution)/shard_map/ppermute | solution.py:299
  21.8 2.7 %collective-permute-start.7 = (bf16[384,768]{1,0:T(8,128)(2,1)S(1)}, bf16[384,768]{1,0:T(8,128)(2,1)}, u32[]{:S(2)}, u32[]{:S(2)}) collective-permute-start(bf16[384,768]{1,0:T(8,128)(2,1)S(1)} %get-tuple-element.16.refs_7_.refs_8_), channel_id=1, source_target_pairs={{0,224},{32,0},{64,32},{96,64},{128,96},{160,128},{192,160},{224,1... | collective-permute-start | bytes 1769480 | tf_op jit(solution)/shard_map/ppermute | solution.py:299
  24.5 1.0 maximum_bitcast_fusion
  25.5 26.0 %all_to_all.10 = bf16[8,8,1536]{2,1,0:T(8,128)(2,1)} all-to-all(bf16[8,8,1536]{2,1,0:T(8,128)(2,1)S(1)} %maximum_bitcast_fusion), channel_id=1, replica_groups=mesh['fsdp'=8,'x'=4,'y'=4,'core'=2] {'fsdp'}, dimensions={0} | all-to-all | bytes 393216 | tf_op jit(solution)/shard_map/all_to_all | solution.py:362
  51.6 2.3 %collective-permute-start.2 = (bf16[384,768]{1,0:T(8,128)(2,1)S(1)}, bf16[384,768]{1,0:T(8,128)(2,1)S(1)}, u32[]{:S(2)}, u32[]{:S(2)}) collective-permute-start(bf16[384,768]{1,0:T(8,128)(2,1)S(1)} %collective-permute-done.refs_1_), channel_id=1, source_target_pairs={{0,32},{32,64},{64,96},{96,128},{128,160},{160,192},{192,224},{224... | collective-permute-start | bytes 1769480 | tf_op jit(solution)/shard_map/ppermute | solution.py:298
  54.8 0.9 collective-permute-start.8
  55.8 9.9 %collective-permute-done.2.refs_3_ = bf16[384,768]{1,0:T(8,128)(2,1)S(1)} collective-permute-done((bf16[384,768]{1,0:T(8,128)(2,1)S(1)}, bf16[384,768]{1,0:T(8,128)(2,1)S(1)}, u32[]{:S(2)}, u32[]{:S(2)}) %collective-permute-start.2) | collective-permute-done | bytes 589856 | tf_op jit(solution)/shard_map/ppermute | solution.py:298
  65.7 2.7 %collective-permute-start.11 = (bf16[384,768]{1,0:T(8,128)(2,1)S(1)}, bf16[384,768]{1,0:T(8,128)(2,1)}, u32[]{:S(2)}, u32[]{:S(2)}) collective-permute-start(bf16[384,768]{1,0:T(8,128)(2,1)S(1)} %collective-permute-done.9.refs_11_.refs_12_), channel_id=1, source_target_pairs={{0,224},{32,0},{64,32},{96,64},{128,96},{160,128},{192,160},{224,1... | collective-permute-start | bytes 1769480 | tf_op jit(solution)/shard_map/ppermute | solution.py:299
  68.3 9.3 %collective-permute-done.3.refs_4_ = bf16[384,768]{1,0:T(8,128)(2,1)S(1)} collective-permute-done((bf16[384,768]{1,0:T(8,128)(2,1)}, bf16[384,768]{1,0:T(8,128)(2,1)S(1)}, u32[]{:S(2)}, u32[]{:S(2)}) %collective-permute-start.3) | collective-permute-done | bytes 589856 | tf_op jit(solution)/shard_map/ppermute | solution.py:299
  77.6 2.5 %collective-permute-start.5 = (bf16[384,768]{1,0:T(8,128)(2,1)S(1)}, bf16[384,768]{1,0:T(8,128)(2,1)S(1)}, u32[]{:S(2)}, u32[]{:S(2)}) collective-permute-start(bf16[384,768]{1,0:T(8,128)(2,1)S(1)} %collective-permute-done.3.refs_4_), channel_id=1, source_target_pairs={{0,224},{32,0},{64,32},{96,64},{128,96},{160,128},{192,160},{224,1... | collective-permute-start | bytes 1769480 | tf_op jit(solution)/shard_map/ppermute | solution.py:299
  80.1 10.8 %collective-permute-done.4.refs_5_ = bf16[384,768]{1,0:T(8,128)(2,1)} collective-permute-done((bf16[384,768]{1,0:T(8,128)(2,1)S(1)}, bf16[384,768]{1,0:T(8,128)(2,1)}, u32[]{:S(2)}, u32[]{:S(2)}) %collective-permute-start.4) | collective-permute-done | bytes 589856 | tf_op jit(solution)/shard_map/ppermute | solution.py:298
  90.9 2.9 %collective-permute-start.13 = (bf16[384,768]{1,0:T(8,128)(2,1)}, bf16[384,768]{1,0:T(8,128)(2,1)}, u32[]{:S(2)}, u32[]{:S(2)}) collective-permute-start(bf16[384,768]{1,0:T(8,128)(2,1)} %collective-permute-done.11.refs_13_.refs_14_), channel_id=1, source_target_pairs={{0,224},{32,0},{64,32},{96,64},{128,96},{160,128},{192,160},{224,1... | collective-permute-start | bytes 1769480 | tf_op jit(solution)/shard_map/ppermute | solution.py:301
  93.9 9.1 %collective-permute-done.5.refs_6_ = bf16[384,768]{1,0:T(8,128)(2,1)S(1)} collective-permute-done((bf16[384,768]{1,0:T(8,128)(2,1)S(1)}, bf16[384,768]{1,0:T(8,128)(2,1)S(1)}, u32[]{:S(2)}, u32[]{:S(2)}) %collective-permute-start.5) | collective-permute-done | bytes 589856 | tf_op jit(solution)/shard_map/ppermute | solution.py:299
  103.0 0.8 copy-done.14
  103.8 6.8 %shard_map.147.sums_ref = f32[256,768]{1,0:T(8,128)} custom-call(bf16[256,12416]{1,0:T(8,128)(2,1)} %all-gather.4.cloned.1.call-done.rows_ref.x_ref.dy_ref.prob_ref, bf16[384,768]{1,0:T(8,128)(2,1)} %copy-done.1, bf16[384,768]{1,0:T(8,128)(2,1)} %copy-done.9, bf16[384,768]{1,0:T(8,128)(2,1)} %collective-permute-done.1.refs_2_, bf16[384,768]{1,0:T(8,128)(2,1)} %copy-done.10, ...), custom_call_target="tpu_custom_call" | custom-call | tf_op jit(solution)/shard_map/pallas_call | solution.py:125
  110.6 5.6 %collective-permute-done.12.first_ref.refs_7_ = bf16[384,768]{1,0:T(8,128)(2,1)S(1)} collective-permute-done((bf16[384,768]{1,0:T(8,128)(2,1)}, bf16[384,768]{1,0:T(8,128)(2,1)S(1)}, u32[]{:S(2)}, u32[]{:S(2)}) %collective-permute-start.12) | collective-permute-done | bytes 589856 | tf_op jit(solution)/shard_map/ppermute | solution.py:301
  116.2 0.8 copy-done.8
  117.0 3.4 %shard_map.148 = (bf16[256,768]{1,0:T(8,128)(2,1)}, bf16[256,128]{1,0:T(8,128)(2,1)}) custom-call(bf16[256,12416]{1,0:T(8,128)(2,1)} %all-gather.4.cloned.1.call-done.rows_ref.x_ref.dy_ref.prob_ref, bf16[256,12416]{1,0:T(8,128)(2,1)} %all-gather.4.cloned.1.call-done.rows_ref.x_ref.dy_ref.prob_ref, ...), custom_call_target="tpu_custom_call" | custom-call | tf_op jit(solution)/shard_map/pallas_call | solution.py:167
  120.5 7.8 %shard_map.149 = (bf16[128,6272]{1,0:T(8,128)(2,1)}, bf16[128,6272]{1,0:T(8,128)(2,1)}) custom-call(s32[1]{0:T(128)} %bitcast.1.core_ref, bf16[256,768]{1,0:T(8,128)(2,1)} %get-tuple-element.17.acts_ref, bf16[256,128]{1,0:T(8,128)(2,1)} %get-tuple-element.18.prob_ref, bf16[384,768]{1,0:T(8,128)(2,1)} %copy-done.1, bf16[384,768]{1,0:T(8,128)(2,1)} %copy-done.9, ...), custom_call_target="tpu_custom_call" | custom-call | tf_op jit(solution)/shard_map/pallas_call | solution.py:218
  128.3 3.9 %collective-permute-start.14 = (bf16[128,6272]{1,0:T(8,128)(2,1)}, bf16[128,6272]{1,0:T(8,128)(2,1)S(1)}, u32[]{:S(2)}, u32[]{:S(2)}) collective-permute-start(bf16[128,6272]{1,0:T(8,128)(2,1)} %get-tuple-element.20), channel_id=1, source_target_pairs={{0,1},{1,0},{2,3},{3,2},{4,5},{5,4},{6,7},{7,6},{8,9},{9,8},{10,11... | collective-permute-start | bytes 4816904 | tf_op jit(solution)/shard_map/ppermute | solution.py:375
  132.2 3.3 %collective-permute-done.14.b_ref = bf16[128,6272]{1,0:T(8,128)(2,1)S(1)} collective-permute-done((bf16[128,6272]{1,0:T(8,128)(2,1)}, bf16[128,6272]{1,0:T(8,128)(2,1)S(1)}, u32[]{:S(2)}, u32[]{:S(2)}) %collective-permute-start.14) | collective-permute-done | bytes 1605664 | tf_op jit(solution)/shard_map/ppermute | solution.py:375
  135.5 1.4 copy-done.3
  137.6 29.2 %all_to_all.11 = bf16[16,8,6272]{2,1,0:T(8,128)(2,1)S(1)} all-to-all(bf16[16,8,6272]{2,1,0:T(8,128)(2,1)S(1)} %bitcast.22), channel_id=1, replica_groups=mesh['fsdp'=8,'x'=4,'y'=4,'core'=2] {'x','y'}, dimensions={0} | all-to-all | bytes 3211264 | tf_op jit(solution)/shard_map/all_to_all | solution.py:377
  168.2 1.8 convolution_convert_fusion
  170.0 2.6 %all-gather.8.cloned.1.call-done.acts_ref = bf16[2048,768]{1,0:T(8,128)(2,1)} async-done(((bf16[256,768]{1,0:T(8,128)(2,1)}), bf16[2048,768]{1,0:T(8,128)(2,1)}) %all-gather.8.cloned.1.call-update) | async-done | bytes 3145744 | tf_op jit(solution)/shard_map/all_gather | solution.py:370
  172.6 7.2 %shard_map.151 = (f32[768,256]{1,0:T(8,128)}, f32[768,256]{1,0:T(8,128)}, f32[256,768]{1,0:T(8,128)}) custom-call(bf16[2048,1536]{1,0:T(8,128)(2,1)} %bitcast.23, bf16[2048,1536]{1,0:T(8,128)(2,1)} %bitcast.24, bf16[2048,768]{1,0:T(8,128)(2,1)} %all-gather.8.cloned.1.call-done.acts_ref), custom_call_target="tpu_custom_call" | custom-call | tf_op jit(solution)/shard_map/pallas_call | solution.py:263
  (87 shorter events, 6.6 us)
Async XLA Ops:
  7.2 2.7 %copy-start = (bf16[128,6144]{1,0:T(8,128)(2,1)S(1)}, bf16[128,6144]{1,0:T(8,128)(2,1)}, u32[]{:S(2)}) copy-start(bf16[128,6144]{1,0:T(8,128)(2,1)} %param.13) | copy-start | bytes 4718596
  7.2 3.6 %copy-start.17 = (f32[128,48]{0,1:T(8,128)S(1)}, f32[128,48]{0,1:T(8,128)}, u32[]{:S(2)}) copy-start(f32[128,48]{0,1:T(8,128)} %param.12) | copy-start | bytes 73732
  7.2 96.6 %all-gather.4.cloned.1.call-start = ((), (), s32[]{:S(2)}) async-start(), calls=%async_computation.2 | async-start | bytes 6555648 | tf_op jit(solution)/shard_map/all_gather | solution.py:360
  8.7 2.7 %copy-start.18 = (pred[128]{0:T(512)(128)(4,1)}, pred[128]{0:T(512)(128)(4,1)S(1)}, u32[]{:S(2)}) copy-start(pred[128]{0:T(512)(128)(4,1)S(1)} %broadcast_compare_fusion) | copy-start | bytes 388
  11.0 2.1 %copy-start.21 = (f32[6,2]{0,1:T(2,128)S(1)}, f32[6,2]{0,1:T(2,128)}, u32[]{:S(2)}) copy-start(f32[6,2]{0,1:T(2,128)} %param.19) | copy-start | bytes 148
  11.0 2.2 %copy-start.4 = (bf16[768,256]{1,0:T(8,128)(2,1)S(1)}, bf16[768,256]{1,0:T(8,128)(2,1)}, u32[]{:S(2)}) copy-start(bf16[768,256]{1,0:T(8,128)(2,1)} %gate.1) | copy-start | bytes 1179652
  11.0 2.2 %copy-start.5 = (bf16[768,256]{1,0:T(8,128)(2,1)S(1)}, bf16[768,256]{1,0:T(8,128)(2,1)}, u32[]{:S(2)}) copy-start(bf16[768,256]{1,0:T(8,128)(2,1)} %up.1) | copy-start | bytes 1179652
  11.0 2.2 %copy-start.7 = (f32[2,6]{1,0:T(2,128)S(1)}, f32[2,6]{1,0:T(2,128)}, u32[]{:S(2)}) copy-start(f32[2,6]{1,0:T(2,128)} %down_s.1) | copy-start | bytes 148
  13.0 157.0 %all-gather.6.cloned.1.call-start = ((), (), s32[]{:S(2)}) async-start(), calls=%async_computation.3 | async-start | bytes 6488064 | tf_op jit(solution)/shard_map/all_gather | solution.py:366
  15.2 88.6 %copy-start.1 = (bf16[384,768]{1,0:T(8,128)(2,1)}, bf16[384,768]{1,0:T(8,128)(2,1)S(1)}, u32[]{:S(2)}) copy-start(bf16[384,768]{1,0:T(8,128)(2,1)S(1)} %get-tuple-element.15.refs_0_) | copy-start | bytes 1769476
  15.2 88.6 %copy-start.2 = (bf16[384,768]{1,0:T(8,128)(2,1)}, bf16[384,768]{1,0:T(8,128)(2,1)S(1)}, u32[]{:S(2)}) copy-start(bf16[384,768]{1,0:T(8,128)(2,1)S(1)} %get-tuple-element.16.refs_7_.refs_8_) | copy-start | bytes 1769476
  15.2 36.2 %collective-permute-start = (bf16[384,768]{1,0:T(8,128)(2,1)S(1)}, bf16[384,768]{1,0:T(8,128)(2,1)S(1)}, u32[]{:S(2)}, u32[]{:S(2)}) collective-permute-start(bf16[384,768]{1,0:T(8,128)(2,1)S(1)} %get-tuple-element.15.refs_0_), channel_id=1, source_target_pairs={{0,32},{32,64},{64,96},{96,128},{128,160},{160,192},{192,224},{224... | collective-permute-start | bytes 1769480 | tf_op jit(solution)/shard_map/ppermute | solution.py:298
  17.8 33.7 %collective-permute-start.1 = (bf16[384,768]{1,0:T(8,128)(2,1)S(1)}, bf16[384,768]{1,0:T(8,128)(2,1)}, u32[]{:S(2)}, u32[]{:S(2)}) collective-permute-start(bf16[384,768]{1,0:T(8,128)(2,1)S(1)} %get-tuple-element.15.refs_0_), channel_id=1, source_target_pairs={{0,224},{32,0},{64,32},{96,64},{128,96},{160,128},{192,160},{224,1... | collective-permute-start | bytes 1769480 | tf_op jit(solution)/shard_map/ppermute | solution.py:299
  21.8 29.6 %collective-permute-start.6 = (bf16[384,768]{1,0:T(8,128)(2,1)S(1)}, bf16[384,768]{1,0:T(8,128)(2,1)}, u32[]{:S(2)}, u32[]{:S(2)}) collective-permute-start(bf16[384,768]{1,0:T(8,128)(2,1)S(1)} %get-tuple-element.16.refs_7_.refs_8_), channel_id=1, source_target_pairs={{0,32},{32,64},{64,96},{96,128},{128,160},{160,192},{192,224},{224... | collective-permute-start | bytes 1769480 | tf_op jit(solution)/shard_map/ppermute | solution.py:298
  21.8 29.7 %collective-permute-start.7 = (bf16[384,768]{1,0:T(8,128)(2,1)S(1)}, bf16[384,768]{1,0:T(8,128)(2,1)}, u32[]{:S(2)}, u32[]{:S(2)}) collective-permute-start(bf16[384,768]{1,0:T(8,128)(2,1)S(1)} %get-tuple-element.16.refs_7_.refs_8_), channel_id=1, source_target_pairs={{0,224},{32,0},{64,32},{96,64},{128,96},{160,128},{192,160},{224,1... | collective-permute-start | bytes 1769480 | tf_op jit(solution)/shard_map/ppermute | solution.py:299
  51.5 28.6 %copy-start.9 = (bf16[384,768]{1,0:T(8,128)(2,1)}, bf16[384,768]{1,0:T(8,128)(2,1)S(1)}, u32[]{:S(2)}) copy-start(bf16[384,768]{1,0:T(8,128)(2,1)S(1)} %collective-permute-done.refs_1_) | copy-start | bytes 1769476
  51.5 121.0 %all-gather.8.cloned.1.call-start = ((), (), s32[]{:S(2)}) async-start(), calls=%async_computation.4 | async-start | bytes 3538944 | tf_op jit(solution)/shard_map/all_gather | solution.py:370
  51.6 14.1 %collective-permute-start.2 = (bf16[384,768]{1,0:T(8,128)(2,1)S(1)}, bf16[384,768]{1,0:T(8,128)(2,1)S(1)}, u32[]{:S(2)}, u32[]{:S(2)}) collective-permute-start(bf16[384,768]{1,0:T(8,128)(2,1)S(1)} %collective-permute-done.refs_1_), channel_id=1, source_target_pairs={{0,32},{32,64},{64,96},{96,128},{128,160},{160,192},{192,224},{224... | collective-permute-start | bytes 1769480 | tf_op jit(solution)/shard_map/ppermute | solution.py:298
  53.8 11.8 %collective-permute-start.9 = (bf16[384,768]{1,0:T(8,128)(2,1)}, bf16[384,768]{1,0:T(8,128)(2,1)S(1)}, u32[]{:S(2)}, u32[]{:S(2)}) collective-permute-start(bf16[384,768]{1,0:T(8,128)(2,1)} %collective-permute-done.7.refs_9_.refs_10_), channel_id=1, source_target_pairs={{0,224},{32,0},{64,32},{96,64},{128,96},{160,128},{192,160},{224,1... | collective-permute-start | bytes 1769480 | tf_op jit(solution)/shard_map/ppermute | solution.py:299
  54.3 23.3 %collective-permute-start.3 = (bf16[384,768]{1,0:T(8,128)(2,1)}, bf16[384,768]{1,0:T(8,128)(2,1)S(1)}, u32[]{:S(2)}, u32[]{:S(2)}) collective-permute-start(bf16[384,768]{1,0:T(8,128)(2,1)} %collective-permute-done.1.refs_2_), channel_id=1, source_target_pairs={{0,224},{32,0},{64,32},{96,64},{128,96},{160,128},{192,160},{224,1... | collective-permute-start | bytes 1769480 | tf_op jit(solution)/shard_map/ppermute | solution.py:299
  54.8 25.2 %collective-permute-start.8 = (bf16[384,768]{1,0:T(8,128)(2,1)}, bf16[384,768]{1,0:T(8,128)(2,1)S(1)}, u32[]{:S(2)}, u32[]{:S(2)}) collective-permute-start(bf16[384,768]{1,0:T(8,128)(2,1)} %collective-permute-done.6.refs_8_.refs_9_), channel_id=1, source_target_pairs={{0,32},{32,64},{64,96},{96,128},{128,160},{160,192},{192,224},{224... | collective-permute-start | bytes 1769480 | tf_op jit(solution)/shard_map/ppermute | solution.py:298
  65.6 25.3 %copy-start.10 = (bf16[384,768]{1,0:T(8,128)(2,1)}, bf16[384,768]{1,0:T(8,128)(2,1)S(1)}, u32[]{:S(2)}) copy-start(bf16[384,768]{1,0:T(8,128)(2,1)S(1)} %collective-permute-done.2.refs_3_) | copy-start | bytes 1769476
  65.6 25.3 %collective-permute-start.4 = (bf16[384,768]{1,0:T(8,128)(2,1)S(1)}, bf16[384,768]{1,0:T(8,128)(2,1)}, u32[]{:S(2)}, u32[]{:S(2)}) collective-permute-start(bf16[384,768]{1,0:T(8,128)(2,1)S(1)} %collective-permute-done.2.refs_3_), channel_id=1, source_target_pairs={{0,32},{32,64},{64,96},{96,128},{128,160},{160,192},{192,224},{224... | collective-permute-start | bytes 1769480 | tf_op jit(solution)/shard_map/ppermute | solution.py:298
  65.6 25.3 %copy-start.11 = (bf16[384,768]{1,0:T(8,128)(2,1)}, bf16[384,768]{1,0:T(8,128)(2,1)S(1)}, u32[]{:S(2)}) copy-start(bf16[384,768]{1,0:T(8,128)(2,1)S(1)} %collective-permute-done.9.refs_11_.refs_12_) | copy-start | bytes 1769476
  65.7 25.3 %collective-permute-start.11 = (bf16[384,768]{1,0:T(8,128)(2,1)S(1)}, bf16[384,768]{1,0:T(8,128)(2,1)}, u32[]{:S(2)}, u32[]{:S(2)}) collective-permute-start(bf16[384,768]{1,0:T(8,128)(2,1)S(1)} %collective-permute-done.9.refs_11_.refs_12_), channel_id=1, source_target_pairs={{0,224},{32,0},{64,32},{96,64},{128,96},{160,128},{192,160},{224,1... | collective-permute-start | bytes 1769480 | tf_op jit(solution)/shard_map/ppermute | solution.py:299
  77.6 13.4 %copy-start.12 = (bf16[384,768]{1,0:T(8,128)(2,1)}, bf16[384,768]{1,0:T(8,128)(2,1)S(1)}, u32[]{:S(2)}) copy-start(bf16[384,768]{1,0:T(8,128)(2,1)S(1)} %collective-permute-done.3.refs_4_) | copy-start | bytes 1769476
  77.6 25.4 %collective-permute-start.5 = (bf16[384,768]{1,0:T(8,128)(2,1)S(1)}, bf16[384,768]{1,0:T(8,128)(2,1)S(1)}, u32[]{:S(2)}, u32[]{:S(2)}) collective-permute-start(bf16[384,768]{1,0:T(8,128)(2,1)S(1)} %collective-permute-done.3.refs_4_), channel_id=1, source_target_pairs={{0,224},{32,0},{64,32},{96,64},{128,96},{160,128},{192,160},{224,1... | collective-permute-start | bytes 1769480 | tf_op jit(solution)/shard_map/ppermute | solution.py:299
  80.1 22.9 %copy-start.13 = (bf16[384,768]{1,0:T(8,128)(2,1)}, bf16[384,768]{1,0:T(8,128)(2,1)S(1)}, u32[]{:S(2)}) copy-start(bf16[384,768]{1,0:T(8,128)(2,1)S(1)} %collective-permute-done.8.refs_10_.refs_11_) | copy-start | bytes 1769476
  80.1 23.7 %collective-permute-start.10 = (bf16[384,768]{1,0:T(8,128)(2,1)S(1)}, bf16[384,768]{1,0:T(8,128)(2,1)}, u32[]{:S(2)}, u32[]{:S(2)}) collective-permute-start(bf16[384,768]{1,0:T(8,128)(2,1)S(1)} %collective-permute-done.8.refs_10_.refs_11_), channel_id=1, source_target_pairs={{0,32},{32,64},{64,96},{96,128},{128,160},{160,192},{192,224},{224... | collective-permute-start | bytes 1769480 | tf_op jit(solution)/shard_map/ppermute | solution.py:298
  90.9 25.3 %collective-permute-start.12 = (bf16[384,768]{1,0:T(8,128)(2,1)}, bf16[384,768]{1,0:T(8,128)(2,1)S(1)}, u32[]{:S(2)}, u32[]{:S(2)}) collective-permute-start(bf16[384,768]{1,0:T(8,128)(2,1)} %collective-permute-done.4.refs_5_), channel_id=1, source_target_pairs={{0,32},{32,64},{64,96},{96,128},{128,160},{160,192},{192,224},{224... | collective-permute-start | bytes 1769480 | tf_op jit(solution)/shard_map/ppermute | solution.py:301
  90.9 25.3 %collective-permute-start.13 = (bf16[384,768]{1,0:T(8,128)(2,1)}, bf16[384,768]{1,0:T(8,128)(2,1)}, u32[]{:S(2)}, u32[]{:S(2)}) collective-permute-start(bf16[384,768]{1,0:T(8,128)(2,1)} %collective-permute-done.11.refs_13_.refs_14_), channel_id=1, source_target_pairs={{0,224},{32,0},{64,32},{96,64},{128,96},{160,128},{192,160},{224,1... | collective-permute-start | bytes 1769480 | tf_op jit(solution)/shard_map/ppermute | solution.py:301
  128.3 7.2 %collective-permute-start.14 = (bf16[128,6272]{1,0:T(8,128)(2,1)}, bf16[128,6272]{1,0:T(8,128)(2,1)S(1)}, u32[]{:S(2)}, u32[]{:S(2)}) collective-permute-start(bf16[128,6272]{1,0:T(8,128)(2,1)} %get-tuple-element.20), channel_id=1, source_target_pairs={{0,1},{1,0},{2,3},{3,2},{4,5},{5,4},{6,7},{7,6},{8,9},{9,8},{10,11... | collective-permute-start | bytes 4816904 | tf_op jit(solution)/shard_map/ppermute | solution.py:375
  (8 other events, 8.9 us)
Sparse Core Ops, SparseCore 0:
  13.1 58.4 all-gather.3
  74.2 53.1 all-gather.5
  129.1 43.3 all-gather.7

commit v3 on v2

--- a/solution.py
+++ b/solution.py
@@ -248,17 +248,41 @@
     )(mine, other)
 
 
-def weight_sums(columns, acts):
-    slots, twice = columns.shape
-    part, units = twice // 2, acts.shape[1] // 3
+def turned_features(columns, part):
+    slots = columns.shape[0]
+    tile = 256
+
+    def body(x_ref, out):
+        out[...] = x_ref[...].astype(F32).T.astype(BF16)
+
+    return kernel_call(
+        body,
+        jax.ShapeDtypeStruct((part, slots), BF16),
+        16,
+        grid=(slots // tile,),
+        in_specs=[pl.BlockSpec((tile, part), lambda i: (i, 0))],
+        out_specs=pl.BlockSpec((part, tile), lambda i: (0, i)),
+    )(columns)
+
+
+def weight_sums(features, columns, acts):
+    part, slots = features.shape
+    units = acts.shape[1] // 3
     tile = 256
     steps = part // tile
 
-    def body(x_ref, weighted_ref, acts_ref, gate_out, up_out, down_out):
-        both = contract(x_ref[...], acts_ref[:, : 2 * units], 0, 0)
+    def body(x_ref, weighted_ref, acts_ref, gate_out, up_out, down_out, hidden):
+        @pl.when(pl.program_id(0) == 0)
+        def _():
+            for at in range(0, slots, tile):
+                hidden[:, at : at + tile] = (
+                    acts_ref[at : at + tile, 2 * units :].astype(F32).T.astype(BF16)
+                )
+
+        both = contract(x_ref[...], acts_ref[:, : 2 * units], 1, 0)
         gate_out[...] = both[:, :units]
         up_out[...] = both[:, units:]
-        down_out[...] = contract(acts_ref[:, 2 * units :], weighted_ref[...], 0, 0)
+        down_out[...] = contract(hidden[...], weighted_ref[...], 1, 0)
 
     return kernel_call(
         body,
@@ -270,7 +294,7 @@
         60,
         grid=(steps,),
         in_specs=[
-            pl.BlockSpec((slots, tile), lambda i: (0, i)),
+            pl.BlockSpec((tile, slots), lambda i: (i, 0)),
             pl.BlockSpec((slots, tile), lambda i: (0, steps + i)),
             whole(acts.shape),
         ],
@@ -279,7 +303,64 @@
             pl.BlockSpec((tile, units), lambda i: (i, 0)),
             pl.BlockSpec((units, tile), lambda i: (0, i)),
         ),
-    )(columns, columns, acts)
+        scratch_shapes=[pltpu.VMEM((units, slots), BF16)],
+    )(features, columns, acts)
+
+
+def pick_slots(place, mask, prob, x_quant, x_scale, grad_out, ring):
+    tokens, width = x_quant.shape
+    part = width // ring
+
+    def body(place_ref, mask_ref, prob_ref, x_ref, scale_ref, dy_ref, rows, sides, slot_out):
+        mask = mask_ref[...]
+        earlier = lax.broadcasted_iota(jnp.int32, (tokens, tokens), 0)
+        later = lax.broadcasted_iota(jnp.int32, (tokens, tokens), 1)
+        upto = (earlier <= later).astype(F32).astype(BF16)
+        ones = jnp.broadcast_to(mask, (CAP, tokens)).astype(F32)
+        rank = contract(ones.astype(BF16), upto, 1, 0) - 1.0
+        wanted = lax.broadcasted_iota(jnp.int32, (CAP, tokens), 0).astype(F32)
+        table = jnp.where((rank == wanted) & (ones == 1.0), 1.0, 0.0)
+        slot_out[...] = jnp.where(mask == 1, rank[:1].astype(jnp.int32), -1)
+        picked = table.astype(BF16)
+        scale = lax.dot_general(
+            table,
+            scale_ref[...],
+            (((1,), (0,)), ((), ())),
+            precision=lax.Precision.HIGHEST,
+            preferred_element_type=F32,
+        )
+        slot_prob = jnp.sum(table * prob_ref[...].astype(F32), axis=1, keepdims=True)
+        for d in range(ring):
+            cols = slice(d * part, (d + 1) * part)
+            turned = ((place_ref[0] - d) & (ring - 1)) * part
+            quant = contract(picked, x_ref[:, cols], 1, 0)
+            x = jnp.concatenate(
+                [
+                    quant[:, k * BLOCK : (k + 1) * BLOCK]
+                    * scale[:, d * part // BLOCK + k : d * part // BLOCK + k + 1]
+                    for k in range(part // BLOCK)
+                ],
+                axis=1,
+            ).astype(BF16)
+            dy = contract(picked, dy_ref[:, cols], 1, 0)
+            rows[:, pl.ds(pl.multiple_of(turned, BLOCK), part)] = x
+            rows[:, pl.ds(pl.multiple_of(width + turned, BLOCK), part)] = dy.astype(BF16)
+            sides[d, :, :part] = x
+            sides[d, :, part:] = (slot_prob * dy).astype(BF16)
+        rows[:, 2 * width :] = jnp.broadcast_to(slot_prob, (CAP, LANES)).astype(BF16)
+
+    shapes = ((CAP, 2 * width + LANES), (ring, CAP, 2 * part), (1, tokens))
+    inputs = [mask.reshape(1, tokens), prob.reshape(1, tokens), x_quant, x_scale, grad_out]
+    return kernel_call(
+        body,
+        tuple(
+            jax.ShapeDtypeStruct(v, t) for v, t in zip(shapes, (BF16, BF16, jnp.int32))
+        ),
+        24,
+        scalars=1,
+        in_specs=[whole(v.shape) for v in inputs],
+        out_specs=tuple(whole(v) for v in shapes),
+    )(place[None], *inputs)
 
 
 def turn(values, axis, place, size):
@@ -329,33 +410,8 @@
         first_near, first_far = ring_gather(first, "fsdp", ring, True)
         second_near, second_far = ring_gather(second, "fsdp", ring, False)
 
-        slot_rank = jnp.cumsum(route_mask) - 1
-        slot_ids = jnp.arange(CAP, dtype=jnp.int32)
-        table = ((slot_rank[None, :] == slot_ids[:, None]) & (route_mask[None, :] == 1)).astype(BF16)
-        table_wide = table.astype(F32)
-        blocks = x_scale.shape[1]
-        slot_quant = jnp.dot(table, x_quant, preferred_element_type=F32)
-        slot_scale = jnp.dot(
-            table_wide, x_scale, precision=lax.Precision.HIGHEST, preferred_element_type=F32
-        )
-        slot_x = (
-            (slot_quant.reshape(CAP, blocks, width // blocks) * slot_scale[:, :, None])
-            .reshape(CAP, width)
-            .astype(BF16)
-        )
-        slot_dy = jnp.dot(table, grad_out, preferred_element_type=F32).astype(BF16)
-        slot_prob = jnp.sum(table_wide * route_prob.astype(F32)[None, :], axis=1)
-        weighted = (slot_prob[:, None] * slot_dy.astype(F32)).astype(BF16)
-
-        sides = jnp.concatenate(
-            [slot_x.reshape(CAP, ring, part), weighted.reshape(CAP, ring, part)], axis=-1
-        ).transpose(1, 0, 2)
-        turned = turn(
-            jnp.stack([slot_x, slot_dy]).reshape(2, CAP, ring, part), 2, place, ring
-        ).reshape(2, CAP, width)
-        packed = jnp.concatenate(
-            [turned[0], turned[1], jnp.broadcast_to(slot_prob.astype(BF16)[:, None], (CAP, 128))],
-            axis=1,
+        packed, sides, token_slot = pick_slots(
+            place, route_mask, route_prob, x_quant, x_scale, grad_out, ring
         )
         rows = lax.all_gather(packed, CORE_FIRST, axis=0, tiled=True)
 
@@ -375,14 +431,17 @@
         got = lax.ppermute(give, "core", [(0, 1), (1, 0)])
         both = pair_sum(keep, got).reshape(-1, CAP, width + LANES)
         shares = lax.all_to_all(both, PLANE, split_axis=0, concat_axis=0, tiled=True)
+        table = token_slot == jnp.arange(CAP, dtype=jnp.int32)[:, None]
         mine = jnp.sum(shares.astype(F32), axis=0)
         mine_grad = mine[:, :width].astype(BF16).reshape(CAP, ring, part)
         mine_grad = turn(mine_grad, 1, place, ring).reshape(CAP, width)
         mine_prob = mine[:, width] + mine[:, width + 1]
-        grad_x = contract(table, mine_grad, 0, 0).astype(BF16)
-        grad_prob = jnp.sum(table_wide * mine_prob[:, None], axis=0)
-
-        grad_gate, grad_up, grad_down = weight_sums(columns, all_acts)
+        grad_x = contract(table.astype(BF16), mine_grad, 0, 0).astype(BF16)
+        grad_prob = jnp.sum(jnp.where(table, mine_prob[:, None], 0.0), axis=0)
+
+        grad_gate, grad_up, grad_down = weight_sums(
+            turned_features(columns, part), columns, all_acts
+        )
         return (grad_x, grad_prob, grad_gate, grad_up, grad_down)
 
     return on_device

time: 187 us -> 188 us (level)
  blocking collectives: 55.3 us -> 27 us
  waiting for transfers between devices: 50.5 us -> 65.4 us
  local copies, waits for them, and re-layouts: 6.12 us -> 13.8 us
  starting transfers between devices: 25.6 us -> 32.4 us
  Pallas kernels: 26.9 us -> 31.7 us
  other arithmetic: 4.68 us -> 1.1 us
    all_to_all x1 -> x0, blocking collectives: 29.2 us -> none  [on_device(): lax.all_to_all(both, PLANE, split_axis=0, concat_axis=0, tiled=True)]
    all_to_all x0 -> x1, waiting for transfers between devices: none -> 16.1 us  [on_device(): lax.all_to_all(both, PLANE, split_axis=0, concat_axis=0, tiled=True)]
    unnamed x47 -> x54, local copies, waits for them, and re-layouts: 5.03 us -> 13.6 us
    all_to_all x0 -> x1, starting transfers between devices: none -> 6.95 us  [on_device(): lax.all_to_all(both, PLANE, split_axis=0, concat_axis=0, tiled=True)]
    pallas_call x0 -> x2, Pallas kernels: none -> 3.4 us  [the longest x1 2.02 us: turned_features(): kernel_call(body, jax.ShapeDtypeStruct((part, slots), BF16), 16, grid=(sl...]
  transfers between devices with their start and end apart: 18 -> 19, of which waited for: 7 -> 8; matrix products, arithmetic and copies ran while one was open for 2% -> 2% of each run, Pallas kernels for 11% -> 12%
where the time goes in v3:
time: 188 us; the launch traced here: 187 us
  waiting for transfers between devices  65.4 us (35%)
  starting transfers between devices  32.4 us (17%)
  Pallas kernels  31.7 us (17%)
  blocking collectives  27 us (14%)
  between operations  14 us (7%)
  local copies, waits for them, and re-layouts  13.8 us (7%)
    all_to_all x1, blocking collectives, on_device(): lax.all_to_all(sides, 'fsdp', split_axis=0, concat_axis=0, tiled=True)  27 us
    ppermute x6, waiting for transfers between devices, ring_gather(): ahead = lax.ppermute(ahead, axis, up)  20.7 us
    ppermute x6, waiting for transfers between devices, ring_gather(): behind = lax.ppermute(behind, axis, down)  18.4 us
    all_to_all x1, waiting for transfers between devices, on_device(): lax.all_to_all(both, PLANE, split_axis=0, concat_axis=0, tiled=True)  16.1 us
    unnamed x54, local copies, waits for them, and re-layouts  13.6 us
    ppermute x6, starting transfers between devices, ring_gather(): behind = lax.ppermute(behind, axis, down)  12.9 us
    pallas_call x1, Pallas kernels, slot_sums(): kernel_call(body, (jax.ShapeDtypeStruct(shape, BF16),) * 2, 60, scalars=1...  7.83 us
    pallas_call x1, Pallas kernels, weight_sums(): kernel_call(body, (jax.ShapeDtypeStruct((part, units), F32), jax.ShapeDty...  7.49 us
  transfers between devices with their start and end apart: 19, of which 8 were waited for; matrix products, arithmetic and copies ran while one was open for 2% of the time, Pallas kernels for 12%

profile of v3, /device:TPU:1, one launch (start us, length us, event | category | flops | bytes accessed | tf_op | source)
XLA Modules:
  0.0 187.2 jit_solution(5935941301138354058)
XLA Ops:
  8.1 1.4 copy-done.5
  9.5 1.4 copy-done.6
  12.2 1.4 shard_map.146
  13.9 1.0 shard_map.147
  14.9 2.5 %collective-permute-start = (bf16[384,768]{1,0:T(8,128)(2,1)S(1)}, bf16[384,768]{1,0:T(8,128)(2,1)S(1)}, u32[]{:S(2)}, u32[]{:S(2)}) collective-permute-start(bf16[384,768]{1,0:T(8,128)(2,1)S(1)} %get-tuple-element.20.refs_0_), channel_id=1, source_target_pairs={{0,32},{32,64},{64,96},{96,128},{128,160},{160,192},{192,224},{224... | collective-permute-start | bytes 1769480 | tf_op jit(solution)/shard_map/ppermute | solution.py:379
  17.5 4.0 %collective-permute-start.1 = (bf16[384,768]{1,0:T(8,128)(2,1)S(1)}, bf16[384,768]{1,0:T(8,128)(2,1)S(1)}, u32[]{:S(2)}, u32[]{:S(2)}) collective-permute-start(bf16[384,768]{1,0:T(8,128)(2,1)S(1)} %get-tuple-element.20.refs_0_), channel_id=1, source_target_pairs={{0,224},{32,0},{64,32},{96,64},{128,96},{160,128},{192,160},{224,1... | collective-permute-start | bytes 1769480 | tf_op jit(solution)/shard_map/ppermute | solution.py:380
  21.5 2.7 %collective-permute-start.7 = (bf16[384,768]{1,0:T(8,128)(2,1)S(1)}, bf16[384,768]{1,0:T(8,128)(2,1)}, u32[]{:S(2)}, u32[]{:S(2)}) collective-permute-start(bf16[384,768]{1,0:T(8,128)(2,1)S(1)} %get-tuple-element.21.refs_7_.refs_8_), channel_id=1, source_target_pairs={{0,224},{32,0},{64,32},{96,64},{128,96},{160,128},{192,160},{224,1... | collective-permute-start | bytes 1769480 | tf_op jit(solution)/shard_map/ppermute | solution.py:380
  24.2 27.0 %all_to_all.10 = bf16[8,8,1536]{2,1,0:T(8,128)(2,1)} all-to-all(bf16[8,8,1536]{2,1,0:T(8,128)(2,1)S(1)} %get-tuple-element.26), channel_id=1, replica_groups=mesh['fsdp'=8,'x'=4,'y'=4,'core'=2] {'fsdp'}, dimensions={0} | all-to-all | bytes 393216 | tf_op jit(solution)/shard_map/all_to_all | solution.py:418
  51.3 2.3 %collective-permute-start.2 = (bf16[384,768]{1,0:T(8,128)(2,1)S(1)}, bf16[384,768]{1,0:T(8,128)(2,1)S(1)}, u32[]{:S(2)}, u32[]{:S(2)}) collective-permute-start(bf16[384,768]{1,0:T(8,128)(2,1)S(1)} %collective-permute-done.refs_1_), channel_id=1, source_target_pairs={{0,32},{32,64},{64,96},{96,128},{128,160},{160,192},{192,224},{224... | collective-permute-start | bytes 1769480 | tf_op jit(solution)/shard_map/ppermute | solution.py:379
  55.5 9.9 %collective-permute-done.2.refs_3_ = bf16[384,768]{1,0:T(8,128)(2,1)S(1)} collective-permute-done((bf16[384,768]{1,0:T(8,128)(2,1)S(1)}, bf16[384,768]{1,0:T(8,128)(2,1)S(1)}, u32[]{:S(2)}, u32[]{:S(2)}) %collective-permute-start.2) | collective-permute-done | bytes 589856 | tf_op jit(solution)/shard_map/ppermute | solution.py:379
  65.3 2.7 %collective-permute-start.11 = (bf16[384,768]{1,0:T(8,128)(2,1)S(1)}, bf16[384,768]{1,0:T(8,128)(2,1)}, u32[]{:S(2)}, u32[]{:S(2)}) collective-permute-start(bf16[384,768]{1,0:T(8,128)(2,1)S(1)} %collective-permute-done.9.refs_11_.refs_12_), channel_id=1, source_target_pairs={{0,224},{32,0},{64,32},{96,64},{128,96},{160,128},{192,160},{224,1... | collective-permute-start | bytes 1769480 | tf_op jit(solution)/shard_map/ppermute | solution.py:380
  68.0 9.3 %collective-permute-done.3.refs_4_ = bf16[384,768]{1,0:T(8,128)(2,1)S(1)} collective-permute-done((bf16[384,768]{1,0:T(8,128)(2,1)S(1)}, bf16[384,768]{1,0:T(8,128)(2,1)S(1)}, u32[]{:S(2)}, u32[]{:S(2)}) %collective-permute-start.3) | collective-permute-done | bytes 589856 | tf_op jit(solution)/shard_map/ppermute | solution.py:380
  77.3 2.5 %collective-permute-start.5 = (bf16[384,768]{1,0:T(8,128)(2,1)S(1)}, bf16[384,768]{1,0:T(8,128)(2,1)S(1)}, u32[]{:S(2)}, u32[]{:S(2)}) collective-permute-start(bf16[384,768]{1,0:T(8,128)(2,1)S(1)} %collective-permute-done.3.refs_4_), channel_id=1, source_target_pairs={{0,224},{32,0},{64,32},{96,64},{128,96},{160,128},{192,160},{224,1... | collective-permute-start | bytes 1769480 | tf_op jit(solution)/shard_map/ppermute | solution.py:380
  79.8 10.8 %collective-permute-done.4.refs_5_ = bf16[384,768]{1,0:T(8,128)(2,1)} collective-permute-done((bf16[384,768]{1,0:T(8,128)(2,1)S(1)}, bf16[384,768]{1,0:T(8,128)(2,1)}, u32[]{:S(2)}, u32[]{:S(2)}) %collective-permute-start.4) | collective-permute-done | bytes 589856 | tf_op jit(solution)/shard_map/ppermute | solution.py:379
  90.6 2.9 %collective-permute-start.13 = (bf16[384,768]{1,0:T(8,128)(2,1)}, bf16[384,768]{1,0:T(8,128)(2,1)S(1)}, u32[]{:S(2)}, u32[]{:S(2)}) collective-permute-start(bf16[384,768]{1,0:T(8,128)(2,1)} %collective-permute-done.11.refs_13_.refs_14_), channel_id=1, source_target_pairs={{0,224},{32,0},{64,32},{96,64},{128,96},{160,128},{192,160},{224,1... | collective-permute-start | bytes 1769480 | tf_op jit(solution)/shard_map/ppermute | solution.py:382
  93.6 9.1 %collective-permute-done.5.refs_6_ = bf16[384,768]{1,0:T(8,128)(2,1)S(1)} collective-permute-done((bf16[384,768]{1,0:T(8,128)(2,1)S(1)}, bf16[384,768]{1,0:T(8,128)(2,1)S(1)}, u32[]{:S(2)}, u32[]{:S(2)}) %collective-permute-start.5) | collective-permute-done | bytes 589856 | tf_op jit(solution)/shard_map/ppermute | solution.py:380
  103.5 6.8 %shard_map.148.sums_ref = f32[256,768]{1,0:T(8,128)} custom-call(bf16[256,12416]{1,0:T(8,128)(2,1)} %all-gather.4.cloned.1.call-done.rows_ref.x_ref.dy_ref.prob_ref, bf16[384,768]{1,0:T(8,128)(2,1)} %copy-done.2, bf16[384,768]{1,0:T(8,128)(2,1)} %copy-done.15, bf16[384,768]{1,0:T(8,128)(2,1)} %copy-done.16, bf16[384,768]{1,0:T(8,128)(2,1)} %copy-done.18, ...), custom_call_target="tpu_custom_call" | custom-call | tf_op jit(solution)/shard_map/pallas_call | solution.py:125
  110.3 5.5 %collective-permute-done.12.first_ref.refs_7_ = bf16[384,768]{1,0:T(8,128)(2,1)S(1)} collective-permute-done((bf16[384,768]{1,0:T(8,128)(2,1)}, bf16[384,768]{1,0:T(8,128)(2,1)S(1)}, u32[]{:S(2)}, u32[]{:S(2)}) %collective-permute-start.12) | collective-permute-done | bytes 589856 | tf_op jit(solution)/shard_map/ppermute | solution.py:382
  117.5 3.4 %shard_map.149 = (bf16[256,768]{1,0:T(8,128)(2,1)}, bf16[256,128]{1,0:T(8,128)(2,1)}) custom-call(bf16[256,12416]{1,0:T(8,128)(2,1)} %all-gather.4.cloned.1.call-done.rows_ref.x_ref.dy_ref.prob_ref, bf16[256,12416]{1,0:T(8,128)(2,1)} %all-gather.4.cloned.1.call-done.rows_ref.x_ref.dy_ref.prob_ref, ...), custom_call_target="tpu_custom_call" | custom-call | tf_op jit(solution)/shard_map/pallas_call | solution.py:167
  120.9 7.8 %shard_map.150 = (bf16[128,6272]{1,0:T(8,128)(2,1)}, bf16[128,6272]{1,0:T(8,128)(2,1)}) custom-call(s32[1]{0:T(128)} %bitcast.4.core_ref, bf16[256,768]{1,0:T(8,128)(2,1)} %get-tuple-element.22.acts_ref, bf16[256,128]{1,0:T(8,128)(2,1)} %get-tuple-element.23.prob_ref, bf16[384,768]{1,0:T(8,128)(2,1)} %copy-done.2, bf16[384,768]{1,0:T(8,128)(2,1)} %copy-done.15, ...), custom_call_target="tpu_custom_call" | custom-call | tf_op jit(solution)/shard_map/pallas_call | solution.py:218
  128.7 3.8 %collective-permute-start.14 = (bf16[128,6272]{1,0:T(8,128)(2,1)}, bf16[128,6272]{1,0:T(8,128)(2,1)S(1)}, u32[]{:S(2)}, u32[]{:S(2)}) collective-permute-start(bf16[128,6272]{1,0:T(8,128)(2,1)} %get-tuple-element.25), channel_id=1, source_target_pairs={{0,1},{1,0},{2,3},{3,2},{4,5},{5,4},{6,7},{7,6},{8,9},{9,8},{10,11... | collective-permute-start | bytes 4816904 | tf_op jit(solution)/shard_map/ppermute | solution.py:431
  132.5 3.3 %collective-permute-done.14.b_ref = bf16[128,6272]{1,0:T(8,128)(2,1)S(1)} collective-permute-done((bf16[128,6272]{1,0:T(8,128)(2,1)}, bf16[128,6272]{1,0:T(8,128)(2,1)S(1)}, u32[]{:S(2)}, u32[]{:S(2)}) %collective-permute-start.14) | collective-permute-done | bytes 1605664 | tf_op jit(solution)/shard_map/ppermute | solution.py:431
  135.8 1.4 copy-done.4
  137.2 1.8 shard_map.151
  139.1 6.9 %all-to-all-start = ((bf16[16,8,6272]{2,1,0:T(8,128)(2,1)}), bf16[16,8,6272]{2,1,0:T(8,128)(2,1)S(1)}, u32[]{:S(2)}, u32[]{:S(2)}) async-start(bf16[16,8,6272]{2,1,0:T(8,128)(2,1)} %bitcast.5), calls=%async_computation | async-start | bytes 3211264 | tf_op jit(solution)/shard_map/all_to_all | solution.py:433
  146.1 2.8 %copy-done = bf16[8,256,1536]{2,1,0:T(8,128)(2,1)S(1)} copy-done((bf16[8,256,1536]{2,1,0:T(8,128)(2,1)S(1)}, bf16[8,256,1536]{2,1,0:T(8,128)(2,1)}, u32[]{:S(2)}) %copy-start) | copy-done | bytes 6291480
  148.9 2.0 %shard_map.152.x_ref = bf16[768,2048]{1,0:T(8,128)(2,1)S(1)} custom-call(bf16[2048,1536]{1,0:T(8,128)(2,1)S(1)} %bitcast.13), custom_call_target="tpu_custom_call" | custom-call | tf_op jit(solution)/shard_map/pallas_call | solution.py:258
  150.9 1.7 copy-done.1
  152.6 16.1 %all-to-all-done = bf16[16,8,6272]{2,1,0:T(8,128)(2,1)S(1)} async-done(((bf16[16,8,6272]{2,1,0:T(8,128)(2,1)}), bf16[16,8,6272]{2,1,0:T(8,128)(2,1)S(1)}, u32[]{:S(2)}, u32[]{:S(2)}) %all-to-all-start) | async-done | bytes 1605664 | tf_op jit(solution)/shard_map/all_to_all | solution.py:433
  170.1 1.8 convolution_convert_fusion
  171.9 1.3 all-gather.8.cloned.1.call-done.acts_ref
  173.2 7.5 %shard_map.153 = (f32[768,256]{1,0:T(8,128)}, f32[768,256]{1,0:T(8,128)}, f32[256,768]{1,0:T(8,128)}) custom-call(bf16[768,2048]{1,0:T(8,128)(2,1)} %copy-done.1, bf16[2048,1536]{1,0:T(8,128)(2,1)} %bitcast.12, bf16[2048,768]{1,0:T(8,128)(2,1)} %all-gather.8.cloned.1.call-done.acts_ref), custom_call_target="tpu_custom_call" | custom-call | tf_op jit(solution)/shard_map/pallas_call | solution.py:287
  (80 shorter events, 8.4 us)
Async XLA Ops:
  7.2 96.3 %all-gather.4.cloned.1.call-start = ((), (), s32[]{:S(2)}) async-start(), calls=%async_computation.2 | async-start | bytes 6555648 | tf_op jit(solution)/shard_map/all_gather | solution.py:416
  12.2 1.7 copy-start.7
  12.2 1.7 copy-start.8
  12.2 1.7 copy-start.9
  13.6 132.4 %all-gather.6.cloned.1.call-start = ((), (), s32[]{:S(2)}) async-start(), calls=%async_computation.3 | async-start | bytes 6488064 | tf_op jit(solution)/shard_map/all_gather | solution.py:422
  14.9 88.6 %copy-start.2 = (bf16[384,768]{1,0:T(8,128)(2,1)}, bf16[384,768]{1,0:T(8,128)(2,1)S(1)}, u32[]{:S(2)}) copy-start(bf16[384,768]{1,0:T(8,128)(2,1)S(1)} %get-tuple-element.20.refs_0_) | copy-start | bytes 1769476
  14.9 88.6 %copy-start.3 = (bf16[384,768]{1,0:T(8,128)(2,1)}, bf16[384,768]{1,0:T(8,128)(2,1)S(1)}, u32[]{:S(2)}) copy-start(bf16[384,768]{1,0:T(8,128)(2,1)S(1)} %get-tuple-element.21.refs_7_.refs_8_) | copy-start | bytes 1769476
  14.9 36.2 %collective-permute-start = (bf16[384,768]{1,0:T(8,128)(2,1)S(1)}, bf16[384,768]{1,0:T(8,128)(2,1)S(1)}, u32[]{:S(2)}, u32[]{:S(2)}) collective-permute-start(bf16[384,768]{1,0:T(8,128)(2,1)S(1)} %get-tuple-element.20.refs_0_), channel_id=1, source_target_pairs={{0,32},{32,64},{64,96},{96,128},{128,160},{160,192},{192,224},{224... | collective-permute-start | bytes 1769480 | tf_op jit(solution)/shard_map/ppermute | solution.py:379
  17.5 33.7 %collective-permute-start.1 = (bf16[384,768]{1,0:T(8,128)(2,1)S(1)}, bf16[384,768]{1,0:T(8,128)(2,1)S(1)}, u32[]{:S(2)}, u32[]{:S(2)}) collective-permute-start(bf16[384,768]{1,0:T(8,128)(2,1)S(1)} %get-tuple-element.20.refs_0_), channel_id=1, source_target_pairs={{0,224},{32,0},{64,32},{96,64},{128,96},{160,128},{192,160},{224,1... | collective-permute-start | bytes 1769480 | tf_op jit(solution)/shard_map/ppermute | solution.py:380
  21.5 29.7 %collective-permute-start.6 = (bf16[384,768]{1,0:T(8,128)(2,1)S(1)}, bf16[384,768]{1,0:T(8,128)(2,1)S(1)}, u32[]{:S(2)}, u32[]{:S(2)}) collective-permute-start(bf16[384,768]{1,0:T(8,128)(2,1)S(1)} %get-tuple-element.21.refs_7_.refs_8_), channel_id=1, source_target_pairs={{0,32},{32,64},{64,96},{96,128},{128,160},{160,192},{192,224},{224... | collective-permute-start | bytes 1769480 | tf_op jit(solution)/shard_map/ppermute | solution.py:379
  21.5 29.7 %collective-permute-start.7 = (bf16[384,768]{1,0:T(8,128)(2,1)S(1)}, bf16[384,768]{1,0:T(8,128)(2,1)}, u32[]{:S(2)}, u32[]{:S(2)}) collective-permute-start(bf16[384,768]{1,0:T(8,128)(2,1)S(1)} %get-tuple-element.21.refs_7_.refs_8_), channel_id=1, source_target_pairs={{0,224},{32,0},{64,32},{96,64},{128,96},{160,128},{192,160},{224,1... | collective-permute-start | bytes 1769480 | tf_op jit(solution)/shard_map/ppermute | solution.py:380
  51.1 52.4 %copy-start.15 = (bf16[384,768]{1,0:T(8,128)(2,1)}, bf16[384,768]{1,0:T(8,128)(2,1)S(1)}, u32[]{:S(2)}) copy-start(bf16[384,768]{1,0:T(8,128)(2,1)S(1)} %collective-permute-done.refs_1_) | copy-start | bytes 1769476
  51.1 28.6 %copy-start.16 = (bf16[384,768]{1,0:T(8,128)(2,1)}, bf16[384,768]{1,0:T(8,128)(2,1)S(1)}, u32[]{:S(2)}) copy-start(bf16[384,768]{1,0:T(8,128)(2,1)S(1)} %collective-permute-done.1.refs_2_) | copy-start | bytes 1769476
  51.2 39.5 %copy-start.17 = (bf16[384,768]{1,0:T(8,128)(2,1)}, bf16[384,768]{1,0:T(8,128)(2,1)S(1)}, u32[]{:S(2)}) copy-start(bf16[384,768]{1,0:T(8,128)(2,1)S(1)} %collective-permute-done.6.refs_8_.refs_9_) | copy-start | bytes 1769476
  51.2 122.0 %all-gather.8.cloned.1.call-start = ((), (), s32[]{:S(2)}) async-start(), calls=%async_computation.4 | async-start | bytes 3538944 | tf_op jit(solution)/shard_map/all_gather | solution.py:426
  51.3 14.1 %collective-permute-start.2 = (bf16[384,768]{1,0:T(8,128)(2,1)S(1)}, bf16[384,768]{1,0:T(8,128)(2,1)S(1)}, u32[]{:S(2)}, u32[]{:S(2)}) collective-permute-start(bf16[384,768]{1,0:T(8,128)(2,1)S(1)} %collective-permute-done.refs_1_), channel_id=1, source_target_pairs={{0,32},{32,64},{64,96},{96,128},{128,160},{160,192},{192,224},{224... | collective-permute-start | bytes 1769480 | tf_op jit(solution)/shard_map/ppermute | solution.py:379
  53.5 11.8 %collective-permute-start.9 = (bf16[384,768]{1,0:T(8,128)(2,1)}, bf16[384,768]{1,0:T(8,128)(2,1)S(1)}, u32[]{:S(2)}, u32[]{:S(2)}) collective-permute-start(bf16[384,768]{1,0:T(8,128)(2,1)} %collective-permute-done.7.refs_9_.refs_10_), channel_id=1, source_target_pairs={{0,224},{32,0},{64,32},{96,64},{128,96},{160,128},{192,160},{224,1... | collective-permute-start | bytes 1769480 | tf_op jit(solution)/shard_map/ppermute | solution.py:380
  54.0 23.3 %collective-permute-start.3 = (bf16[384,768]{1,0:T(8,128)(2,1)S(1)}, bf16[384,768]{1,0:T(8,128)(2,1)S(1)}, u32[]{:S(2)}, u32[]{:S(2)}) collective-permute-start(bf16[384,768]{1,0:T(8,128)(2,1)S(1)} %collective-permute-done.1.refs_2_), channel_id=1, source_target_pairs={{0,224},{32,0},{64,32},{96,64},{128,96},{160,128},{192,160},{224,1... | collective-permute-start | bytes 1769480 | tf_op jit(solution)/shard_map/ppermute | solution.py:380
  54.5 25.2 %collective-permute-start.8 = (bf16[384,768]{1,0:T(8,128)(2,1)S(1)}, bf16[384,768]{1,0:T(8,128)(2,1)S(1)}, u32[]{:S(2)}, u32[]{:S(2)}) collective-permute-start(bf16[384,768]{1,0:T(8,128)(2,1)S(1)} %collective-permute-done.6.refs_8_.refs_9_), channel_id=1, source_target_pairs={{0,32},{32,64},{64,96},{96,128},{128,160},{160,192},{192,224},{224... | collective-permute-start | bytes 1769480 | tf_op jit(solution)/shard_map/ppermute | solution.py:379
  65.3 25.3 %copy-start.18 = (bf16[384,768]{1,0:T(8,128)(2,1)}, bf16[384,768]{1,0:T(8,128)(2,1)S(1)}, u32[]{:S(2)}) copy-start(bf16[384,768]{1,0:T(8,128)(2,1)S(1)} %collective-permute-done.2.refs_3_) | copy-start | bytes 1769476
  65.3 25.3 %collective-permute-start.4 = (bf16[384,768]{1,0:T(8,128)(2,1)S(1)}, bf16[384,768]{1,0:T(8,128)(2,1)}, u32[]{:S(2)}, u32[]{:S(2)}) collective-permute-start(bf16[384,768]{1,0:T(8,128)(2,1)S(1)} %collective-permute-done.2.refs_3_), channel_id=1, source_target_pairs={{0,32},{32,64},{64,96},{96,128},{128,160},{160,192},{192,224},{224... | collective-permute-start | bytes 1769480 | tf_op jit(solution)/shard_map/ppermute | solution.py:379
  65.3 28.2 %copy-start.19 = (bf16[384,768]{1,0:T(8,128)(2,1)}, bf16[384,768]{1,0:T(8,128)(2,1)S(1)}, u32[]{:S(2)}) copy-start(bf16[384,768]{1,0:T(8,128)(2,1)S(1)} %collective-permute-done.9.refs_11_.refs_12_) | copy-start | bytes 1769476
  65.3 25.3 %collective-permute-start.11 = (bf16[384,768]{1,0:T(8,128)(2,1)S(1)}, bf16[384,768]{1,0:T(8,128)(2,1)}, u32[]{:S(2)}, u32[]{:S(2)}) collective-permute-start(bf16[384,768]{1,0:T(8,128)(2,1)S(1)} %collective-permute-done.9.refs_11_.refs_12_), channel_id=1, source_target_pairs={{0,224},{32,0},{64,32},{96,64},{128,96},{160,128},{192,160},{224,1... | collective-permute-start | bytes 1769480 | tf_op jit(solution)/shard_map/ppermute | solution.py:380
  77.3 25.4 %copy-start.20 = (bf16[384,768]{1,0:T(8,128)(2,1)}, bf16[384,768]{1,0:T(8,128)(2,1)S(1)}, u32[]{:S(2)}) copy-start(bf16[384,768]{1,0:T(8,128)(2,1)S(1)} %collective-permute-done.3.refs_4_) | copy-start | bytes 1769476
  77.3 25.4 %collective-permute-start.5 = (bf16[384,768]{1,0:T(8,128)(2,1)S(1)}, bf16[384,768]{1,0:T(8,128)(2,1)S(1)}, u32[]{:S(2)}, u32[]{:S(2)}) collective-permute-start(bf16[384,768]{1,0:T(8,128)(2,1)S(1)} %collective-permute-done.3.refs_4_), channel_id=1, source_target_pairs={{0,224},{32,0},{64,32},{96,64},{128,96},{160,128},{192,160},{224,1... | collective-permute-start | bytes 1769480 | tf_op jit(solution)/shard_map/ppermute | solution.py:380
  79.8 22.9 %copy-start.21 = (bf16[384,768]{1,0:T(8,128)(2,1)}, bf16[384,768]{1,0:T(8,128)(2,1)S(1)}, u32[]{:S(2)}) copy-start(bf16[384,768]{1,0:T(8,128)(2,1)S(1)} %collective-permute-done.8.refs_10_.refs_11_) | copy-start | bytes 1769476
  79.8 23.7 %collective-permute-start.10 = (bf16[384,768]{1,0:T(8,128)(2,1)S(1)}, bf16[384,768]{1,0:T(8,128)(2,1)}, u32[]{:S(2)}, u32[]{:S(2)}) collective-permute-start(bf16[384,768]{1,0:T(8,128)(2,1)S(1)} %collective-permute-done.8.refs_10_.refs_11_), channel_id=1, source_target_pairs={{0,32},{32,64},{64,96},{96,128},{128,160},{160,192},{192,224},{224... | collective-permute-start | bytes 1769480 | tf_op jit(solution)/shard_map/ppermute | solution.py:379
  90.6 25.3 %collective-permute-start.12 = (bf16[384,768]{1,0:T(8,128)(2,1)}, bf16[384,768]{1,0:T(8,128)(2,1)S(1)}, u32[]{:S(2)}, u32[]{:S(2)}) collective-permute-start(bf16[384,768]{1,0:T(8,128)(2,1)} %collective-permute-done.4.refs_5_), channel_id=1, source_target_pairs={{0,32},{32,64},{64,96},{96,128},{128,160},{160,192},{192,224},{224... | collective-permute-start | bytes 1769480 | tf_op jit(solution)/shard_map/ppermute | solution.py:382
  90.6 25.3 %collective-permute-start.13 = (bf16[384,768]{1,0:T(8,128)(2,1)}, bf16[384,768]{1,0:T(8,128)(2,1)S(1)}, u32[]{:S(2)}, u32[]{:S(2)}) collective-permute-start(bf16[384,768]{1,0:T(8,128)(2,1)} %collective-permute-done.11.refs_13_.refs_14_), channel_id=1, source_target_pairs={{0,224},{32,0},{64,32},{96,64},{128,96},{160,128},{192,160},{224,1... | collective-permute-start | bytes 1769480 | tf_op jit(solution)/shard_map/ppermute | solution.py:382
  128.7 7.1 %collective-permute-start.14 = (bf16[128,6272]{1,0:T(8,128)(2,1)}, bf16[128,6272]{1,0:T(8,128)(2,1)S(1)}, u32[]{:S(2)}, u32[]{:S(2)}) collective-permute-start(bf16[128,6272]{1,0:T(8,128)(2,1)} %get-tuple-element.25), channel_id=1, source_target_pairs={{0,1},{1,0},{2,3},{3,2},{4,5},{5,4},{6,7},{7,6},{8,9},{9,8},{10,11... | collective-permute-start | bytes 4816904 | tf_op jit(solution)/shard_map/ppermute | solution.py:431
  139.1 29.6 %all-to-all-start = ((bf16[16,8,6272]{2,1,0:T(8,128)(2,1)}), bf16[16,8,6272]{2,1,0:T(8,128)(2,1)S(1)}, u32[]{:S(2)}, u32[]{:S(2)}) async-start(bf16[16,8,6272]{2,1,0:T(8,128)(2,1)} %bitcast.5), calls=%async_computation | async-start | bytes 3211264 | tf_op jit(solution)/shard_map/all_to_all | solution.py:433
  146.1 2.8 %copy-start = (bf16[8,256,1536]{2,1,0:T(8,128)(2,1)S(1)}, bf16[8,256,1536]{2,1,0:T(8,128)(2,1)}, u32[]{:S(2)}) copy-start(bf16[8,256,1536]{2,1,0:T(8,128)(2,1)} %all-gather.6.cloned.1.call-done) | copy-start | bytes 18874372
  (12 other events, 14.4 us)
Sparse Core Ops, SparseCore 0:
  13.7 58.4 all-gather.3
  74.8 53.1 all-gather.5
  129.8 43.3 all-gather.7

commit v4 on v3

--- a/solution.py
+++ b/solution.py
@@ -62,20 +62,20 @@
             for j in range(units // BLOCK):
                 cols = slice(j * BLOCK, (j + 1) * BLOCK)
                 tiles = (
-                    gate[rows, cols].astype(F32) * gate_s[i, j],
-                    up[rows, cols].astype(F32) * up_s[i, j],
+                    gate[rows, cols].astype(F32) * gate_s[j, i],
+                    up[rows, cols].astype(F32) * up_s[j, i],
                     (down[cols, rows].astype(F32) * down_s[j, i]).T,
                 )
                 for k, tile in enumerate(tiles):
                     to = k * units + j * BLOCK
                     out[at : at + BLOCK, to : to + BLOCK] = tile.astype(BF16)
 
-    quants, scales = [gate_quant, up_quant, down_quant], [gate_scale, up_scale, down_scale]
+    quants, scales = [gate_quant, up_quant, down_quant], [gate_scale.T, up_scale.T, down_scale]
     shape = (half, 3 * units)
     return kernel_call(
         body,
         (jax.ShapeDtypeStruct(shape, BF16),) * 2,
-        16,
+        60,
         in_specs=[whole(v.shape) for v in quants] + [pl.BlockSpec(memory_space=pltpu.SMEM)] * 3,
         out_specs=(whole(shape),) * 2,
     )(*quants, *scales)
@@ -248,63 +248,51 @@
     )(mine, other)
 
 
-def turned_features(columns, part):
+def split_columns(columns, part):
     slots = columns.shape[0]
     tile = 256
 
-    def body(x_ref, out):
-        out[...] = x_ref[...].astype(F32).T.astype(BF16)
-
-    return kernel_call(
-        body,
-        jax.ShapeDtypeStruct((part, slots), BF16),
+    def body(x_ref, weighted_ref, features, weighted):
+        features[...] = x_ref[...].astype(F32).T.astype(BF16)
+        weighted[...] = weighted_ref[...]
+
+    return kernel_call(
+        body,
+        (
+            jax.ShapeDtypeStruct((part, slots), BF16),
+            jax.ShapeDtypeStruct((slots, part), BF16),
+        ),
         16,
         grid=(slots // tile,),
-        in_specs=[pl.BlockSpec((tile, part), lambda i: (i, 0))],
-        out_specs=pl.BlockSpec((part, tile), lambda i: (0, i)),
-    )(columns)
-
-
-def weight_sums(features, columns, acts):
+        in_specs=[
+            pl.BlockSpec((tile, part), lambda i: (i, 0)),
+            pl.BlockSpec((tile, part), lambda i: (i, 1)),
+        ],
+        out_specs=(
+            pl.BlockSpec((part, tile), lambda i: (0, i)),
+            pl.BlockSpec((tile, part), lambda i: (i, 0)),
+        ),
+    )(columns, columns)
+
+
+def weight_sums(features, weighted, acts):
     part, slots = features.shape
     units = acts.shape[1] // 3
-    tile = 256
-    steps = part // tile
-
-    def body(x_ref, weighted_ref, acts_ref, gate_out, up_out, down_out, hidden):
-        @pl.when(pl.program_id(0) == 0)
-        def _():
-            for at in range(0, slots, tile):
-                hidden[:, at : at + tile] = (
-                    acts_ref[at : at + tile, 2 * units :].astype(F32).T.astype(BF16)
-                )
-
-        both = contract(x_ref[...], acts_ref[:, : 2 * units], 1, 0)
-        gate_out[...] = both[:, :units]
-        up_out[...] = both[:, units:]
-        down_out[...] = contract(hidden[...], weighted_ref[...], 1, 0)
-
-    return kernel_call(
-        body,
-        (
-            jax.ShapeDtypeStruct((part, units), F32),
-            jax.ShapeDtypeStruct((part, units), F32),
-            jax.ShapeDtypeStruct((units, part), F32),
-        ),
-        60,
-        grid=(steps,),
-        in_specs=[
-            pl.BlockSpec((tile, slots), lambda i: (i, 0)),
-            pl.BlockSpec((slots, tile), lambda i: (0, steps + i)),
-            whole(acts.shape),
-        ],
-        out_specs=(
-            pl.BlockSpec((tile, units), lambda i: (i, 0)),
-            pl.BlockSpec((tile, units), lambda i: (i, 0)),
-            pl.BlockSpec((units, tile), lambda i: (0, i)),
-        ),
-        scratch_shapes=[pltpu.VMEM((units, slots), BF16)],
-    )(features, columns, acts)
+
+    def body(x_ref, weighted_ref, acts_ref, gate_out, up_out, down_out):
+        gate_up = contract(x_ref[...], acts_ref[:, : 2 * units], 1, 0)
+        gate_out[...] = gate_up[:, :units]
+        up_out[...] = gate_up[:, units:]
+        down_out[...] = contract(acts_ref[:, 2 * units :], weighted_ref[...], 0, 0)
+
+    shapes = ((part, units), (part, units), (units, part))
+    return kernel_call(
+        body,
+        tuple(jax.ShapeDtypeStruct(v, F32) for v in shapes),
+        55,
+        in_specs=[whole(features.shape), whole(weighted.shape), whole(acts.shape)],
+        out_specs=tuple(whole(v) for v in shapes),
+    )(features, weighted, acts)
 
 
 def pick_slots(place, mask, prob, x_quant, x_scale, grad_out, ring):
@@ -325,7 +313,7 @@
         scale = lax.dot_general(
             table,
             scale_ref[...],
-            (((1,), (0,)), ((), ())),
+            (((1,), (1,)), ((), ())),
             precision=lax.Precision.HIGHEST,
             preferred_element_type=F32,
         )
@@ -350,13 +338,13 @@
         rows[:, 2 * width :] = jnp.broadcast_to(slot_prob, (CAP, LANES)).astype(BF16)
 
     shapes = ((CAP, 2 * width + LANES), (ring, CAP, 2 * part), (1, tokens))
-    inputs = [mask.reshape(1, tokens), prob.reshape(1, tokens), x_quant, x_scale, grad_out]
+    inputs = [mask.reshape(1, tokens), prob.reshape(1, tokens), x_quant, x_scale.T, grad_out]
     return kernel_call(
         body,
         tuple(
             jax.ShapeDtypeStruct(v, t) for v, t in zip(shapes, (BF16, BF16, jnp.int32))
         ),
-        24,
+        60,
         scalars=1,
         in_specs=[whole(v.shape) for v in inputs],
         out_specs=tuple(whole(v) for v in shapes),
@@ -440,7 +428,7 @@
         grad_prob = jnp.sum(jnp.where(table, mine_prob[:, None], 0.0), axis=0)
 
         grad_gate, grad_up, grad_down = weight_sums(
-            turned_features(columns, part), columns, all_acts
+            *split_columns(columns, part), all_acts
         )
         return (grad_x, grad_prob, grad_gate, grad_up, grad_down)
 

time: 188 us -> 185 us (0.984)
  Pallas kernels: 31.7 us -> 35.4 us
  local copies, waits for them, and re-layouts: 13.8 us -> 10.4 us
  waiting for transfers between devices: 65.4 us -> 62.6 us
    unnamed x54 -> x33, local copies, waits for them, and re-layouts: 13.6 us -> 10.2 us
    all_to_all x1, waiting for transfers between devices: 16.1 us -> 14 us  [on_device(): lax.all_to_all(both, PLANE, split_axis=0, concat_axis=0, tiled=True)]
    pallas_call x1, Pallas kernels: 1.38 us -> 3.37 us  [pick_slots(): kernel_call(body, tuple((jax.ShapeDtypeStruct(v, t) for v, t in zip(shape...]
  transfers between devices with their start and end apart: 19 -> 19, of which waited for: 8 -> 8; matrix products, arithmetic and copies ran while one was open for 2% -> 2% of each run, Pallas kernels for 12% -> 13%
where the time goes in v4:
time: 185 us; the launch traced here: 184 us
  waiting for transfers between devices  62.6 us (34%)
  Pallas kernels  35.4 us (19%)
  starting transfers between devices  31.9 us (17%)
  blocking collectives  27.3 us (15%)
  between operations  14 us (8%)
  local copies, waits for them, and re-layouts  10.4 us (6%)
    all_to_all x1, blocking collectives, on_device(): lax.all_to_all(sides, 'fsdp', split_axis=0, concat_axis=0, tiled=True)  27.3 us
    ppermute x6, waiting for transfers between devices, ring_gather(): ahead = lax.ppermute(ahead, axis, up)  20.9 us
    ppermute x6, waiting for transfers between devices, ring_gather(): behind = lax.ppermute(behind, axis, down)  18.1 us
    all_to_all x1, waiting for transfers between devices, on_device(): lax.all_to_all(both, PLANE, split_axis=0, concat_axis=0, tiled=True)  14 us
    ppermute x6, starting transfers between devices, ring_gather(): behind = lax.ppermute(behind, axis, down)  12.5 us
    unnamed x33, local copies, waits for them, and re-layouts  10.2 us
    pallas_call x1, Pallas kernels, slot_sums(): kernel_call(body, (jax.ShapeDtypeStruct(shape, BF16),) * 2, 60, scalars=1...  7.88 us
    pallas_call x1, Pallas kernels, weight_sums(): kernel_call(body, tuple((jax.ShapeDtypeStruct(v, F32) for v in shapes)),...  7.24 us
  transfers between devices with their start and end apart: 19, of which 8 were waited for; matrix products, arithmetic and copies ran while one was open for 2% of the time, Pallas kernels for 13%

profile of v4, /device:TPU:1, one launch (start us, length us, event | category | flops | bytes accessed | tf_op | source)
XLA Modules:
  0.0 184.4 jit_solution(10106707025358733874)
XLA Ops:
  7.2 3.4 %shard_map.146 = (bf16[8,12416]{1,0:T(8,128)(2,1)}, bf16[8,8,1536]{2,1,0:T(8,128)(2,1)}, s32[1,128]{1,0:T(1,128)}) custom-call(s32[1]{0:T(128)} %bitcast.place_ref, s32[1,128]{1,0:T(1,128)} %bitcast.22, bf16[1,128]{1,0:T(2,128)(2,1)} %bitcast.23, bf16[128,6144]{1,0:T(8,128)(2,1)} %x_ref.1, f32[48,128]{1,0:T(8,128)} %bitcast.19, bf16[128,6144]{1,0:T(8,128)(2,1)} %dy_ref.1), custom_call_target="tpu_custom_call" | custom-call | tf_op jit(solution)/shard_map/pallas_call | solution.py:342
  10.7 2.5 %shard_map.147 = (bf16[384,768]{1,0:T(8,128)(2,1)}, bf16[384,768]{1,0:T(8,128)(2,1)}) custom-call(bf16[768,256]{1,0:T(8,128)(2,1)} %gate.1, bf16[768,256]{1,0:T(8,128)(2,1)} %up.1, bf16[256,768]{1,0:T(8,128)(2,1)} %down.1, f32[2,6]{1,0:T(2,128)} %bitcast.20, f32[2,6]{1,0:T(2,128)} %bitcast.21, f32[2,6]{1,0:T(2,128)} %down_s.1), custom_call_target="tpu_custom_call" | custom-call | tf_op jit(solution)/shard_map/pallas_call | solution.py:75
  13.2 2.5 %collective-permute-start = (bf16[384,768]{1,0:T(8,128)(2,1)}, bf16[384,768]{1,0:T(8,128)(2,1)S(1)}, u32[]{:S(2)}, u32[]{:S(2)}) collective-permute-start(bf16[384,768]{1,0:T(8,128)(2,1)} %get-tuple-element.22.refs_0_), channel_id=1, source_target_pairs={{0,32},{32,64},{64,96},{96,128},{128,160},{160,192},{192,224},{224... | collective-permute-start | bytes 1769480 | tf_op jit(solution)/shard_map/ppermute | solution.py:367
  15.6 3.9 %collective-permute-start.1 = (bf16[384,768]{1,0:T(8,128)(2,1)}, bf16[384,768]{1,0:T(8,128)(2,1)S(1)}, u32[]{:S(2)}, u32[]{:S(2)}) collective-permute-start(bf16[384,768]{1,0:T(8,128)(2,1)} %get-tuple-element.22.refs_0_), channel_id=1, source_target_pairs={{0,224},{32,0},{64,32},{96,64},{128,96},{160,128},{192,160},{224,1... | collective-permute-start | bytes 1769480 | tf_op jit(solution)/shard_map/ppermute | solution.py:368
  19.6 2.7 %collective-permute-start.7 = (bf16[384,768]{1,0:T(8,128)(2,1)}, bf16[384,768]{1,0:T(8,128)(2,1)S(1)}, u32[]{:S(2)}, u32[]{:S(2)}) collective-permute-start(bf16[384,768]{1,0:T(8,128)(2,1)} %get-tuple-element.23.refs_7_.refs_8_), channel_id=1, source_target_pairs={{0,224},{32,0},{64,32},{96,64},{128,96},{160,128},{192,160},{224,1... | collective-permute-start | bytes 1769480 | tf_op jit(solution)/shard_map/ppermute | solution.py:368
  22.2 27.3 %all_to_all.10 = bf16[8,8,1536]{2,1,0:T(8,128)(2,1)} all-to-all(bf16[8,8,1536]{2,1,0:T(8,128)(2,1)} %get-tuple-element.28), channel_id=1, replica_groups=mesh['fsdp'=8,'x'=4,'y'=4,'core'=2] {'fsdp'}, dimensions={0} | all-to-all | bytes 393216 | tf_op jit(solution)/shard_map/all_to_all | solution.py:406
  49.6 2.3 %collective-permute-start.2 = (bf16[384,768]{1,0:T(8,128)(2,1)S(1)}, bf16[384,768]{1,0:T(8,128)(2,1)S(1)}, u32[]{:S(2)}, u32[]{:S(2)}) collective-permute-start(bf16[384,768]{1,0:T(8,128)(2,1)S(1)} %collective-permute-done.refs_1_), channel_id=1, source_target_pairs={{0,32},{32,64},{64,96},{96,128},{128,160},{160,192},{192,224},{224... | collective-permute-start | bytes 1769480 | tf_op jit(solution)/shard_map/ppermute | solution.py:367
  52.8 1.1 collective-permute-start.8
  53.9 9.8 %collective-permute-done.2.refs_3_ = bf16[384,768]{1,0:T(8,128)(2,1)S(1)} collective-permute-done((bf16[384,768]{1,0:T(8,128)(2,1)S(1)}, bf16[384,768]{1,0:T(8,128)(2,1)S(1)}, u32[]{:S(2)}, u32[]{:S(2)}) %collective-permute-start.2) | collective-permute-done | bytes 589856 | tf_op jit(solution)/shard_map/ppermute | solution.py:367
  63.7 2.7 %collective-permute-start.11 = (bf16[384,768]{1,0:T(8,128)(2,1)S(1)}, bf16[384,768]{1,0:T(8,128)(2,1)}, u32[]{:S(2)}, u32[]{:S(2)}) collective-permute-start(bf16[384,768]{1,0:T(8,128)(2,1)S(1)} %collective-permute-done.9.refs_11_.refs_12_), channel_id=1, source_target_pairs={{0,224},{32,0},{64,32},{96,64},{128,96},{160,128},{192,160},{224,1... | collective-permute-start | bytes 1769480 | tf_op jit(solution)/shard_map/ppermute | solution.py:368
  66.4 9.1 %collective-permute-done.3.refs_4_ = bf16[384,768]{1,0:T(8,128)(2,1)S(1)} collective-permute-done((bf16[384,768]{1,0:T(8,128)(2,1)S(1)}, bf16[384,768]{1,0:T(8,128)(2,1)S(1)}, u32[]{:S(2)}, u32[]{:S(2)}) %collective-permute-start.3) | collective-permute-done | bytes 589856 | tf_op jit(solution)/shard_map/ppermute | solution.py:368
  75.5 2.4 %collective-permute-start.5 = (bf16[384,768]{1,0:T(8,128)(2,1)S(1)}, bf16[384,768]{1,0:T(8,128)(2,1)S(1)}, u32[]{:S(2)}, u32[]{:S(2)}) collective-permute-start(bf16[384,768]{1,0:T(8,128)(2,1)S(1)} %collective-permute-done.3.refs_4_), channel_id=1, source_target_pairs={{0,224},{32,0},{64,32},{96,64},{128,96},{160,128},{192,160},{224,1... | collective-permute-start | bytes 1769480 | tf_op jit(solution)/shard_map/ppermute | solution.py:368
  77.9 11.0 %collective-permute-done.4.refs_5_ = bf16[384,768]{1,0:T(8,128)(2,1)} collective-permute-done((bf16[384,768]{1,0:T(8,128)(2,1)S(1)}, bf16[384,768]{1,0:T(8,128)(2,1)}, u32[]{:S(2)}, u32[]{:S(2)}) %collective-permute-start.4) | collective-permute-done | bytes 589856 | tf_op jit(solution)/shard_map/ppermute | solution.py:367
  89.0 2.9 %collective-permute-start.13 = (bf16[384,768]{1,0:T(8,128)(2,1)}, bf16[384,768]{1,0:T(8,128)(2,1)S(1)}, u32[]{:S(2)}, u32[]{:S(2)}) collective-permute-start(bf16[384,768]{1,0:T(8,128)(2,1)} %collective-permute-done.11.refs_13_.refs_14_), channel_id=1, source_target_pairs={{0,224},{32,0},{64,32},{96,64},{128,96},{160,128},{192,160},{224,1... | collective-permute-start | bytes 1769480 | tf_op jit(solution)/shard_map/ppermute | solution.py:370
  91.9 9.0 %collective-permute-done.5.refs_6_ = bf16[384,768]{1,0:T(8,128)(2,1)S(1)} collective-permute-done((bf16[384,768]{1,0:T(8,128)(2,1)S(1)}, bf16[384,768]{1,0:T(8,128)(2,1)S(1)}, u32[]{:S(2)}, u32[]{:S(2)}) %collective-permute-start.5) | collective-permute-done | bytes 589856 | tf_op jit(solution)/shard_map/ppermute | solution.py:368
  101.8 6.8 %shard_map.148.sums_ref = f32[256,768]{1,0:T(8,128)} custom-call(bf16[256,12416]{1,0:T(8,128)(2,1)} %all-gather.4.cloned.1.call-done.rows_ref.x_ref.dy_ref.prob_ref, bf16[384,768]{1,0:T(8,128)(2,1)} %get-tuple-element.22.refs_0_, bf16[384,768]{1,0:T(8,128)(2,1)} %copy-done.6, bf16[384,768]{1,0:T(8,128)(2,1)} %copy-done.7, bf16[384,768]{1,0:T(8,128)(2,1)} %copy-done.10, ...), custom_call_target="tpu_custom_call" | custom-call | tf_op jit(solution)/shard_map/pallas_call | solution.py:125
  108.6 5.6 %collective-permute-done.12.first_ref.refs_7_ = bf16[384,768]{1,0:T(8,128)(2,1)S(1)} collective-permute-done((bf16[384,768]{1,0:T(8,128)(2,1)}, bf16[384,768]{1,0:T(8,128)(2,1)S(1)}, u32[]{:S(2)}, u32[]{:S(2)}) %collective-permute-start.12) | collective-permute-done | bytes 589856 | tf_op jit(solution)/shard_map/ppermute | solution.py:370
  115.1 0.8 copy-done.5
  115.9 3.3 %shard_map.149 = (bf16[256,768]{1,0:T(8,128)(2,1)}, bf16[256,128]{1,0:T(8,128)(2,1)}) custom-call(bf16[256,12416]{1,0:T(8,128)(2,1)} %all-gather.4.cloned.1.call-done.rows_ref.x_ref.dy_ref.prob_ref, bf16[256,12416]{1,0:T(8,128)(2,1)} %all-gather.4.cloned.1.call-done.rows_ref.x_ref.dy_ref.prob_ref, ...), custom_call_target="tpu_custom_call" | custom-call | tf_op jit(solution)/shard_map/pallas_call | solution.py:167
  119.2 7.9 %shard_map.150 = (bf16[128,6272]{1,0:T(8,128)(2,1)}, bf16[128,6272]{1,0:T(8,128)(2,1)}) custom-call(s32[1]{0:T(128)} %bitcast.5.core_ref, bf16[256,768]{1,0:T(8,128)(2,1)} %get-tuple-element.24.acts_ref, bf16[256,128]{1,0:T(8,128)(2,1)} %get-tuple-element.25.prob_ref, bf16[384,768]{1,0:T(8,128)(2,1)} %get-tuple-element.22.refs_0_, ...), custom_call_target="tpu_custom_call" | custom-call | tf_op jit(solution)/shard_map/pallas_call | solution.py:218
  127.1 3.8 %collective-permute-start.14 = (bf16[128,6272]{1,0:T(8,128)(2,1)}, bf16[128,6272]{1,0:T(8,128)(2,1)S(1)}, u32[]{:S(2)}, u32[]{:S(2)}) collective-permute-start(bf16[128,6272]{1,0:T(8,128)(2,1)} %get-tuple-element.27), channel_id=1, source_target_pairs={{0,1},{1,0},{2,3},{3,2},{4,5},{5,4},{6,7},{7,6},{8,9},{9,8},{10,11... | collective-permute-start | bytes 4816904 | tf_op jit(solution)/shard_map/ppermute | solution.py:419
  130.9 3.3 %collective-permute-done.14.b_ref = bf16[128,6272]{1,0:T(8,128)(2,1)S(1)} collective-permute-done((bf16[128,6272]{1,0:T(8,128)(2,1)}, bf16[128,6272]{1,0:T(8,128)(2,1)S(1)}, u32[]{:S(2)}, u32[]{:S(2)}) %collective-permute-start.14) | collective-permute-done | bytes 1605664 | tf_op jit(solution)/shard_map/ppermute | solution.py:419
  134.2 1.4 copy-done.3
  135.6 1.9 %shard_map.151 = bf16[128,6272]{1,0:T(8,128)(2,1)} custom-call(bf16[128,6272]{1,0:T(8,128)(2,1)S(1)} %copy-done.3, bf16[128,6272]{1,0:T(8,128)(2,1)S(1)} %collective-permute-done.14.b_ref), custom_call_target="tpu_custom_call" | custom-call | tf_op jit(solution)/shard_map/pallas_call | solution.py:242
  137.5 6.7 %all-to-all-start = ((bf16[16,8,6272]{2,1,0:T(8,128)(2,1)}), bf16[16,8,6272]{2,1,0:T(8,128)(2,1)S(1)}, u32[]{:S(2)}, u32[]{:S(2)}) async-start(bf16[16,8,6272]{2,1,0:T(8,128)(2,1)} %bitcast.8), calls=%async_computation | async-start | bytes 3211264 | tf_op jit(solution)/shard_map/all_to_all | solution.py:421
  144.3 2.8 %copy-done = bf16[8,256,1536]{2,1,0:T(8,128)(2,1)S(1)} copy-done((bf16[8,256,1536]{2,1,0:T(8,128)(2,1)S(1)}, bf16[8,256,1536]{2,1,0:T(8,128)(2,1)}, u32[]{:S(2)}) %copy-start) | copy-done | bytes 6291480
  147.1 2.4 %shard_map.152 = (bf16[768,2048]{1,0:T(8,128)(2,1)S(1)}, bf16[2048,768]{1,0:T(8,128)(2,1)S(1)}) custom-call(bf16[2048,1536]{1,0:T(8,128)(2,1)S(1)} %bitcast.15, bf16[2048,1536]{1,0:T(8,128)(2,1)S(1)} %bitcast.16), custom_call_target="tpu_custom_call" | custom-call | tf_op jit(solution)/shard_map/pallas_call | solution.py:259
  149.6 1.7 copy-done.1
  151.2 1.7 copy-done.2
  152.9 14.0 %all-to-all-done = bf16[16,8,6272]{2,1,0:T(8,128)(2,1)S(1)} async-done(((bf16[16,8,6272]{2,1,0:T(8,128)(2,1)}), bf16[16,8,6272]{2,1,0:T(8,128)(2,1)S(1)}, u32[]{:S(2)}, u32[]{:S(2)}) %all-to-all-start) | async-done | bytes 1605664 | tf_op jit(solution)/shard_map/all_to_all | solution.py:421
  168.3 1.8 convolution_convert_fusion
  170.6 7.2 %shard_map.153 = (f32[768,256]{1,0:T(8,128)}, f32[768,256]{1,0:T(8,128)}, f32[256,768]{1,0:T(8,128)}) custom-call(bf16[768,2048]{1,0:T(8,128)(2,1)} %copy-done.1, bf16[2048,768]{1,0:T(8,128)(2,1)} %copy-done.2, bf16[2048,768]{1,0:T(8,128)(2,1)} %all-gather.8.cloned.1.call-done.acts_ref), custom_call_target="tpu_custom_call" | custom-call | tf_op jit(solution)/shard_map/pallas_call | solution.py:289
  (59 shorter events, 4.7 us)
Async XLA Ops:
  7.2 94.6 %all-gather.4.cloned.1.call-start = ((), (), s32[]{:S(2)}) async-start(), calls=%async_computation.2 | async-start | bytes 6555648 | tf_op jit(solution)/shard_map/all_gather | solution.py:404
  10.6 133.6 %all-gather.6.cloned.1.call-start = ((), (), s32[]{:S(2)}) async-start(), calls=%async_computation.3 | async-start | bytes 6488064 | tf_op jit(solution)/shard_map/all_gather | solution.py:410
  13.2 36.3 %collective-permute-start = (bf16[384,768]{1,0:T(8,128)(2,1)}, bf16[384,768]{1,0:T(8,128)(2,1)S(1)}, u32[]{:S(2)}, u32[]{:S(2)}) collective-permute-start(bf16[384,768]{1,0:T(8,128)(2,1)} %get-tuple-element.22.refs_0_), channel_id=1, source_target_pairs={{0,32},{32,64},{64,96},{96,128},{128,160},{160,192},{192,224},{224... | collective-permute-start | bytes 1769480 | tf_op jit(solution)/shard_map/ppermute | solution.py:367
  15.6 33.9 %collective-permute-start.1 = (bf16[384,768]{1,0:T(8,128)(2,1)}, bf16[384,768]{1,0:T(8,128)(2,1)S(1)}, u32[]{:S(2)}, u32[]{:S(2)}) collective-permute-start(bf16[384,768]{1,0:T(8,128)(2,1)} %get-tuple-element.22.refs_0_), channel_id=1, source_target_pairs={{0,224},{32,0},{64,32},{96,64},{128,96},{160,128},{192,160},{224,1... | collective-permute-start | bytes 1769480 | tf_op jit(solution)/shard_map/ppermute | solution.py:368
  19.6 30.0 %collective-permute-start.6 = (bf16[384,768]{1,0:T(8,128)(2,1)}, bf16[384,768]{1,0:T(8,128)(2,1)S(1)}, u32[]{:S(2)}, u32[]{:S(2)}) collective-permute-start(bf16[384,768]{1,0:T(8,128)(2,1)} %get-tuple-element.23.refs_7_.refs_8_), channel_id=1, source_target_pairs={{0,32},{32,64},{64,96},{96,128},{128,160},{160,192},{192,224},{224... | collective-permute-start | bytes 1769480 | tf_op jit(solution)/shard_map/ppermute | solution.py:367
  19.6 30.0 %collective-permute-start.7 = (bf16[384,768]{1,0:T(8,128)(2,1)}, bf16[384,768]{1,0:T(8,128)(2,1)S(1)}, u32[]{:S(2)}, u32[]{:S(2)}) collective-permute-start(bf16[384,768]{1,0:T(8,128)(2,1)} %get-tuple-element.23.refs_7_.refs_8_), channel_id=1, source_target_pairs={{0,224},{32,0},{64,32},{96,64},{128,96},{160,128},{192,160},{224,1... | collective-permute-start | bytes 1769480 | tf_op jit(solution)/shard_map/ppermute | solution.py:368
  49.5 52.2 %copy-start.6 = (bf16[384,768]{1,0:T(8,128)(2,1)}, bf16[384,768]{1,0:T(8,128)(2,1)S(1)}, u32[]{:S(2)}) copy-start(bf16[384,768]{1,0:T(8,128)(2,1)S(1)} %collective-permute-done.refs_1_) | copy-start | bytes 1769476
  49.5 52.2 %copy-start.7 = (bf16[384,768]{1,0:T(8,128)(2,1)}, bf16[384,768]{1,0:T(8,128)(2,1)S(1)}, u32[]{:S(2)}) copy-start(bf16[384,768]{1,0:T(8,128)(2,1)S(1)} %collective-permute-done.1.refs_2_) | copy-start | bytes 1769476
  49.5 52.2 %copy-start.8 = (bf16[384,768]{1,0:T(8,128)(2,1)}, bf16[384,768]{1,0:T(8,128)(2,1)S(1)}, u32[]{:S(2)}) copy-start(bf16[384,768]{1,0:T(8,128)(2,1)S(1)} %collective-permute-done.6.refs_8_.refs_9_) | copy-start | bytes 1769476
  49.6 52.2 %copy-start.9 = (bf16[384,768]{1,0:T(8,128)(2,1)}, bf16[384,768]{1,0:T(8,128)(2,1)S(1)}, u32[]{:S(2)}) copy-start(bf16[384,768]{1,0:T(8,128)(2,1)S(1)} %collective-permute-done.7.refs_9_.refs_10_) | copy-start | bytes 1769476
  49.6 121.1 %all-gather.8.cloned.1.call-start = ((), (), s32[]{:S(2)}) async-start(), calls=%async_computation.4 | async-start | bytes 3538944 | tf_op jit(solution)/shard_map/all_gather | solution.py:414
  49.6 14.1 %collective-permute-start.2 = (bf16[384,768]{1,0:T(8,128)(2,1)S(1)}, bf16[384,768]{1,0:T(8,128)(2,1)S(1)}, u32[]{:S(2)}, u32[]{:S(2)}) collective-permute-start(bf16[384,768]{1,0:T(8,128)(2,1)S(1)} %collective-permute-done.refs_1_), channel_id=1, source_target_pairs={{0,32},{32,64},{64,96},{96,128},{128,160},{160,192},{192,224},{224... | collective-permute-start | bytes 1769480 | tf_op jit(solution)/shard_map/ppermute | solution.py:367
  51.9 11.8 %collective-permute-start.9 = (bf16[384,768]{1,0:T(8,128)(2,1)S(1)}, bf16[384,768]{1,0:T(8,128)(2,1)S(1)}, u32[]{:S(2)}, u32[]{:S(2)}) collective-permute-start(bf16[384,768]{1,0:T(8,128)(2,1)S(1)} %collective-permute-done.7.refs_9_.refs_10_), channel_id=1, source_target_pairs={{0,224},{32,0},{64,32},{96,64},{128,96},{160,128},{192,160},{224,1... | collective-permute-start | bytes 1769480 | tf_op jit(solution)/shard_map/ppermute | solution.py:368
  52.4 23.1 %collective-permute-start.3 = (bf16[384,768]{1,0:T(8,128)(2,1)S(1)}, bf16[384,768]{1,0:T(8,128)(2,1)S(1)}, u32[]{:S(2)}, u32[]{:S(2)}) collective-permute-start(bf16[384,768]{1,0:T(8,128)(2,1)S(1)} %collective-permute-done.1.refs_2_), channel_id=1, source_target_pairs={{0,224},{32,0},{64,32},{96,64},{128,96},{160,128},{192,160},{224,1... | collective-permute-start | bytes 1769480 | tf_op jit(solution)/shard_map/ppermute | solution.py:368
  52.8 25.1 %collective-permute-start.8 = (bf16[384,768]{1,0:T(8,128)(2,1)S(1)}, bf16[384,768]{1,0:T(8,128)(2,1)S(1)}, u32[]{:S(2)}, u32[]{:S(2)}) collective-permute-start(bf16[384,768]{1,0:T(8,128)(2,1)S(1)} %collective-permute-done.6.refs_8_.refs_9_), channel_id=1, source_target_pairs={{0,32},{32,64},{64,96},{96,128},{128,160},{160,192},{192,224},{224... | collective-permute-start | bytes 1769480 | tf_op jit(solution)/shard_map/ppermute | solution.py:367
  63.7 25.3 %copy-start.10 = (bf16[384,768]{1,0:T(8,128)(2,1)}, bf16[384,768]{1,0:T(8,128)(2,1)S(1)}, u32[]{:S(2)}) copy-start(bf16[384,768]{1,0:T(8,128)(2,1)S(1)} %collective-permute-done.2.refs_3_) | copy-start | bytes 1769476
  63.7 25.3 %collective-permute-start.4 = (bf16[384,768]{1,0:T(8,128)(2,1)S(1)}, bf16[384,768]{1,0:T(8,128)(2,1)}, u32[]{:S(2)}, u32[]{:S(2)}) collective-permute-start(bf16[384,768]{1,0:T(8,128)(2,1)S(1)} %collective-permute-done.2.refs_3_), channel_id=1, source_target_pairs={{0,32},{32,64},{64,96},{96,128},{128,160},{160,192},{192,224},{224... | collective-permute-start | bytes 1769480 | tf_op jit(solution)/shard_map/ppermute | solution.py:367
  63.7 25.3 %copy-start.11 = (bf16[384,768]{1,0:T(8,128)(2,1)}, bf16[384,768]{1,0:T(8,128)(2,1)S(1)}, u32[]{:S(2)}) copy-start(bf16[384,768]{1,0:T(8,128)(2,1)S(1)} %collective-permute-done.9.refs_11_.refs_12_) | copy-start | bytes 1769476
  63.7 25.3 %collective-permute-start.11 = (bf16[384,768]{1,0:T(8,128)(2,1)S(1)}, bf16[384,768]{1,0:T(8,128)(2,1)}, u32[]{:S(2)}, u32[]{:S(2)}) collective-permute-start(bf16[384,768]{1,0:T(8,128)(2,1)S(1)} %collective-permute-done.9.refs_11_.refs_12_), channel_id=1, source_target_pairs={{0,224},{32,0},{64,32},{96,64},{128,96},{160,128},{192,160},{224,1... | collective-permute-start | bytes 1769480 | tf_op jit(solution)/shard_map/ppermute | solution.py:368
  75.5 13.5 %copy-start.12 = (bf16[384,768]{1,0:T(8,128)(2,1)}, bf16[384,768]{1,0:T(8,128)(2,1)S(1)}, u32[]{:S(2)}) copy-start(bf16[384,768]{1,0:T(8,128)(2,1)S(1)} %collective-permute-done.3.refs_4_) | copy-start | bytes 1769476
  75.5 25.4 %collective-permute-start.5 = (bf16[384,768]{1,0:T(8,128)(2,1)S(1)}, bf16[384,768]{1,0:T(8,128)(2,1)S(1)}, u32[]{:S(2)}, u32[]{:S(2)}) collective-permute-start(bf16[384,768]{1,0:T(8,128)(2,1)S(1)} %collective-permute-done.3.refs_4_), channel_id=1, source_target_pairs={{0,224},{32,0},{64,32},{96,64},{128,96},{160,128},{192,160},{224,1... | collective-permute-start | bytes 1769480 | tf_op jit(solution)/shard_map/ppermute | solution.py:368
  77.9 23.0 %copy-start.13 = (bf16[384,768]{1,0:T(8,128)(2,1)}, bf16[384,768]{1,0:T(8,128)(2,1)S(1)}, u32[]{:S(2)}) copy-start(bf16[384,768]{1,0:T(8,128)(2,1)S(1)} %collective-permute-done.8.refs_10_.refs_11_) | copy-start | bytes 1769476
  77.9 23.8 %collective-permute-start.10 = (bf16[384,768]{1,0:T(8,128)(2,1)S(1)}, bf16[384,768]{1,0:T(8,128)(2,1)}, u32[]{:S(2)}, u32[]{:S(2)}) collective-permute-start(bf16[384,768]{1,0:T(8,128)(2,1)S(1)} %collective-permute-done.8.refs_10_.refs_11_), channel_id=1, source_target_pairs={{0,32},{32,64},{64,96},{96,128},{128,160},{160,192},{192,224},{224... | collective-permute-start | bytes 1769480 | tf_op jit(solution)/shard_map/ppermute | solution.py:367
  89.0 25.3 %collective-permute-start.12 = (bf16[384,768]{1,0:T(8,128)(2,1)}, bf16[384,768]{1,0:T(8,128)(2,1)S(1)}, u32[]{:S(2)}, u32[]{:S(2)}) collective-permute-start(bf16[384,768]{1,0:T(8,128)(2,1)} %collective-permute-done.4.refs_5_), channel_id=1, source_target_pairs={{0,32},{32,64},{64,96},{96,128},{128,160},{160,192},{192,224},{224... | collective-permute-start | bytes 1769480 | tf_op jit(solution)/shard_map/ppermute | solution.py:370
  89.0 25.3 %collective-permute-start.13 = (bf16[384,768]{1,0:T(8,128)(2,1)}, bf16[384,768]{1,0:T(8,128)(2,1)S(1)}, u32[]{:S(2)}, u32[]{:S(2)}) collective-permute-start(bf16[384,768]{1,0:T(8,128)(2,1)} %collective-permute-done.11.refs_13_.refs_14_), channel_id=1, source_target_pairs={{0,224},{32,0},{64,32},{96,64},{128,96},{160,128},{192,160},{224,1... | collective-permute-start | bytes 1769480 | tf_op jit(solution)/shard_map/ppermute | solution.py:370
  127.1 7.1 %collective-permute-start.14 = (bf16[128,6272]{1,0:T(8,128)(2,1)}, bf16[128,6272]{1,0:T(8,128)(2,1)S(1)}, u32[]{:S(2)}, u32[]{:S(2)}) collective-permute-start(bf16[128,6272]{1,0:T(8,128)(2,1)} %get-tuple-element.27), channel_id=1, source_target_pairs={{0,1},{1,0},{2,3},{3,2},{4,5},{5,4},{6,7},{7,6},{8,9},{9,8},{10,11... | collective-permute-start | bytes 4816904 | tf_op jit(solution)/shard_map/ppermute | solution.py:419
  134.2 1.4 copy-start.3
  137.5 29.4 %all-to-all-start = ((bf16[16,8,6272]{2,1,0:T(8,128)(2,1)}), bf16[16,8,6272]{2,1,0:T(8,128)(2,1)S(1)}, u32[]{:S(2)}, u32[]{:S(2)}) async-start(bf16[16,8,6272]{2,1,0:T(8,128)(2,1)} %bitcast.8), calls=%async_computation | async-start | bytes 3211264 | tf_op jit(solution)/shard_map/all_to_all | solution.py:421
  144.3 2.9 %copy-start = (bf16[8,256,1536]{2,1,0:T(8,128)(2,1)S(1)}, bf16[8,256,1536]{2,1,0:T(8,128)(2,1)}, u32[]{:S(2)}) copy-start(bf16[8,256,1536]{2,1,0:T(8,128)(2,1)} %all-gather.6.cloned.1.call-done) | copy-start | bytes 18874372
  149.5 1.7 copy-start.1
  151.2 1.7 copy-start.2
  152.9 14.8 %copy-start.15 = (s32[1,128]{1,0:T(1,128)S(1)}, s32[1,128]{1,0:T(1,128)}, u32[]{:S(2)}) copy-start(s32[1,128]{1,0:T(1,128)} %get-tuple-element.20) | copy-start | bytes 1540
  (3 other events, 2.5 us)
Sparse Core Ops, SparseCore 0:
  11.2 58.4 all-gather.3
  72.3 53.1 all-gather.5
  127.2 43.3 all-gather.7

commit v5 on v4

--- a/solution.py
+++ b/solution.py
@@ -81,12 +81,11 @@
     )(*quants, *scales)
 
 
-def pre_sums(rows, first_parts, second_parts):
+def pre_sums(rows, width, first_parts, second_parts):
     count = len(first_parts)
     half, wide = first_parts[0][1].shape
     part, both = 2 * half, wide // 3 * 2
     slots = rows.shape[0]
-    width = (rows.shape[1] - LANES) // 2
     places = [r for r, _ in first_parts]
     assert places == [r for r, _ in second_parts]
 
@@ -137,14 +136,13 @@
     )(rows, *weights)
 
 
-def activations(rows, sums, first_part, second_part):
+def activations(rows, width, sums, first_part, second_part):
     count = rows.shape[0]
     far, first = first_part
     second = second_part[1]
     half, wide = first.shape
     part, units = 2 * half, wide // 3
     both = 2 * units
-    width = (rows.shape[1] - LANES) // 2
 
     def body(x_ref, dy_ref, prob_ref, sums_ref, first_ref, second_ref, acts_ref, prob_out):
         pre = sums_ref[:, :both] + contract(x_ref[:, :half], first_ref[:, :both], 1, 0)
@@ -248,31 +246,55 @@
     )(mine, other)
 
 
-def split_columns(columns, part):
-    slots = columns.shape[0]
-    tile = 256
-
-    def body(x_ref, weighted_ref, features, weighted):
-        features[...] = x_ref[...].astype(F32).T.astype(BF16)
-        weighted[...] = weighted_ref[...]
-
-    return kernel_call(
-        body,
-        (
-            jax.ShapeDtypeStruct((part, slots), BF16),
-            jax.ShapeDtypeStruct((slots, part), BF16),
-        ),
-        16,
-        grid=(slots // tile,),
-        in_specs=[
-            pl.BlockSpec((tile, part), lambda i: (i, 0)),
-            pl.BlockSpec((tile, part), lambda i: (i, 1)),
+def joined(packed, sides):
+    ring, _, wide = sides.shape
+    start = packed.shape[1]
+
+    def body(packed_ref, sides_ref, out):
+        out[:, :start] = packed_ref[...]
+        for d in range(ring):
+            out[:, start + d * wide : start + (d + 1) * wide] = sides_ref[d]
+
+    shape = (CAP, start + ring * wide)
+    return kernel_call(
+        body,
+        jax.ShapeDtypeStruct(shape, BF16),
+        60,
+        in_specs=[whole(packed.shape), whole(sides.shape)],
+        out_specs=whole(shape),
+    )(packed, sides)
+
+
+def split_columns(rows, start, part, ring):
+    slots = rows.shape[0]
+
+    def body(rows_ref, features, weighted, sides, sems):
+        copies = [
+            pltpu.make_async_copy(
+                rows_ref.at[:, pl.ds(start + d * 2 * part, 2 * part)], sides.at[d], sems.at[d]
+            )
+            for d in range(ring)
+        ]
+        for copy in copies:
+            copy.start()
+        for d in range(ring):
+            copies[d].wait()
+            at = slice(d * slots, (d + 1) * slots)
+            features[:, at] = sides[d, :, :part].astype(F32).T.astype(BF16)
+            weighted[at, :] = sides[d, :, part:]
+
+    shapes = ((part, ring * slots), (ring * slots, part))
+    return kernel_call(
+        body,
+        tuple(jax.ShapeDtypeStruct(v, BF16) for v in shapes),
+        60,
+        in_specs=[far_memory()],
+        out_specs=tuple(whole(v) for v in shapes),
+        scratch_shapes=[
+            pltpu.VMEM((ring, slots, 2 * part), BF16),
+            pltpu.SemaphoreType.DMA((ring,)),
         ],
-        out_specs=(
-            pl.BlockSpec((part, tile), lambda i: (0, i)),
-            pl.BlockSpec((tile, part), lambda i: (i, 0)),
-        ),
-    )(columns, columns)
+    )(rows)
 
 
 def weight_sums(features, weighted, acts):
@@ -401,16 +423,12 @@
         packed, sides, token_slot = pick_slots(
             place, route_mask, route_prob, x_quant, x_scale, grad_out, ring
         )
-        rows = lax.all_gather(packed, CORE_FIRST, axis=0, tiled=True)
-
         sides = lax.all_to_all(sides, "fsdp", split_axis=0, concat_axis=0, tiled=True)
-        sides, *_ = lax.optimization_barrier(
-            (sides, *(w for _, w in first_near[1:3] + second_near[1:3]))
-        )
-        columns = lax.all_gather(sides, CORE_FIRST, axis=1, tiled=True).reshape(-1, 2 * part)
-
-        sums = pre_sums(rows, first_near, second_near)
-        acts, prob_lanes = activations(rows, sums, first_far, second_far)
+        sides, *_ = lax.optimization_barrier((sides, *(w for _, w in first_near[1:3])))
+        rows = lax.all_gather(joined(packed, sides), CORE_FIRST, axis=0, tiled=True)
+
+        sums = pre_sums(rows, width, first_near, second_near)
+        acts, prob_lanes = activations(rows, width, sums, first_far, second_far)
         all_acts = lax.all_gather(acts, "fsdp", axis=0, tiled=True)
 
         give, keep = slot_sums(
@@ -428,7 +446,7 @@
         grad_prob = jnp.sum(jnp.where(table, mine_prob[:, None], 0.0), axis=0)
 
         grad_gate, grad_up, grad_down = weight_sums(
-            *split_columns(columns, part), all_acts
+            *split_columns(rows, 2 * width + LANES, part, ring), all_acts
         )
         return (grad_x, grad_prob, grad_gate, grad_up, grad_down)
 

time: 185 us -> 183 us (0.989)
  blocking collectives: 27.3 us -> 14.1 us
  waiting for transfers between devices: 62.6 us -> 74 us
  local copies, waits for them, and re-layouts: 10.4 us -> 2.53 us
  Pallas kernels: 35.4 us -> 40.8 us
    all_to_all x1, blocking collectives: 27.3 us -> 14.1 us  [on_device(): lax.all_to_all(sides, 'fsdp', split_axis=0, concat_axis=0, tiled=True)]
    unnamed x33 -> x25, local copies, waits for them, and re-layouts: 10.2 us -> 2.3 us
    pallas_call x1 -> x2, Pallas kernels: 2.41 us -> 7.94 us  [the longest x1 5.72 us: split_columns(): kernel_call(body, tuple((jax.ShapeDtypeStruct(v, BF16) for v in shapes)),...]
    ppermute x6, waiting for transfers between devices: 20.9 us -> 25.9 us  [ring_gather(): ahead = lax.ppermute(ahead, axis, up)]
    all_gather x2 -> x1, waiting for transfers between devices: 0.02 us -> 4.28 us  [on_device(): rows = lax.all_gather(joined(packed, sides), CORE_FIRST, axis=0, tiled=True)]
    ppermute x1, waiting for transfers between devices: 5.65 us -> 1.49 us  [ring_gather(): lax.ppermute(ahead, axis, up)]
    ppermute x6, waiting for transfers between devices: 18.1 us -> 22 us  [ring_gather(): behind = lax.ppermute(behind, axis, down)]
    all_to_all x1, waiting for transfers between devices: 14 us -> 17 us  [on_device(): lax.all_to_all(both, PLANE, split_axis=0, concat_axis=0, tiled=True)]
  transfers between devices with their start and end apart: 19 -> 18, of which waited for: 8 -> 10; matrix products, arithmetic and copies ran while one was open for 2% -> 2% of each run, Pallas kernels for 13% -> 14%
where the time goes in v5:
time: 183 us; the launch traced here: 182 us
  waiting for transfers between devices  74 us (40%)
  Pallas kernels  40.8 us (22%)
  starting transfers between devices  33.6 us (18%)
  between operations  14.2 us (8%)
  blocking collectives  14.1 us (8%)
  local copies, waits for them, and re-layouts  2.53 us (1%)
    ppermute x6, waiting for transfers between devices, ring_gather(): ahead = lax.ppermute(ahead, axis, up)  25.9 us
    ppermute x6, waiting for transfers between devices, ring_gather(): behind = lax.ppermute(behind, axis, down)  22 us
    all_to_all x1, waiting for transfers between devices, on_device(): lax.all_to_all(both, PLANE, split_axis=0, concat_axis=0, tiled=True)  17 us
    ppermute x6, starting transfers between devices, ring_gather(): behind = lax.ppermute(behind, axis, down)  14.6 us
    all_to_all x1, blocking collectives, on_device(): lax.all_to_all(sides, 'fsdp', split_axis=0, concat_axis=0, tiled=True)  14.1 us
    pallas_call x1, Pallas kernels, slot_sums(): kernel_call(body, (jax.ShapeDtypeStruct(shape, BF16),) * 2, 60, scalars=1...  7.74 us
    pallas_call x1, Pallas kernels, weight_sums(): kernel_call(body, tuple((jax.ShapeDtypeStruct(v, F32) for v in shapes)),...  7.24 us
    pallas_call x1, Pallas kernels, pre_sums(): kernel_call(body, jax.ShapeDtypeStruct(shape, F32), 60, in_specs=[far_mem...  6.83 us
  transfers between devices with their start and end apart: 18, of which 10 were waited for; matrix products, arithmetic and copies ran while one was open for 2% of the time, Pallas kernels for 14%

profile of v5, /device:TPU:1, one launch (start us, length us, event | category | flops | bytes accessed | tf_op | source)
XLA Modules:
  0.0 182.1 jit_solution(5392771563060535407)
XLA Ops:
  7.2 2.5 %shard_map.147 = (bf16[384,768]{1,0:T(8,128)(2,1)}, bf16[384,768]{1,0:T(8,128)(2,1)}) custom-call(bf16[768,256]{1,0:T(8,128)(2,1)} %gate.1, bf16[768,256]{1,0:T(8,128)(2,1)} %up.1, bf16[256,768]{1,0:T(8,128)(2,1)} %down.1, f32[2,6]{1,0:T(2,128)} %bitcast.17, f32[2,6]{1,0:T(2,128)} %bitcast.18, f32[2,6]{1,0:T(2,128)} %down_s.1), custom_call_target="tpu_custom_call" | custom-call | tf_op jit(solution)/shard_map/pallas_call | solution.py:75
  9.7 2.5 %collective-permute-start = (bf16[384,768]{1,0:T(8,128)(2,1)}, bf16[384,768]{1,0:T(8,128)(2,1)S(1)}, u32[]{:S(2)}, u32[]{:S(2)}) collective-permute-start(bf16[384,768]{1,0:T(8,128)(2,1)} %get-tuple-element.23.refs_0_), channel_id=1, source_target_pairs={{0,32},{32,64},{64,96},{96,128},{128,160},{160,192},{192,224},{224... | collective-permute-start | bytes 1769480 | tf_op jit(solution)/shard_map/ppermute | solution.py:389
  12.2 3.9 %collective-permute-start.1 = (bf16[384,768]{1,0:T(8,128)(2,1)}, bf16[384,768]{1,0:T(8,128)(2,1)S(1)}, u32[]{:S(2)}, u32[]{:S(2)}) collective-permute-start(bf16[384,768]{1,0:T(8,128)(2,1)} %get-tuple-element.23.refs_0_), channel_id=1, source_target_pairs={{0,224},{32,0},{64,32},{96,64},{128,96},{160,128},{192,160},{224,1... | collective-permute-start | bytes 1769480 | tf_op jit(solution)/shard_map/ppermute | solution.py:390
  16.1 3.4 %shard_map.146 = (bf16[8,12416]{1,0:T(8,128)(2,1)}, bf16[8,8,1536]{2,1,0:T(8,128)(2,1)}, s32[1,128]{1,0:T(1,128)}) custom-call(s32[1]{0:T(128)} %bitcast.place_ref, s32[1,128]{1,0:T(1,128)} %bitcast.19, bf16[1,128]{1,0:T(2,128)(2,1)} %bitcast.20, bf16[128,6144]{1,0:T(8,128)(2,1)} %x_ref.1, f32[48,128]{1,0:T(8,128)} %bitcast.16, bf16[128,6144]{1,0:T(8,128)(2,1)} %dy_ref.1), custom_call_target="tpu_custom_call" | custom-call | tf_op jit(solution)/shard_map/pallas_call | solution.py:364
  19.6 14.1 %all_to_all.10.sides_ref = bf16[8,8,1536]{2,1,0:T(8,128)(2,1)} all-to-all(bf16[8,8,1536]{2,1,0:T(8,128)(2,1)} %get-tuple-element.22), channel_id=1, replica_groups=mesh['fsdp'=8,'x'=4,'y'=4,'core'=2] {'fsdp'}, dimensions={0} | all-to-all | bytes 393216 | tf_op jit(solution)/shard_map/all_to_all | solution.py:426
  33.6 2.2 %shard_map.148 = bf16[8,24704]{1,0:T(8,128)(2,1)} custom-call(bf16[8,12416]{1,0:T(8,128)(2,1)} %get-tuple-element.21.packed_ref, bf16[8,8,1536]{2,1,0:T(8,128)(2,1)} %all_to_all.10.sides_ref), custom_call_target="tpu_custom_call" | custom-call | tf_op jit(solution)/shard_map/pallas_call | solution.py:259
  35.9 1.5 collective-permute-start.7
  38.2 1.4 collective-permute-start.2
  39.6 8.7 %collective-permute-done.7.refs_9_.refs_10_ = bf16[384,768]{1,0:T(8,128)(2,1)S(1)} collective-permute-done((bf16[384,768]{1,0:T(8,128)(2,1)S(1)}, bf16[384,768]{1,0:T(8,128)(2,1)S(1)}, u32[]{:S(2)}, u32[]{:S(2)}) %collective-permute-start.7) | collective-permute-done | bytes 589856 | tf_op jit(solution)/shard_map/ppermute | solution.py:390
  48.2 2.7 %collective-permute-start.9 = (bf16[384,768]{1,0:T(8,128)(2,1)S(1)}, bf16[384,768]{1,0:T(8,128)(2,1)S(1)}, u32[]{:S(2)}, u32[]{:S(2)}) collective-permute-start(bf16[384,768]{1,0:T(8,128)(2,1)S(1)} %collective-permute-done.7.refs_9_.refs_10_), channel_id=1, source_target_pairs={{0,224},{32,0},{64,32},{96,64},{128,96},{160,128},{192,160},{224,1... | collective-permute-start | bytes 1769480 | tf_op jit(solution)/shard_map/ppermute | solution.py:390
  52.4 11.0 %collective-permute-done.2.refs_3_ = bf16[384,768]{1,0:T(8,128)(2,1)S(1)} collective-permute-done((bf16[384,768]{1,0:T(8,128)(2,1)S(1)}, bf16[384,768]{1,0:T(8,128)(2,1)S(1)}, u32[]{:S(2)}, u32[]{:S(2)}) %collective-permute-start.2) | collective-permute-done | bytes 589856 | tf_op jit(solution)/shard_map/ppermute | solution.py:389
  63.4 2.7 %collective-permute-start.11 = (bf16[384,768]{1,0:T(8,128)(2,1)S(1)}, bf16[384,768]{1,0:T(8,128)(2,1)}, u32[]{:S(2)}, u32[]{:S(2)}) collective-permute-start(bf16[384,768]{1,0:T(8,128)(2,1)S(1)} %collective-permute-done.9.refs_11_.refs_12_), channel_id=1, source_target_pairs={{0,224},{32,0},{64,32},{96,64},{128,96},{160,128},{192,160},{224,1... | collective-permute-start | bytes 1769480 | tf_op jit(solution)/shard_map/ppermute | solution.py:390
  66.1 6.7 %collective-permute-done.3.refs_4_ = bf16[384,768]{1,0:T(8,128)(2,1)S(1)} collective-permute-done((bf16[384,768]{1,0:T(8,128)(2,1)S(1)}, bf16[384,768]{1,0:T(8,128)(2,1)S(1)}, u32[]{:S(2)}, u32[]{:S(2)}) %collective-permute-start.3) | collective-permute-done | bytes 589856 | tf_op jit(solution)/shard_map/ppermute | solution.py:390
  72.7 3.4 %collective-permute-start.5 = (bf16[384,768]{1,0:T(8,128)(2,1)S(1)}, bf16[384,768]{1,0:T(8,128)(2,1)S(1)}, u32[]{:S(2)}, u32[]{:S(2)}) collective-permute-start(bf16[384,768]{1,0:T(8,128)(2,1)S(1)} %collective-permute-done.3.refs_4_), channel_id=1, source_target_pairs={{0,224},{32,0},{64,32},{96,64},{128,96},{160,128},{192,160},{224,1... | collective-permute-start | bytes 1769480 | tf_op jit(solution)/shard_map/ppermute | solution.py:390
  76.2 12.5 %collective-permute-done.4.refs_5_ = bf16[384,768]{1,0:T(8,128)(2,1)} collective-permute-done((bf16[384,768]{1,0:T(8,128)(2,1)S(1)}, bf16[384,768]{1,0:T(8,128)(2,1)}, u32[]{:S(2)}, u32[]{:S(2)}) %collective-permute-start.4) | collective-permute-done | bytes 589856 | tf_op jit(solution)/shard_map/ppermute | solution.py:389
  88.7 2.7 %collective-permute-start.13 = (bf16[384,768]{1,0:T(8,128)(2,1)}, bf16[384,768]{1,0:T(8,128)(2,1)}, u32[]{:S(2)}, u32[]{:S(2)}) collective-permute-start(bf16[384,768]{1,0:T(8,128)(2,1)} %collective-permute-done.11.refs_13_.refs_14_), channel_id=1, source_target_pairs={{0,224},{32,0},{64,32},{96,64},{128,96},{160,128},{192,160},{224,1... | collective-permute-start | bytes 1769480 | tf_op jit(solution)/shard_map/ppermute | solution.py:392
  91.3 6.7 %collective-permute-done.5.refs_6_ = bf16[384,768]{1,0:T(8,128)(2,1)S(1)} collective-permute-done((bf16[384,768]{1,0:T(8,128)(2,1)S(1)}, bf16[384,768]{1,0:T(8,128)(2,1)S(1)}, u32[]{:S(2)}, u32[]{:S(2)}) %collective-permute-start.5) | collective-permute-done | bytes 589856 | tf_op jit(solution)/shard_map/ppermute | solution.py:390
  98.9 2.4 %collective-permute-done.10.refs_12_.refs_13_ = bf16[384,768]{1,0:T(8,128)(2,1)} collective-permute-done((bf16[384,768]{1,0:T(8,128)(2,1)S(1)}, bf16[384,768]{1,0:T(8,128)(2,1)}, u32[]{:S(2)}, u32[]{:S(2)}) %collective-permute-start.10) | collective-permute-done | bytes 589856 | tf_op jit(solution)/shard_map/ppermute | solution.py:389
  101.3 4.3 %all-gather.3.cloned.1.call-done.rows_ref.x_ref.dy_ref.prob_ref = bf16[256,24704]{1,0:T(8,128)(2,1)} async-done(((bf16[8,24704]{1,0:T(8,128)(2,1)}), bf16[256,24704]{1,0:T(8,128)(2,1)}) %all-gather.3.cloned.1.call-update) | async-done | bytes 12648464 | tf_op jit(solution)/shard_map/all_gather | solution.py:428
  105.6 6.8 %shard_map.149.sums_ref = f32[256,768]{1,0:T(8,128)} custom-call(bf16[256,24704]{1,0:T(8,128)(2,1)} %all-gather.3.cloned.1.call-done.rows_ref.x_ref.dy_ref.prob_ref, bf16[384,768]{1,0:T(8,128)(2,1)} %get-tuple-element.23.refs_0_, bf16[384,768]{1,0:T(8,128)(2,1)} %copy-done.2, bf16[384,768]{1,0:T(8,128)(2,1)} %copy-done.3, bf16[384,768]{1,0:T(8,128)(2,1)} %copy-done.6, ...), custom_call_target="tpu_custom_call" | custom-call | tf_op jit(solution)/shard_map/pallas_call | solution.py:124
  112.5 1.5 collective-permute-done.12.first_ref.refs_7_
  113.9 3.3 %shard_map.150 = (bf16[256,768]{1,0:T(8,128)(2,1)}, bf16[256,128]{1,0:T(8,128)(2,1)}) custom-call(bf16[256,24704]{1,0:T(8,128)(2,1)} %all-gather.3.cloned.1.call-done.rows_ref.x_ref.dy_ref.prob_ref, bf16[256,24704]{1,0:T(8,128)(2,1)} %all-gather.3.cloned.1.call-done.rows_ref.x_ref.dy_ref.prob_ref, ...), custom_call_target="tpu_custom_call" | custom-call | tf_op jit(solution)/shard_map/pallas_call | solution.py:165
  117.2 7.7 %shard_map.151 = (bf16[128,6272]{1,0:T(8,128)(2,1)}, bf16[128,6272]{1,0:T(8,128)(2,1)}) custom-call(s32[1]{0:T(128)} %bitcast.5.core_ref, bf16[256,768]{1,0:T(8,128)(2,1)} %get-tuple-element.26.acts_ref, bf16[256,128]{1,0:T(8,128)(2,1)} %get-tuple-element.27.prob_ref, bf16[384,768]{1,0:T(8,128)(2,1)} %get-tuple-element.23.refs_0_, ...), custom_call_target="tpu_custom_call" | custom-call | tf_op jit(solution)/shard_map/pallas_call | solution.py:216
  125.0 3.8 %collective-permute-start.14 = (bf16[128,6272]{1,0:T(8,128)(2,1)}, bf16[128,6272]{1,0:T(8,128)(2,1)S(1)}, u32[]{:S(2)}, u32[]{:S(2)}) collective-permute-start(bf16[128,6272]{1,0:T(8,128)(2,1)} %get-tuple-element.29), channel_id=1, source_target_pairs={{0,1},{1,0},{2,3},{3,2},{4,5},{5,4},{6,7},{7,6},{8,9},{9,8},{10,11... | collective-permute-start | bytes 4816904 | tf_op jit(solution)/shard_map/ppermute | solution.py:437
  128.8 3.3 %collective-permute-done.14.b_ref = bf16[128,6272]{1,0:T(8,128)(2,1)S(1)} collective-permute-done((bf16[128,6272]{1,0:T(8,128)(2,1)}, bf16[128,6272]{1,0:T(8,128)(2,1)S(1)}, u32[]{:S(2)}, u32[]{:S(2)}) %collective-permute-start.14) | collective-permute-done | bytes 1605664 | tf_op jit(solution)/shard_map/ppermute | solution.py:437
  132.1 1.4 copy-done
  133.5 1.9 %shard_map.152 = bf16[128,6272]{1,0:T(8,128)(2,1)} custom-call(bf16[128,6272]{1,0:T(8,128)(2,1)S(1)} %copy-done, bf16[128,6272]{1,0:T(8,128)(2,1)S(1)} %collective-permute-done.14.b_ref), custom_call_target="tpu_custom_call" | custom-call | tf_op jit(solution)/shard_map/pallas_call | solution.py:240
  135.4 6.8 %all-to-all-start.1 = ((bf16[16,8,6272]{2,1,0:T(8,128)(2,1)}), bf16[16,8,6272]{2,1,0:T(8,128)(2,1)S(1)}, u32[]{:S(2)}, u32[]{:S(2)}) async-start(bf16[16,8,6272]{2,1,0:T(8,128)(2,1)} %bitcast.8), calls=%async_computation.1 | async-start | bytes 3211264 | tf_op jit(solution)/shard_map/all_to_all | solution.py:439
  142.2 5.7 %shard_map.153 = (bf16[768,2048]{1,0:T(8,128)(2,1)}, bf16[2048,768]{1,0:T(8,128)(2,1)}) custom-call(bf16[256,24704]{1,0:T(8,128)(2,1)} %all-gather.3.cloned.1.call-done.rows_ref.x_ref.dy_ref.prob_ref), custom_call_target="tpu_custom_call" | custom-call | tf_op jit(solution)/shard_map/pallas_call | solution.py:287
  147.9 17.0 %all-to-all-done.1 = bf16[16,8,6272]{2,1,0:T(8,128)(2,1)S(1)} async-done(((bf16[16,8,6272]{2,1,0:T(8,128)(2,1)}), bf16[16,8,6272]{2,1,0:T(8,128)(2,1)S(1)}, u32[]{:S(2)}, u32[]{:S(2)}) %all-to-all-start.1) | async-done | bytes 1605664 | tf_op jit(solution)/shard_map/all_to_all | solution.py:439
  166.2 1.8 convolution_convert_fusion
  168.0 7.2 %shard_map.154 = (f32[768,256]{1,0:T(8,128)}, f32[768,256]{1,0:T(8,128)}, f32[256,768]{1,0:T(8,128)}) custom-call(bf16[768,2048]{1,0:T(8,128)(2,1)} %get-tuple-element.30.x_ref, bf16[2048,768]{1,0:T(8,128)(2,1)} %get-tuple-element.31.weighted_ref, bf16[2048,768]{1,0:T(8,128)(2,1)} %all-gather.5.cloned.1.call-done.acts_ref), custom_call_target="tpu_custom_call" | custom-call | tf_op jit(solution)/shard_map/pallas_call | solution.py:311
  (49 shorter events, 4.6 us)
Async XLA Ops:
  7.2 98.4 %all-gather.3.cloned.1.call-start = ((), (), s32[]{:S(2)}) async-start(), calls=%async_computation.2 | async-start | bytes 13043712 | tf_op jit(solution)/shard_map/all_gather | solution.py:428
  9.7 23.9 %collective-permute-start = (bf16[384,768]{1,0:T(8,128)(2,1)}, bf16[384,768]{1,0:T(8,128)(2,1)S(1)}, u32[]{:S(2)}, u32[]{:S(2)}) collective-permute-start(bf16[384,768]{1,0:T(8,128)(2,1)} %get-tuple-element.23.refs_0_), channel_id=1, source_target_pairs={{0,32},{32,64},{64,96},{96,128},{128,160},{160,192},{192,224},{224... | collective-permute-start | bytes 1769480 | tf_op jit(solution)/shard_map/ppermute | solution.py:389
  12.2 21.4 %collective-permute-start.1 = (bf16[384,768]{1,0:T(8,128)(2,1)}, bf16[384,768]{1,0:T(8,128)(2,1)S(1)}, u32[]{:S(2)}, u32[]{:S(2)}) collective-permute-start(bf16[384,768]{1,0:T(8,128)(2,1)} %get-tuple-element.23.refs_0_), channel_id=1, source_target_pairs={{0,224},{32,0},{64,32},{96,64},{128,96},{160,128},{192,160},{224,1... | collective-permute-start | bytes 1769480 | tf_op jit(solution)/shard_map/ppermute | solution.py:390
  16.1 19.8 %copy-start.1 = (bf16[384,768]{1,0:T(8,128)(2,1)S(1)}, bf16[384,768]{1,0:T(8,128)(2,1)}, u32[]{:S(2)}) copy-start(bf16[384,768]{1,0:T(8,128)(2,1)} %get-tuple-element.25.refs_7_.refs_8_) | copy-start | bytes 1769476
  33.6 72.0 %copy-start.2 = (bf16[384,768]{1,0:T(8,128)(2,1)}, bf16[384,768]{1,0:T(8,128)(2,1)S(1)}, u32[]{:S(2)}) copy-start(bf16[384,768]{1,0:T(8,128)(2,1)S(1)} %collective-permute-done.refs_1_) | copy-start | bytes 1769476
  33.6 72.0 %copy-start.3 = (bf16[384,768]{1,0:T(8,128)(2,1)}, bf16[384,768]{1,0:T(8,128)(2,1)S(1)}, u32[]{:S(2)}) copy-start(bf16[384,768]{1,0:T(8,128)(2,1)S(1)} %collective-permute-done.1.refs_2_) | copy-start | bytes 1769476
  35.9 132.1 %all-gather.5.cloned.1.call-start = ((), (), s32[]{:S(2)}) async-start(), calls=%async_computation.3 | async-start | bytes 3538944 | tf_op jit(solution)/shard_map/all_gather | solution.py:432
  35.9 12.3 %collective-permute-start.7 = (bf16[384,768]{1,0:T(8,128)(2,1)S(1)}, bf16[384,768]{1,0:T(8,128)(2,1)S(1)}, u32[]{:S(2)}, u32[]{:S(2)}) collective-permute-start(bf16[384,768]{1,0:T(8,128)(2,1)S(1)} %copy-done.1), channel_id=1, source_target_pairs={{0,224},{32,0},{64,32},{96,64},{128,96},{160,128},{192,160},{224,1... | collective-permute-start | bytes 1769480 | tf_op jit(solution)/shard_map/ppermute | solution.py:390
  37.4 13.9 %collective-permute-start.6 = (bf16[384,768]{1,0:T(8,128)(2,1)S(1)}, bf16[384,768]{1,0:T(8,128)(2,1)S(1)}, u32[]{:S(2)}, u32[]{:S(2)}) collective-permute-start(bf16[384,768]{1,0:T(8,128)(2,1)S(1)} %copy-done.1), channel_id=1, source_target_pairs={{0,32},{32,64},{64,96},{96,128},{128,160},{160,192},{192,224},{224... | collective-permute-start | bytes 1769480 | tf_op jit(solution)/shard_map/ppermute | solution.py:389
  38.2 25.2 %collective-permute-start.2 = (bf16[384,768]{1,0:T(8,128)(2,1)S(1)}, bf16[384,768]{1,0:T(8,128)(2,1)S(1)}, u32[]{:S(2)}, u32[]{:S(2)}) collective-permute-start(bf16[384,768]{1,0:T(8,128)(2,1)S(1)} %collective-permute-done.refs_1_), channel_id=1, source_target_pairs={{0,32},{32,64},{64,96},{96,128},{128,160},{160,192},{192,224},{224... | collective-permute-start | bytes 1769480 | tf_op jit(solution)/shard_map/ppermute | solution.py:389
  48.2 57.4 %copy-start.4 = (bf16[384,768]{1,0:T(8,128)(2,1)}, bf16[384,768]{1,0:T(8,128)(2,1)S(1)}, u32[]{:S(2)}) copy-start(bf16[384,768]{1,0:T(8,128)(2,1)S(1)} %collective-permute-done.7.refs_9_.refs_10_) | copy-start | bytes 1769476
  48.2 15.2 %collective-permute-start.9 = (bf16[384,768]{1,0:T(8,128)(2,1)S(1)}, bf16[384,768]{1,0:T(8,128)(2,1)S(1)}, u32[]{:S(2)}, u32[]{:S(2)}) collective-permute-start(bf16[384,768]{1,0:T(8,128)(2,1)S(1)} %collective-permute-done.7.refs_9_.refs_10_), channel_id=1, source_target_pairs={{0,224},{32,0},{64,32},{96,64},{128,96},{160,128},{192,160},{224,1... | collective-permute-start | bytes 1769480 | tf_op jit(solution)/shard_map/ppermute | solution.py:390
  50.9 21.8 %collective-permute-start.3 = (bf16[384,768]{1,0:T(8,128)(2,1)S(1)}, bf16[384,768]{1,0:T(8,128)(2,1)S(1)}, u32[]{:S(2)}, u32[]{:S(2)}) collective-permute-start(bf16[384,768]{1,0:T(8,128)(2,1)S(1)} %collective-permute-done.1.refs_2_), channel_id=1, source_target_pairs={{0,224},{32,0},{64,32},{96,64},{128,96},{160,128},{192,160},{224,1... | collective-permute-start | bytes 1769480 | tf_op jit(solution)/shard_map/ppermute | solution.py:390
  51.3 54.3 %copy-start.5 = (bf16[384,768]{1,0:T(8,128)(2,1)}, bf16[384,768]{1,0:T(8,128)(2,1)S(1)}, u32[]{:S(2)}) copy-start(bf16[384,768]{1,0:T(8,128)(2,1)S(1)} %collective-permute-done.6.refs_8_.refs_9_) | copy-start | bytes 1769476
  51.3 24.8 %collective-permute-start.8 = (bf16[384,768]{1,0:T(8,128)(2,1)S(1)}, bf16[384,768]{1,0:T(8,128)(2,1)S(1)}, u32[]{:S(2)}, u32[]{:S(2)}) collective-permute-start(bf16[384,768]{1,0:T(8,128)(2,1)S(1)} %collective-permute-done.6.refs_8_.refs_9_), channel_id=1, source_target_pairs={{0,32},{32,64},{64,96},{96,128},{128,160},{160,192},{192,224},{224... | collective-permute-start | bytes 1769480 | tf_op jit(solution)/shard_map/ppermute | solution.py:389
  63.4 42.2 %copy-start.6 = (bf16[384,768]{1,0:T(8,128)(2,1)}, bf16[384,768]{1,0:T(8,128)(2,1)S(1)}, u32[]{:S(2)}) copy-start(bf16[384,768]{1,0:T(8,128)(2,1)S(1)} %collective-permute-done.2.refs_3_) | copy-start | bytes 1769476
  63.4 25.3 %collective-permute-start.4 = (bf16[384,768]{1,0:T(8,128)(2,1)S(1)}, bf16[384,768]{1,0:T(8,128)(2,1)}, u32[]{:S(2)}, u32[]{:S(2)}) collective-permute-start(bf16[384,768]{1,0:T(8,128)(2,1)S(1)} %collective-permute-done.2.refs_3_), channel_id=1, source_target_pairs={{0,32},{32,64},{64,96},{96,128},{128,160},{160,192},{192,224},{224... | collective-permute-start | bytes 1769480 | tf_op jit(solution)/shard_map/ppermute | solution.py:389
  63.4 25.3 %copy-start.7 = (bf16[384,768]{1,0:T(8,128)(2,1)}, bf16[384,768]{1,0:T(8,128)(2,1)S(1)}, u32[]{:S(2)}) copy-start(bf16[384,768]{1,0:T(8,128)(2,1)S(1)} %collective-permute-done.9.refs_11_.refs_12_) | copy-start | bytes 1769476
  63.4 25.3 %collective-permute-start.11 = (bf16[384,768]{1,0:T(8,128)(2,1)S(1)}, bf16[384,768]{1,0:T(8,128)(2,1)}, u32[]{:S(2)}, u32[]{:S(2)}) collective-permute-start(bf16[384,768]{1,0:T(8,128)(2,1)S(1)} %collective-permute-done.9.refs_11_.refs_12_), channel_id=1, source_target_pairs={{0,224},{32,0},{64,32},{96,64},{128,96},{160,128},{192,160},{224,1... | collective-permute-start | bytes 1769480 | tf_op jit(solution)/shard_map/ppermute | solution.py:390
  72.7 16.0 %copy-start.8 = (bf16[384,768]{1,0:T(8,128)(2,1)}, bf16[384,768]{1,0:T(8,128)(2,1)S(1)}, u32[]{:S(2)}) copy-start(bf16[384,768]{1,0:T(8,128)(2,1)S(1)} %collective-permute-done.3.refs_4_) | copy-start | bytes 1769476
  72.7 25.3 %collective-permute-start.5 = (bf16[384,768]{1,0:T(8,128)(2,1)S(1)}, bf16[384,768]{1,0:T(8,128)(2,1)S(1)}, u32[]{:S(2)}, u32[]{:S(2)}) collective-permute-start(bf16[384,768]{1,0:T(8,128)(2,1)S(1)} %collective-permute-done.3.refs_4_), channel_id=1, source_target_pairs={{0,224},{32,0},{64,32},{96,64},{128,96},{160,128},{192,160},{224,1... | collective-permute-start | bytes 1769480 | tf_op jit(solution)/shard_map/ppermute | solution.py:390
  76.1 29.5 %copy-start.9 = (bf16[384,768]{1,0:T(8,128)(2,1)}, bf16[384,768]{1,0:T(8,128)(2,1)S(1)}, u32[]{:S(2)}) copy-start(bf16[384,768]{1,0:T(8,128)(2,1)S(1)} %collective-permute-done.8.refs_10_.refs_11_) | copy-start | bytes 1769476
  76.1 25.2 %collective-permute-start.10 = (bf16[384,768]{1,0:T(8,128)(2,1)S(1)}, bf16[384,768]{1,0:T(8,128)(2,1)}, u32[]{:S(2)}, u32[]{:S(2)}) collective-permute-start(bf16[384,768]{1,0:T(8,128)(2,1)S(1)} %collective-permute-done.8.refs_10_.refs_11_), channel_id=1, source_target_pairs={{0,32},{32,64},{64,96},{96,128},{128,160},{160,192},{192,224},{224... | collective-permute-start | bytes 1769480 | tf_op jit(solution)/shard_map/ppermute | solution.py:389
  88.7 25.3 %collective-permute-start.12 = (bf16[384,768]{1,0:T(8,128)(2,1)}, bf16[384,768]{1,0:T(8,128)(2,1)}, u32[]{:S(2)}, u32[]{:S(2)}) collective-permute-start(bf16[384,768]{1,0:T(8,128)(2,1)} %collective-permute-done.4.refs_5_), channel_id=1, source_target_pairs={{0,32},{32,64},{64,96},{96,128},{128,160},{160,192},{192,224},{224... | collective-permute-start | bytes 1769480 | tf_op jit(solution)/shard_map/ppermute | solution.py:392
  88.7 25.3 %collective-permute-start.13 = (bf16[384,768]{1,0:T(8,128)(2,1)}, bf16[384,768]{1,0:T(8,128)(2,1)}, u32[]{:S(2)}, u32[]{:S(2)}) collective-permute-start(bf16[384,768]{1,0:T(8,128)(2,1)} %collective-permute-done.11.refs_13_.refs_14_), channel_id=1, source_target_pairs={{0,224},{32,0},{64,32},{96,64},{128,96},{160,128},{192,160},{224,1... | collective-permute-start | bytes 1769480 | tf_op jit(solution)/shard_map/ppermute | solution.py:392
  98.0 0.8 copy-start.10
  125.0 7.1 %collective-permute-start.14 = (bf16[128,6272]{1,0:T(8,128)(2,1)}, bf16[128,6272]{1,0:T(8,128)(2,1)S(1)}, u32[]{:S(2)}, u32[]{:S(2)}) collective-permute-start(bf16[128,6272]{1,0:T(8,128)(2,1)} %get-tuple-element.29), channel_id=1, source_target_pairs={{0,1},{1,0},{2,3},{3,2},{4,5},{5,4},{6,7},{7,6},{8,9},{9,8},{10,11... | collective-permute-start | bytes 4816904 | tf_op jit(solution)/shard_map/ppermute | solution.py:437
  132.1 1.4 copy-start
  135.4 29.5 %all-to-all-start.1 = ((bf16[16,8,6272]{2,1,0:T(8,128)(2,1)}), bf16[16,8,6272]{2,1,0:T(8,128)(2,1)S(1)}, u32[]{:S(2)}, u32[]{:S(2)}) async-start(bf16[16,8,6272]{2,1,0:T(8,128)(2,1)} %bitcast.8), calls=%async_computation.1 | async-start | bytes 3211264 | tf_op jit(solution)/shard_map/all_to_all | solution.py:439
  147.9 17.8 %copy-start.11 = (s32[1,128]{1,0:T(1,128)S(1)}, s32[1,128]{1,0:T(1,128)}, u32[]{:S(2)}) copy-start(s32[1,128]{1,0:T(1,128)} %get-tuple-element.20) | copy-start | bytes 1540
Sparse Core Ops, SparseCore 0:
  36.0 69.5 all-gather.2
  117.4 47.4 all-gather.4

commit v6 on v5

--- a/solution.py
+++ b/solution.py
@@ -51,34 +51,38 @@
     return spread.astype(BF16)
 
 
-def scaled_weights(gate_quant, gate_scale, up_quant, up_scale, down_quant, down_scale):
+def scaled_weights(gate_quant, gate_scale, up_quant, up_scale, down_quant, down_scale, which):
     part, units = gate_quant.shape
     half = part // 2
 
-    def body(gate, up, down, gate_s, up_s, down_s, first, second):
-        for i in range(part // BLOCK):
+    def body(gate, up, down, gate_s, up_s, down_s, out):
+        for i in range(half // BLOCK):
             rows = slice(i * BLOCK, (i + 1) * BLOCK)
-            out, at = (first, i * BLOCK) if i * BLOCK < half else (second, i * BLOCK - half)
+            at = which * half // BLOCK + i
             for j in range(units // BLOCK):
                 cols = slice(j * BLOCK, (j + 1) * BLOCK)
                 tiles = (
-                    gate[rows, cols].astype(F32) * gate_s[j, i],
-                    up[rows, cols].astype(F32) * up_s[j, i],
-                    (down[cols, rows].astype(F32) * down_s[j, i]).T,
+                    gate[rows, cols].astype(F32) * gate_s[j, at],
+                    up[rows, cols].astype(F32) * up_s[j, at],
+                    (down[cols, rows].astype(F32) * down_s[j, at]).T,
                 )
                 for k, tile in enumerate(tiles):
                     to = k * units + j * BLOCK
-                    out[at : at + BLOCK, to : to + BLOCK] = tile.astype(BF16)
-
-    quants, scales = [gate_quant, up_quant, down_quant], [gate_scale.T, up_scale.T, down_scale]
+                    out[rows, to : to + BLOCK] = tile.astype(BF16)
+
     shape = (half, 3 * units)
     return kernel_call(
         body,
-        (jax.ShapeDtypeStruct(shape, BF16),) * 2,
-        60,
-        in_specs=[whole(v.shape) for v in quants] + [pl.BlockSpec(memory_space=pltpu.SMEM)] * 3,
-        out_specs=(whole(shape),) * 2,
-    )(*quants, *scales)
+        jax.ShapeDtypeStruct(shape, BF16),
+        60,
+        in_specs=[
+            block_at((half, units), (which, 0)),
+            block_at((half, units), (which, 0)),
+            block_at((units, half), (0, which)),
+        ]
+        + [pl.BlockSpec(memory_space=pltpu.SMEM)] * 3,
+        out_specs=whole(shape),
+    )(gate_quant, up_quant, down_quant, gate_scale.T, up_scale.T, down_scale)
 
 
 def pre_sums(rows, width, first_parts, second_parts):
@@ -265,10 +269,10 @@
     )(packed, sides)
 
 
-def split_columns(rows, start, part, ring):
+def turned_columns(rows, start, part, ring):
     slots = rows.shape[0]
 
-    def body(rows_ref, features, weighted, sides, sems):
+    def body(rows_ref, out, sides, sems):
         copies = [
             pltpu.make_async_copy(
                 rows_ref.at[:, pl.ds(start + d * 2 * part, 2 * part)], sides.at[d], sems.at[d]
@@ -279,17 +283,15 @@
             copy.start()
         for d in range(ring):
             copies[d].wait()
-            at = slice(d * slots, (d + 1) * slots)
-            features[:, at] = sides[d, :, :part].astype(F32).T.astype(BF16)
-            weighted[at, :] = sides[d, :, part:]
-
-    shapes = ((part, ring * slots), (ring * slots, part))
-    return kernel_call(
-        body,
-        tuple(jax.ShapeDtypeStruct(v, BF16) for v in shapes),
+            out[:, d * slots : (d + 1) * slots] = sides[d].astype(F32).T.astype(BF16)
+
+    shape = (2 * part, ring * slots)
+    return kernel_call(
+        body,
+        jax.ShapeDtypeStruct(shape, BF16),
         60,
         in_specs=[far_memory()],
-        out_specs=tuple(whole(v) for v in shapes),
+        out_specs=whole(shape),
         scratch_shapes=[
             pltpu.VMEM((ring, slots, 2 * part), BF16),
             pltpu.SemaphoreType.DMA((ring,)),
@@ -297,24 +299,56 @@
     )(rows)
 
 
-def weight_sums(features, weighted, acts):
-    part, slots = features.shape
-    units = acts.shape[1] // 3
-
-    def body(x_ref, weighted_ref, acts_ref, gate_out, up_out, down_out):
-        gate_up = contract(x_ref[...], acts_ref[:, : 2 * units], 1, 0)
-        gate_out[...] = gate_up[:, :units]
-        up_out[...] = gate_up[:, units:]
-        down_out[...] = contract(acts_ref[:, 2 * units :], weighted_ref[...], 0, 0)
+def weight_sums(columns, acts):
+    twice, slots = columns.shape
+    part = twice // 2
+    wide = acts.shape[1]
+    units = wide // 3
+    both = 2 * units
+    steps = 4
+    span = slots // steps
+
+    def body(columns_ref, acts_ref, gate_out, up_out, down_out, cols_in, acts_in, sums, sems):
+        copies = []
+        for i in range(steps):
+            at = pl.ds(i * span, span)
+            copies.append(
+                (
+                    pltpu.make_async_copy(acts_ref.at[at], acts_in.at[i], sems.at[0, i]),
+                    pltpu.make_async_copy(columns_ref.at[:, at], cols_in.at[i], sems.at[1, i]),
+                )
+            )
+            for copy in copies[-1]:
+                copy.start()
+        for i in range(steps):
+            for copy in copies[i]:
+                copy.wait()
+            one = contract(cols_in[i, :part], acts_in[i, :, :both], 1, 0)
+            two = contract(cols_in[i, part:], acts_in[i, :, both:], 1, 0)
+            if i > 0:
+                one, two = sums[:, :both] + one, sums[:, both:] + two
+            if i < steps - 1:
+                sums[:, :both] = one
+                sums[:, both:] = two
+            else:
+                gate_out[...] = one[:, :units]
+                up_out[...] = one[:, units:]
+                down_out[...] = two.T
 
     shapes = ((part, units), (part, units), (units, part))
     return kernel_call(
         body,
         tuple(jax.ShapeDtypeStruct(v, F32) for v in shapes),
-        55,
-        in_specs=[whole(features.shape), whole(weighted.shape), whole(acts.shape)],
+        60,
+        in_specs=[far_memory()] * 2,
         out_specs=tuple(whole(v) for v in shapes),
-    )(features, weighted, acts)
+        scratch_shapes=[
+            pltpu.VMEM((steps, twice, span), BF16),
+            pltpu.VMEM((steps, span, wide), BF16),
+            pltpu.VMEM((part, wide), F32),
+            pltpu.SemaphoreType.DMA((2, steps)),
+        ],
+    )(columns, acts)
 
 
 def pick_slots(place, mask, prob, x_quant, x_scale, grad_out, ring):
@@ -414,8 +448,11 @@
         width = x_quant.shape[1]
         part = width // ring
 
-        first, second = scaled_weights(
-            gate_quant, gate_scale, up_quant, up_scale, down_quant, down_scale
+        first, second = (
+            scaled_weights(
+                gate_quant, gate_scale, up_quant, up_scale, down_quant, down_scale, which
+            )
+            for which in range(2)
         )
         first_near, first_far = ring_gather(first, "fsdp", ring, True)
         second_near, second_far = ring_gather(second, "fsdp", ring, False)
@@ -437,6 +474,10 @@
         got = lax.ppermute(give, "core", [(0, 1), (1, 0)])
         both = pair_sum(keep, got).reshape(-1, CAP, width + LANES)
         shares = lax.all_to_all(both, PLANE, split_axis=0, concat_axis=0, tiled=True)
+        grad_gate, grad_up, grad_down = weight_sums(
+            turned_columns(rows, 2 * width + LANES, part, ring), all_acts
+        )
+        shares, grad_up = lax.optimization_barrier((shares, grad_up))
         table = token_slot == jnp.arange(CAP, dtype=jnp.int32)[:, None]
         mine = jnp.sum(shares.astype(F32), axis=0)
         mine_grad = mine[:, :width].astype(BF16).reshape(CAP, ring, part)
@@ -445,9 +486,6 @@
         grad_x = contract(table.astype(BF16), mine_grad, 0, 0).astype(BF16)
         grad_prob = jnp.sum(jnp.where(table, mine_prob[:, None], 0.0), axis=0)
 
-        grad_gate, grad_up, grad_down = weight_sums(
-            *split_columns(rows, 2 * width + LANES, part, ring), all_acts
-        )
         return (grad_x, grad_prob, grad_gate, grad_up, grad_down)
 
     return on_device

time: 183 us -> 184 us (level)
  Pallas kernels: 40.8 us -> 42.8 us
    all_to_all x1, waiting for transfers between devices: 17 us -> 0.01 us  [on_device(): lax.all_to_all(both, PLANE, split_axis=0, concat_axis=0, tiled=True)]
    all_gather x1, waiting for transfers between devices: 0.01 us -> 16.4 us  [on_device(): all_acts = lax.all_gather(acts, 'fsdp', axis=0, tiled=True)]
    ppermute x1, waiting for transfers between devices: 1.49 us -> 3.76 us  [ring_gather(): lax.ppermute(ahead, axis, up)]
    all_gather x1, waiting for transfers between devices: 4.28 us -> 2.01 us  [on_device(): rows = lax.all_gather(joined(packed, sides), CORE_FIRST, axis=0, tiled=True)]
    pallas_call x2 -> x3, Pallas kernels: 8.21 us -> 10.4 us  [the longest x1 6.17 us: turned_columns(): kernel_call(body, jax.ShapeDtypeStruct(shape, BF16), 60, in_specs=[far_me...]
  transfers between devices with their start and end apart: 18 -> 18, of which waited for: 10 -> 10; matrix products, arithmetic and copies ran while one was open for 2% -> 0% of each run, Pallas kernels for 14% -> 19%
where the time goes in v6:
time: 184 us
  waiting for transfers between devices  73.7 us (40%)
  Pallas kernels  42.8 us (23%)
  starting transfers between devices  33.5 us (18%)
  between operations  14.2 us (8%)
  blocking collectives  14.1 us (8%)
  local copies, waits for them, and re-layouts  2.51 us (1%)
    ppermute x6, waiting for transfers between devices, ring_gather(): ahead = lax.ppermute(ahead, axis, up)  25.8 us
    ppermute x6, waiting for transfers between devices, ring_gather(): behind = lax.ppermute(behind, axis, down)  22.4 us
    all_gather x1, waiting for transfers between devices, on_device(): all_acts = lax.all_gather(acts, 'fsdp', axis=0, tiled=True)  16.4 us
    ppermute x6, starting transfers between devices, ring_gather(): behind = lax.ppermute(behind, axis, down)  14.5 us
    all_to_all x1, blocking collectives, on_device(): lax.all_to_all(sides, 'fsdp', split_axis=0, concat_axis=0, tiled=True)  14.1 us
    pallas_call x1, Pallas kernels, slot_sums(): kernel_call(body, (jax.ShapeDtypeStruct(shape, BF16),) * 2, 60, scalars=1...  7.81 us
    pallas_call x1, Pallas kernels, weight_sums(): kernel_call(body, tuple((jax.ShapeDtypeStruct(v, F32) for v in shapes)),...  6.98 us
    pallas_call x1, Pallas kernels, pre_sums(): kernel_call(body, jax.ShapeDtypeStruct(shape, F32), 60, in_specs=[far_mem...  6.83 us
  transfers between devices with their start and end apart: 18, of which 10 were waited for; matrix products, arithmetic and copies ran while one was open for 0% of the time, Pallas kernels for 19%

profile of v6, /device:TPU:1, one launch (start us, length us, event | category | flops | bytes accessed | tf_op | source)
XLA Modules:
  0.0 183.7 jit_solution(9146902674753054353)
XLA Ops:
  7.2 2.1 %shard_map.147.refs_0_ = bf16[384,768]{1,0:T(8,128)(2,1)} custom-call(bf16[768,256]{1,0:T(8,128)(2,1)} %gate.3, bf16[768,256]{1,0:T(8,128)(2,1)} %up.3, bf16[256,768]{1,0:T(8,128)(2,1)} %down.3, f32[2,6]{1,0:T(2,128)} %bitcast.17, f32[2,6]{1,0:T(2,128)} %bitcast.19, f32[2,6]{1,0:T(2,128)} %down_s.3), custom_call_target="tpu_custom_call" | custom-call | tf_op jit(solution)/shard_map/pallas_call | solution.py:74
  9.3 2.5 %collective-permute-start = (bf16[384,768]{1,0:T(8,128)(2,1)}, bf16[384,768]{1,0:T(8,128)(2,1)S(1)}, u32[]{:S(2)}, u32[]{:S(2)}) collective-permute-start(bf16[384,768]{1,0:T(8,128)(2,1)} %shard_map.147.refs_0_), channel_id=1, source_target_pairs={{0,32},{32,64},{64,96},{96,128},{128,160},{160,192},{192,224},{224... | collective-permute-start | bytes 1769480 | tf_op jit(solution)/shard_map/ppermute | solution.py:423
  11.8 3.9 %collective-permute-start.1 = (bf16[384,768]{1,0:T(8,128)(2,1)}, bf16[384,768]{1,0:T(8,128)(2,1)S(1)}, u32[]{:S(2)}, u32[]{:S(2)}) collective-permute-start(bf16[384,768]{1,0:T(8,128)(2,1)} %shard_map.147.refs_0_), channel_id=1, source_target_pairs={{0,224},{32,0},{64,32},{96,64},{128,96},{160,128},{192,160},{224,1... | collective-permute-start | bytes 1769480 | tf_op jit(solution)/shard_map/ppermute | solution.py:424
  15.8 3.4 %shard_map.146 = (bf16[8,12416]{1,0:T(8,128)(2,1)}, bf16[8,8,1536]{2,1,0:T(8,128)(2,1)}, s32[1,128]{1,0:T(1,128)}) custom-call(s32[1]{0:T(128)} %bitcast.place_ref, s32[1,128]{1,0:T(1,128)} %bitcast.21, bf16[1,128]{1,0:T(2,128)(2,1)} %bitcast.22, bf16[128,6144]{1,0:T(8,128)(2,1)} %x_ref.1, f32[48,128]{1,0:T(8,128)} %bitcast.16, bf16[128,6144]{1,0:T(8,128)(2,1)} %dy_ref.1), custom_call_target="tpu_custom_call" | custom-call | tf_op jit(solution)/shard_map/pallas_call | solution.py:398
  19.1 14.1 %all_to_all.10.sides_ref = bf16[8,8,1536]{2,1,0:T(8,128)(2,1)} all-to-all(bf16[8,8,1536]{2,1,0:T(8,128)(2,1)} %get-tuple-element.20), channel_id=1, replica_groups=mesh['fsdp'=8,'x'=4,'y'=4,'core'=2] {'fsdp'}, dimensions={0} | all-to-all | bytes 393216 | tf_op jit(solution)/shard_map/all_to_all | solution.py:463
  33.3 2.2 %shard_map.148 = bf16[8,24704]{1,0:T(8,128)(2,1)} custom-call(bf16[8,12416]{1,0:T(8,128)(2,1)} %get-tuple-element.19.packed_ref, bf16[8,8,1536]{2,1,0:T(8,128)(2,1)} %all_to_all.10.sides_ref), custom_call_target="tpu_custom_call" | custom-call | tf_op jit(solution)/shard_map/pallas_call | solution.py:263
  35.6 2.1 %shard_map.149.refs_7_.refs_8_ = bf16[384,768]{1,0:T(8,128)(2,1)} custom-call(bf16[768,256]{1,0:T(8,128)(2,1)} %gate.3, bf16[768,256]{1,0:T(8,128)(2,1)} %up.3, bf16[256,768]{1,0:T(8,128)(2,1)} %down.3, f32[2,6]{1,0:T(2,128)} %bitcast.18, f32[2,6]{1,0:T(2,128)} %bitcast.20, f32[2,6]{1,0:T(2,128)} %down_s.3), custom_call_target="tpu_custom_call" | custom-call | tf_op jit(solution)/shard_map/pallas_call | solution.py:74
  39.8 1.5 collective-permute-start.2
  41.3 8.9 %collective-permute-done.7.refs_9_.refs_10_ = bf16[384,768]{1,0:T(8,128)(2,1)S(1)} collective-permute-done((bf16[384,768]{1,0:T(8,128)(2,1)}, bf16[384,768]{1,0:T(8,128)(2,1)S(1)}, u32[]{:S(2)}, u32[]{:S(2)}) %collective-permute-start.7) | collective-permute-done | bytes 589856 | tf_op jit(solution)/shard_map/ppermute | solution.py:424
  50.2 2.6 %collective-permute-start.9 = (bf16[384,768]{1,0:T(8,128)(2,1)S(1)}, bf16[384,768]{1,0:T(8,128)(2,1)S(1)}, u32[]{:S(2)}, u32[]{:S(2)}) collective-permute-start(bf16[384,768]{1,0:T(8,128)(2,1)S(1)} %collective-permute-done.7.refs_9_.refs_10_), channel_id=1, source_target_pairs={{0,224},{32,0},{64,32},{96,64},{128,96},{160,128},{192,160},{224,1... | collective-permute-start | bytes 1769480 | tf_op jit(solution)/shard_map/ppermute | solution.py:424
  54.3 10.9 %collective-permute-done.2.refs_3_ = bf16[384,768]{1,0:T(8,128)(2,1)S(1)} collective-permute-done((bf16[384,768]{1,0:T(8,128)(2,1)S(1)}, bf16[384,768]{1,0:T(8,128)(2,1)S(1)}, u32[]{:S(2)}, u32[]{:S(2)}) %collective-permute-start.2) | collective-permute-done | bytes 589856 | tf_op jit(solution)/shard_map/ppermute | solution.py:423
  65.2 2.7 %collective-permute-start.11 = (bf16[384,768]{1,0:T(8,128)(2,1)S(1)}, bf16[384,768]{1,0:T(8,128)(2,1)}, u32[]{:S(2)}, u32[]{:S(2)}) collective-permute-start(bf16[384,768]{1,0:T(8,128)(2,1)S(1)} %collective-permute-done.9.refs_11_.refs_12_), channel_id=1, source_target_pairs={{0,224},{32,0},{64,32},{96,64},{128,96},{160,128},{192,160},{224,1... | collective-permute-start | bytes 1769480 | tf_op jit(solution)/shard_map/ppermute | solution.py:424
  67.9 6.8 %collective-permute-done.3.refs_4_ = bf16[384,768]{1,0:T(8,128)(2,1)S(1)} collective-permute-done((bf16[384,768]{1,0:T(8,128)(2,1)S(1)}, bf16[384,768]{1,0:T(8,128)(2,1)S(1)}, u32[]{:S(2)}, u32[]{:S(2)}) %collective-permute-start.3) | collective-permute-done | bytes 589856 | tf_op jit(solution)/shard_map/ppermute | solution.py:424
  74.6 3.4 %collective-permute-start.5 = (bf16[384,768]{1,0:T(8,128)(2,1)S(1)}, bf16[384,768]{1,0:T(8,128)(2,1)S(1)}, u32[]{:S(2)}, u32[]{:S(2)}) collective-permute-start(bf16[384,768]{1,0:T(8,128)(2,1)S(1)} %collective-permute-done.3.refs_4_), channel_id=1, source_target_pairs={{0,224},{32,0},{64,32},{96,64},{128,96},{160,128},{192,160},{224,1... | collective-permute-start | bytes 1769480 | tf_op jit(solution)/shard_map/ppermute | solution.py:424
  78.1 12.5 %collective-permute-done.4.refs_5_ = bf16[384,768]{1,0:T(8,128)(2,1)} collective-permute-done((bf16[384,768]{1,0:T(8,128)(2,1)S(1)}, bf16[384,768]{1,0:T(8,128)(2,1)}, u32[]{:S(2)}, u32[]{:S(2)}) %collective-permute-start.4) | collective-permute-done | bytes 589856 | tf_op jit(solution)/shard_map/ppermute | solution.py:423
  90.6 2.7 %collective-permute-start.13 = (bf16[384,768]{1,0:T(8,128)(2,1)}, bf16[384,768]{1,0:T(8,128)(2,1)}, u32[]{:S(2)}, u32[]{:S(2)}) collective-permute-start(bf16[384,768]{1,0:T(8,128)(2,1)} %collective-permute-done.11.refs_13_.refs_14_), channel_id=1, source_target_pairs={{0,224},{32,0},{64,32},{96,64},{128,96},{160,128},{192,160},{224,1... | collective-permute-start | bytes 1769480 | tf_op jit(solution)/shard_map/ppermute | solution.py:426
  93.3 6.7 %collective-permute-done.5.refs_6_ = bf16[384,768]{1,0:T(8,128)(2,1)S(1)} collective-permute-done((bf16[384,768]{1,0:T(8,128)(2,1)S(1)}, bf16[384,768]{1,0:T(8,128)(2,1)S(1)}, u32[]{:S(2)}, u32[]{:S(2)}) %collective-permute-start.5) | collective-permute-done | bytes 589856 | tf_op jit(solution)/shard_map/ppermute | solution.py:424
  100.8 2.4 %collective-permute-done.10.refs_12_.refs_13_ = bf16[384,768]{1,0:T(8,128)(2,1)} collective-permute-done((bf16[384,768]{1,0:T(8,128)(2,1)S(1)}, bf16[384,768]{1,0:T(8,128)(2,1)}, u32[]{:S(2)}, u32[]{:S(2)}) %collective-permute-start.10) | collective-permute-done | bytes 589856 | tf_op jit(solution)/shard_map/ppermute | solution.py:423
  103.2 2.0 %all-gather.3.cloned.1.call-done.rows_ref.x_ref.dy_ref.prob_ref = bf16[256,24704]{1,0:T(8,128)(2,1)} async-done(((bf16[8,24704]{1,0:T(8,128)(2,1)}), bf16[256,24704]{1,0:T(8,128)(2,1)}) %all-gather.3.cloned.1.call-update) | async-done | bytes 12648464 | tf_op jit(solution)/shard_map/all_gather | solution.py:465
  105.3 6.8 %shard_map.150.sums_ref = f32[256,768]{1,0:T(8,128)} custom-call(bf16[256,24704]{1,0:T(8,128)(2,1)} %all-gather.3.cloned.1.call-done.rows_ref.x_ref.dy_ref.prob_ref, bf16[384,768]{1,0:T(8,128)(2,1)} %shard_map.147.refs_0_, bf16[384,768]{1,0:T(8,128)(2,1)} %copy-done.1, bf16[384,768]{1,0:T(8,128)(2,1)} %copy-done.2, bf16[384,768]{1,0:T(8,128)(2,1)} %copy-done.5, ...), custom_call_target="tpu_custom_call" | custom-call | tf_op jit(solution)/shard_map/pallas_call | solution.py:128
  112.1 3.8 %collective-permute-done.12.first_ref.refs_7_ = bf16[384,768]{1,0:T(8,128)(2,1)} collective-permute-done((bf16[384,768]{1,0:T(8,128)(2,1)}, bf16[384,768]{1,0:T(8,128)(2,1)}, u32[]{:S(2)}, u32[]{:S(2)}) %collective-permute-start.12) | collective-permute-done | bytes 589856 | tf_op jit(solution)/shard_map/ppermute | solution.py:426
  115.9 3.2 %shard_map.151 = (bf16[256,768]{1,0:T(8,128)(2,1)}, bf16[256,128]{1,0:T(8,128)(2,1)}) custom-call(bf16[256,24704]{1,0:T(8,128)(2,1)} %all-gather.3.cloned.1.call-done.rows_ref.x_ref.dy_ref.prob_ref, bf16[256,24704]{1,0:T(8,128)(2,1)} %all-gather.3.cloned.1.call-done.rows_ref.x_ref.dy_ref.prob_ref, ...), custom_call_target="tpu_custom_call" | custom-call | tf_op jit(solution)/shard_map/pallas_call | solution.py:169
  119.1 7.8 %shard_map.152 = (bf16[128,6272]{1,0:T(8,128)(2,1)}, bf16[128,6272]{1,0:T(8,128)(2,1)}) custom-call(s32[1]{0:T(128)} %bitcast.5.core_ref, bf16[256,768]{1,0:T(8,128)(2,1)} %get-tuple-element.22.acts_ref, bf16[256,128]{1,0:T(8,128)(2,1)} %get-tuple-element.23.prob_ref, bf16[384,768]{1,0:T(8,128)(2,1)} %shard_map.147.refs_0_, bf16[384,768]{1,0:T(8,128)(2,1)} %copy-done.1, ...), custom_call_target="tpu_custom_call" | custom-call | tf_op jit(solution)/shard_map/pallas_call | solution.py:220
  126.9 3.8 %collective-permute-start.14 = (bf16[128,6272]{1,0:T(8,128)(2,1)}, bf16[128,6272]{1,0:T(8,128)(2,1)S(1)}, u32[]{:S(2)}, u32[]{:S(2)}) collective-permute-start(bf16[128,6272]{1,0:T(8,128)(2,1)} %get-tuple-element.25), channel_id=1, source_target_pairs={{0,1},{1,0},{2,3},{3,2},{4,5},{5,4},{6,7},{7,6},{8,9},{9,8},{10,11... | collective-permute-start | bytes 4816904 | tf_op jit(solution)/shard_map/ppermute | solution.py:474
  130.8 3.3 %collective-permute-done.14.b_ref = bf16[128,6272]{1,0:T(8,128)(2,1)S(1)} collective-permute-done((bf16[128,6272]{1,0:T(8,128)(2,1)}, bf16[128,6272]{1,0:T(8,128)(2,1)S(1)}, u32[]{:S(2)}, u32[]{:S(2)}) %collective-permute-start.14) | collective-permute-done | bytes 1605664 | tf_op jit(solution)/shard_map/ppermute | solution.py:474
  134.1 1.4 copy-done
  135.5 1.9 %shard_map.153 = bf16[128,6272]{1,0:T(8,128)(2,1)} custom-call(bf16[128,6272]{1,0:T(8,128)(2,1)S(1)} %copy-done, bf16[128,6272]{1,0:T(8,128)(2,1)S(1)} %collective-permute-done.14.b_ref), custom_call_target="tpu_custom_call" | custom-call | tf_op jit(solution)/shard_map/pallas_call | solution.py:244
  137.4 6.8 %all-to-all-start.1 = ((bf16[16,8,6272]{2,1,0:T(8,128)(2,1)}), bf16[16,8,6272]{2,1,0:T(8,128)(2,1)S(1)}, u32[]{:S(2)}, u32[]{:S(2)}) async-start(bf16[16,8,6272]{2,1,0:T(8,128)(2,1)} %bitcast.8), calls=%async_computation.1 | async-start | bytes 3211264 | tf_op jit(solution)/shard_map/all_to_all | solution.py:476
  144.1 6.2 %shard_map.154.columns_ref = bf16[1536,2048]{1,0:T(8,128)(2,1)} custom-call(bf16[256,24704]{1,0:T(8,128)(2,1)} %all-gather.3.cloned.1.call-done.rows_ref.x_ref.dy_ref.prob_ref), custom_call_target="tpu_custom_call" | custom-call | tf_op jit(solution)/shard_map/pallas_call | solution.py:289
  150.3 16.4 %all-gather.5.cloned.1.call-done.acts_ref = bf16[2048,768]{1,0:T(8,128)(2,1)} async-done(((bf16[256,768]{1,0:T(8,128)(2,1)}), bf16[2048,768]{1,0:T(8,128)(2,1)}) %all-gather.5.cloned.1.call-update) | async-done | bytes 3145744 | tf_op jit(solution)/shard_map/all_gather | solution.py:469
  166.7 7.0 %shard_map.155 = (f32[768,256]{1,0:T(8,128)}, f32[768,256]{1,0:T(8,128)}, f32[256,768]{1,0:T(8,128)}) custom-call(bf16[1536,2048]{1,0:T(8,128)(2,1)} %shard_map.154.columns_ref, bf16[2048,768]{1,0:T(8,128)(2,1)} %all-gather.5.cloned.1.call-done.acts_ref), custom_call_target="tpu_custom_call" | custom-call | tf_op jit(solution)/shard_map/pallas_call | solution.py:339
  174.5 1.8 convolution_convert_fusion
  (48 shorter events, 5.9 us)
Async XLA Ops:
  7.2 98.1 %all-gather.3.cloned.1.call-start = ((), (), s32[]{:S(2)}) async-start(), calls=%async_computation.2 | async-start | bytes 13043712 | tf_op jit(solution)/shard_map/all_gather | solution.py:465
  9.3 23.9 %collective-permute-start = (bf16[384,768]{1,0:T(8,128)(2,1)}, bf16[384,768]{1,0:T(8,128)(2,1)S(1)}, u32[]{:S(2)}, u32[]{:S(2)}) collective-permute-start(bf16[384,768]{1,0:T(8,128)(2,1)} %shard_map.147.refs_0_), channel_id=1, source_target_pairs={{0,32},{32,64},{64,96},{96,128},{128,160},{160,192},{192,224},{224... | collective-permute-start | bytes 1769480 | tf_op jit(solution)/shard_map/ppermute | solution.py:423
  11.8 21.4 %collective-permute-start.1 = (bf16[384,768]{1,0:T(8,128)(2,1)}, bf16[384,768]{1,0:T(8,128)(2,1)S(1)}, u32[]{:S(2)}, u32[]{:S(2)}) collective-permute-start(bf16[384,768]{1,0:T(8,128)(2,1)} %shard_map.147.refs_0_), channel_id=1, source_target_pairs={{0,224},{32,0},{64,32},{96,64},{128,96},{160,128},{192,160},{224,1... | collective-permute-start | bytes 1769480 | tf_op jit(solution)/shard_map/ppermute | solution.py:424
  33.2 72.0 %copy-start.1 = (bf16[384,768]{1,0:T(8,128)(2,1)}, bf16[384,768]{1,0:T(8,128)(2,1)S(1)}, u32[]{:S(2)}) copy-start(bf16[384,768]{1,0:T(8,128)(2,1)S(1)} %collective-permute-done.refs_1_) | copy-start | bytes 1769476
  33.3 72.0 %copy-start.2 = (bf16[384,768]{1,0:T(8,128)(2,1)}, bf16[384,768]{1,0:T(8,128)(2,1)S(1)}, u32[]{:S(2)}) copy-start(bf16[384,768]{1,0:T(8,128)(2,1)S(1)} %collective-permute-done.1.refs_2_) | copy-start | bytes 1769476
  35.5 131.2 %all-gather.5.cloned.1.call-start = ((), (), s32[]{:S(2)}) async-start(), calls=%async_computation.3 | async-start | bytes 3538944 | tf_op jit(solution)/shard_map/all_gather | solution.py:469
  37.7 12.5 %collective-permute-start.7 = (bf16[384,768]{1,0:T(8,128)(2,1)}, bf16[384,768]{1,0:T(8,128)(2,1)S(1)}, u32[]{:S(2)}, u32[]{:S(2)}) collective-permute-start(bf16[384,768]{1,0:T(8,128)(2,1)} %shard_map.149.refs_7_.refs_8_), channel_id=1, source_target_pairs={{0,224},{32,0},{64,32},{96,64},{128,96},{160,128},{192,160},{224,1... | collective-permute-start | bytes 1769480 | tf_op jit(solution)/shard_map/ppermute | solution.py:424
  39.1 14.1 %collective-permute-start.6 = (bf16[384,768]{1,0:T(8,128)(2,1)}, bf16[384,768]{1,0:T(8,128)(2,1)S(1)}, u32[]{:S(2)}, u32[]{:S(2)}) collective-permute-start(bf16[384,768]{1,0:T(8,128)(2,1)} %shard_map.149.refs_7_.refs_8_), channel_id=1, source_target_pairs={{0,32},{32,64},{64,96},{96,128},{128,160},{160,192},{192,224},{224... | collective-permute-start | bytes 1769480 | tf_op jit(solution)/shard_map/ppermute | solution.py:423
  39.8 25.4 %collective-permute-start.2 = (bf16[384,768]{1,0:T(8,128)(2,1)S(1)}, bf16[384,768]{1,0:T(8,128)(2,1)S(1)}, u32[]{:S(2)}, u32[]{:S(2)}) collective-permute-start(bf16[384,768]{1,0:T(8,128)(2,1)S(1)} %collective-permute-done.refs_1_), channel_id=1, source_target_pairs={{0,32},{32,64},{64,96},{96,128},{128,160},{160,192},{192,224},{224... | collective-permute-start | bytes 1769480 | tf_op jit(solution)/shard_map/ppermute | solution.py:423
  50.2 55.0 %copy-start.3 = (bf16[384,768]{1,0:T(8,128)(2,1)}, bf16[384,768]{1,0:T(8,128)(2,1)S(1)}, u32[]{:S(2)}) copy-start(bf16[384,768]{1,0:T(8,128)(2,1)S(1)} %collective-permute-done.7.refs_9_.refs_10_) | copy-start | bytes 1769476
  50.2 15.0 %collective-permute-start.9 = (bf16[384,768]{1,0:T(8,128)(2,1)S(1)}, bf16[384,768]{1,0:T(8,128)(2,1)S(1)}, u32[]{:S(2)}, u32[]{:S(2)}) collective-permute-start(bf16[384,768]{1,0:T(8,128)(2,1)S(1)} %collective-permute-done.7.refs_9_.refs_10_), channel_id=1, source_target_pairs={{0,224},{32,0},{64,32},{96,64},{128,96},{160,128},{192,160},{224,1... | collective-permute-start | bytes 1769480 | tf_op jit(solution)/shard_map/ppermute | solution.py:424
  52.8 21.8 %collective-permute-start.3 = (bf16[384,768]{1,0:T(8,128)(2,1)S(1)}, bf16[384,768]{1,0:T(8,128)(2,1)S(1)}, u32[]{:S(2)}, u32[]{:S(2)}) collective-permute-start(bf16[384,768]{1,0:T(8,128)(2,1)S(1)} %collective-permute-done.1.refs_2_), channel_id=1, source_target_pairs={{0,224},{32,0},{64,32},{96,64},{128,96},{160,128},{192,160},{224,1... | collective-permute-start | bytes 1769480 | tf_op jit(solution)/shard_map/ppermute | solution.py:424
  53.2 52.0 %copy-start.4 = (bf16[384,768]{1,0:T(8,128)(2,1)}, bf16[384,768]{1,0:T(8,128)(2,1)S(1)}, u32[]{:S(2)}) copy-start(bf16[384,768]{1,0:T(8,128)(2,1)S(1)} %collective-permute-done.6.refs_8_.refs_9_) | copy-start | bytes 1769476
  53.2 24.8 %collective-permute-start.8 = (bf16[384,768]{1,0:T(8,128)(2,1)S(1)}, bf16[384,768]{1,0:T(8,128)(2,1)S(1)}, u32[]{:S(2)}, u32[]{:S(2)}) collective-permute-start(bf16[384,768]{1,0:T(8,128)(2,1)S(1)} %collective-permute-done.6.refs_8_.refs_9_), channel_id=1, source_target_pairs={{0,32},{32,64},{64,96},{96,128},{128,160},{160,192},{192,224},{224... | collective-permute-start | bytes 1769480 | tf_op jit(solution)/shard_map/ppermute | solution.py:423
  65.2 40.1 %copy-start.5 = (bf16[384,768]{1,0:T(8,128)(2,1)}, bf16[384,768]{1,0:T(8,128)(2,1)S(1)}, u32[]{:S(2)}) copy-start(bf16[384,768]{1,0:T(8,128)(2,1)S(1)} %collective-permute-done.2.refs_3_) | copy-start | bytes 1769476
  65.2 25.4 %collective-permute-start.4 = (bf16[384,768]{1,0:T(8,128)(2,1)S(1)}, bf16[384,768]{1,0:T(8,128)(2,1)}, u32[]{:S(2)}, u32[]{:S(2)}) collective-permute-start(bf16[384,768]{1,0:T(8,128)(2,1)S(1)} %collective-permute-done.2.refs_3_), channel_id=1, source_target_pairs={{0,32},{32,64},{64,96},{96,128},{128,160},{160,192},{192,224},{224... | collective-permute-start | bytes 1769480 | tf_op jit(solution)/shard_map/ppermute | solution.py:423
  65.2 40.1 %copy-start.6 = (bf16[384,768]{1,0:T(8,128)(2,1)}, bf16[384,768]{1,0:T(8,128)(2,1)S(1)}, u32[]{:S(2)}) copy-start(bf16[384,768]{1,0:T(8,128)(2,1)S(1)} %collective-permute-done.9.refs_11_.refs_12_) | copy-start | bytes 1769476
  65.2 25.4 %collective-permute-start.11 = (bf16[384,768]{1,0:T(8,128)(2,1)S(1)}, bf16[384,768]{1,0:T(8,128)(2,1)}, u32[]{:S(2)}, u32[]{:S(2)}) collective-permute-start(bf16[384,768]{1,0:T(8,128)(2,1)S(1)} %collective-permute-done.9.refs_11_.refs_12_), channel_id=1, source_target_pairs={{0,224},{32,0},{64,32},{96,64},{128,96},{160,128},{192,160},{224,1... | collective-permute-start | bytes 1769480 | tf_op jit(solution)/shard_map/ppermute | solution.py:424
  74.6 15.9 %copy-start.7 = (bf16[384,768]{1,0:T(8,128)(2,1)}, bf16[384,768]{1,0:T(8,128)(2,1)S(1)}, u32[]{:S(2)}) copy-start(bf16[384,768]{1,0:T(8,128)(2,1)S(1)} %collective-permute-done.3.refs_4_) | copy-start | bytes 1769476
  74.6 25.4 %collective-permute-start.5 = (bf16[384,768]{1,0:T(8,128)(2,1)S(1)}, bf16[384,768]{1,0:T(8,128)(2,1)S(1)}, u32[]{:S(2)}, u32[]{:S(2)}) collective-permute-start(bf16[384,768]{1,0:T(8,128)(2,1)S(1)} %collective-permute-done.3.refs_4_), channel_id=1, source_target_pairs={{0,224},{32,0},{64,32},{96,64},{128,96},{160,128},{192,160},{224,1... | collective-permute-start | bytes 1769480 | tf_op jit(solution)/shard_map/ppermute | solution.py:424
  78.0 21.9 %copy-start.8 = (bf16[384,768]{1,0:T(8,128)(2,1)}, bf16[384,768]{1,0:T(8,128)(2,1)S(1)}, u32[]{:S(2)}) copy-start(bf16[384,768]{1,0:T(8,128)(2,1)S(1)} %collective-permute-done.8.refs_10_.refs_11_) | copy-start | bytes 1769476
  78.1 25.2 %collective-permute-start.10 = (bf16[384,768]{1,0:T(8,128)(2,1)S(1)}, bf16[384,768]{1,0:T(8,128)(2,1)}, u32[]{:S(2)}, u32[]{:S(2)}) collective-permute-start(bf16[384,768]{1,0:T(8,128)(2,1)S(1)} %collective-permute-done.8.refs_10_.refs_11_), channel_id=1, source_target_pairs={{0,32},{32,64},{64,96},{96,128},{128,160},{160,192},{192,224},{224... | collective-permute-start | bytes 1769480 | tf_op jit(solution)/shard_map/ppermute | solution.py:423
  90.6 25.3 %collective-permute-start.12 = (bf16[384,768]{1,0:T(8,128)(2,1)}, bf16[384,768]{1,0:T(8,128)(2,1)}, u32[]{:S(2)}, u32[]{:S(2)}) collective-permute-start(bf16[384,768]{1,0:T(8,128)(2,1)} %collective-permute-done.4.refs_5_), channel_id=1, source_target_pairs={{0,32},{32,64},{64,96},{96,128},{128,160},{160,192},{192,224},{224... | collective-permute-start | bytes 1769480 | tf_op jit(solution)/shard_map/ppermute | solution.py:426
  90.6 25.3 %collective-permute-start.13 = (bf16[384,768]{1,0:T(8,128)(2,1)}, bf16[384,768]{1,0:T(8,128)(2,1)}, u32[]{:S(2)}, u32[]{:S(2)}) collective-permute-start(bf16[384,768]{1,0:T(8,128)(2,1)} %collective-permute-done.11.refs_13_.refs_14_), channel_id=1, source_target_pairs={{0,224},{32,0},{64,32},{96,64},{128,96},{160,128},{192,160},{224,1... | collective-permute-start | bytes 1769480 | tf_op jit(solution)/shard_map/ppermute | solution.py:426
  100.0 0.8 copy-start.9
  126.9 7.1 %collective-permute-start.14 = (bf16[128,6272]{1,0:T(8,128)(2,1)}, bf16[128,6272]{1,0:T(8,128)(2,1)S(1)}, u32[]{:S(2)}, u32[]{:S(2)}) collective-permute-start(bf16[128,6272]{1,0:T(8,128)(2,1)} %get-tuple-element.25), channel_id=1, source_target_pairs={{0,1},{1,0},{2,3},{3,2},{4,5},{5,4},{6,7},{7,6},{8,9},{9,8},{10,11... | collective-permute-start | bytes 4816904 | tf_op jit(solution)/shard_map/ppermute | solution.py:474
  134.1 1.4 copy-start
  137.4 36.3 %all-to-all-start.1 = ((bf16[16,8,6272]{2,1,0:T(8,128)(2,1)}), bf16[16,8,6272]{2,1,0:T(8,128)(2,1)S(1)}, u32[]{:S(2)}, u32[]{:S(2)}) async-start(bf16[16,8,6272]{2,1,0:T(8,128)(2,1)} %bitcast.8), calls=%async_computation.1 | async-start | bytes 3211264 | tf_op jit(solution)/shard_map/all_to_all | solution.py:476
  173.7 0.8 copy-start.10
Sparse Core Ops, SparseCore 0:
  35.6 69.5 all-gather.2
  119.2 47.4 all-gather.4

commit v7 on v6

--- a/solution.py
+++ b/solution.py
@@ -51,38 +51,34 @@
     return spread.astype(BF16)
 
 
-def scaled_weights(gate_quant, gate_scale, up_quant, up_scale, down_quant, down_scale, which):
+def scaled_weights(gate_quant, gate_scale, up_quant, up_scale, down_quant, down_scale):
     part, units = gate_quant.shape
     half = part // 2
 
-    def body(gate, up, down, gate_s, up_s, down_s, out):
-        for i in range(half // BLOCK):
+    def body(gate, up, down, gate_s, up_s, down_s, first, second):
+        for i in range(part // BLOCK):
             rows = slice(i * BLOCK, (i + 1) * BLOCK)
-            at = which * half // BLOCK + i
+            out, at = (first, i * BLOCK) if i * BLOCK < half else (second, i * BLOCK - half)
             for j in range(units // BLOCK):
                 cols = slice(j * BLOCK, (j + 1) * BLOCK)
                 tiles = (
-                    gate[rows, cols].astype(F32) * gate_s[j, at],
-                    up[rows, cols].astype(F32) * up_s[j, at],
-                    (down[cols, rows].astype(F32) * down_s[j, at]).T,
+                    gate[rows, cols].astype(F32) * gate_s[j, i],
+                    up[rows, cols].astype(F32) * up_s[j, i],
+                    (down[cols, rows].astype(F32) * down_s[j, i]).T,
                 )
                 for k, tile in enumerate(tiles):
                     to = k * units + j * BLOCK
-                    out[rows, to : to + BLOCK] = tile.astype(BF16)
-
+                    out[at : at + BLOCK, to : to + BLOCK] = tile.astype(BF16)
+
+    quants, scales = [gate_quant, up_quant, down_quant], [gate_scale.T, up_scale.T, down_scale]
     shape = (half, 3 * units)
     return kernel_call(
         body,
-        jax.ShapeDtypeStruct(shape, BF16),
-        60,
-        in_specs=[
-            block_at((half, units), (which, 0)),
-            block_at((half, units), (which, 0)),
-            block_at((units, half), (0, which)),
-        ]
-        + [pl.BlockSpec(memory_space=pltpu.SMEM)] * 3,
-        out_specs=whole(shape),
-    )(gate_quant, up_quant, down_quant, gate_scale.T, up_scale.T, down_scale)
+        (jax.ShapeDtypeStruct(shape, BF16),) * 2,
+        60,
+        in_specs=[whole(v.shape) for v in quants] + [pl.BlockSpec(memory_space=pltpu.SMEM)] * 3,
+        out_specs=(whole(shape),) * 2,
+    )(*quants, *scales)
 
 
 def pre_sums(rows, width, first_parts, second_parts):
@@ -188,8 +184,8 @@
     half, wide = first_parts[0][1].shape
     part, both = 2 * half, wide // 3 * 2
     width = count * part
-    places = [r for r, _ in first_parts]
-    assert places == [r for r, _ in second_parts]
+    first_parts = sorted(first_parts, key=lambda p: p[0])
+    second_parts = sorted(second_parts, key=lambda p: p[0])
 
     def body(core_ref, acts_ref, prob_ref, *refs):
         weights, give, keep, weights_in, sems = refs[: 2 * count], *refs[2 * count :]
@@ -206,12 +202,20 @@
         theirs = pl.ds(pl.multiple_of((1 - core_ref[0]) * rows_half, rows_half), rows_half)
         mine = pl.ds(pl.multiple_of(core_ref[0] * rows_half, rows_half), rows_half)
         acts = jnp.concatenate([acts_ref[theirs, :both], acts_ref[mine, :both]], axis=0)
-        for i, r in enumerate(places):
-            copies[2 * i].wait()
-            copies[2 * i + 1].wait()
+
+        def step(i, carry):
+            for k in range(2):
+                rows = pl.ds(k * half, half)
+                pltpu.make_async_copy(
+                    weights[0].at[:, pl.ds(0, both)], weights_in.at[i, rows], sems.at[k, i]
+                ).wait()
             sums = contract(acts, weights_in[i], 1, 1).astype(BF16)
-            give[:, r * part : (r + 1) * part] = sums[:rows_half]
-            keep[:, r * part : (r + 1) * part] = sums[rows_half:]
+            cols = pl.ds(pl.multiple_of(i * part, BLOCK), part)
+            give[:, cols] = sums[:rows_half]
+            keep[:, cols] = sums[rows_half:]
+            return carry
+
+        lax.fori_loop(0, count, step, 0)
         give[:, width:] = prob_ref[theirs, :]
         keep[:, width:] = prob_ref[mine, :]
 
@@ -320,20 +324,20 @@
             )
             for copy in copies[-1]:
                 copy.start()
-        for i in range(steps):
-            for copy in copies[i]:
-                copy.wait()
-            one = contract(cols_in[i, :part], acts_in[i, :, :both], 1, 0)
-            two = contract(cols_in[i, part:], acts_in[i, :, both:], 1, 0)
-            if i > 0:
-                one, two = sums[:, :both] + one, sums[:, both:] + two
-            if i < steps - 1:
-                sums[:, :both] = one
-                sums[:, both:] = two
-            else:
-                gate_out[...] = one[:, :units]
-                up_out[...] = one[:, units:]
-                down_out[...] = two.T
+        sums[...] = jnp.zeros_like(sums)
+
+        def step(i, carry):
+            at = pl.ds(0, span)
+            pltpu.make_async_copy(acts_ref.at[at], acts_in.at[i], sems.at[0, i]).wait()
+            pltpu.make_async_copy(columns_ref.at[:, at], cols_in.at[i], sems.at[1, i]).wait()
+            sums[:, :both] += contract(cols_in[i, :part], acts_in[i, :, :both], 1, 0)
+            sums[:, both:] += contract(cols_in[i, part:], acts_in[i, :, both:], 1, 0)
+            return carry
+
+        lax.fori_loop(0, steps, step, 0)
+        gate_out[...] = sums[:, :units]
+        up_out[...] = sums[:, units:both]
+        down_out[...] = sums[:, both:].T
 
     shapes = ((part, units), (part, units), (units, part))
     return kernel_call(
@@ -448,11 +452,8 @@
         width = x_quant.shape[1]
         part = width // ring
 
-        first, second = (
-            scaled_weights(
-                gate_quant, gate_scale, up_quant, up_scale, down_quant, down_scale, which
-            )
-            for which in range(2)
+        first, second = scaled_weights(
+            gate_quant, gate_scale, up_quant, up_scale, down_quant, down_scale
         )
         first_near, first_far = ring_gather(first, "fsdp", ring, True)
         second_near, second_far = ring_gather(second, "fsdp", ring, False)

time: 184 us -> 182 us (0.989)
  Pallas kernels: 42.8 us -> 40.1 us
    ppermute x1, waiting for transfers between devices: 3.76 us -> 1.49 us  [ring_gather(): lax.ppermute(ahead, axis, up)]
    all_gather x1, waiting for transfers between devices: 2.01 us -> 4.28 us  [on_device(): rows = lax.all_gather(joined(packed, sides), CORE_FIRST, axis=0, tiled=True)]
    pallas_call x2 -> x1, Pallas kernels: 4.28 us -> 2.49 us  [scaled_weights(): kernel_call(body, (jax.ShapeDtypeStruct(shape, BF16),) * 2, 60, in_specs=...]
  transfers between devices with their start and end apart: 18 -> 18, of which waited for: 10 -> 10; matrix products, arithmetic and copies ran while one was open for 0% -> 0% of each run, Pallas kernels for 19% -> 18%
where the time goes in v7:
time: 182 us; the launch traced here: 181 us
  waiting for transfers between devices  74 us (41%)
  Pallas kernels  40.1 us (22%)
  starting transfers between devices  33.6 us (18%)
  between operations  14.2 us (8%)
  blocking collectives  14.1 us (8%)
  local copies, waits for them, and re-layouts  2.54 us (1%)
    ppermute x6, waiting for transfers between devices, ring_gather(): ahead = lax.ppermute(ahead, axis, up)  25.9 us
    ppermute x6, waiting for transfers between devices, ring_gather(): behind = lax.ppermute(behind, axis, down)  22 us
    all_gather x1, waiting for transfers between devices, on_device(): all_acts = lax.all_gather(acts, 'fsdp', axis=0, tiled=True)  16.9 us
    ppermute x6, starting transfers between devices, ring_gather(): behind = lax.ppermute(behind, axis, down)  14.6 us
    all_to_all x1, blocking collectives, on_device(): lax.all_to_all(sides, 'fsdp', split_axis=0, concat_axis=0, tiled=True)  14.1 us
    pallas_call x1, Pallas kernels, slot_sums(): kernel_call(body, (jax.ShapeDtypeStruct(shape, BF16),) * 2, 60, scalars=1...  7.35 us
    pallas_call x1, Pallas kernels, pre_sums(): kernel_call(body, jax.ShapeDtypeStruct(shape, F32), 60, in_specs=[far_mem...  6.83 us
    all_to_all x1, starting transfers between devices, on_device(): lax.all_to_all(both, PLANE, split_axis=0, concat_axis=0, tiled=True)  6.74 us
  transfers between devices with their start and end apart: 18, of which 10 were waited for; matrix products, arithmetic and copies ran while one was open for 0% of the time, Pallas kernels for 18%

profile of v7, /device:TPU:1, one launch (start us, length us, event | category | flops | bytes accessed | tf_op | source)
XLA Modules:
  0.0 181.3 jit_solution(13233327679059185648)
XLA Ops:
  7.2 2.5 %shard_map.147 = (bf16[384,768]{1,0:T(8,128)(2,1)}, bf16[384,768]{1,0:T(8,128)(2,1)}) custom-call(bf16[768,256]{1,0:T(8,128)(2,1)} %gate.1, bf16[768,256]{1,0:T(8,128)(2,1)} %up.1, bf16[256,768]{1,0:T(8,128)(2,1)} %down.1, f32[2,6]{1,0:T(2,128)} %bitcast.17, f32[2,6]{1,0:T(2,128)} %bitcast.18, f32[2,6]{1,0:T(2,128)} %down_s.1), custom_call_target="tpu_custom_call" | custom-call | tf_op jit(solution)/shard_map/pallas_call | solution.py:75
  9.7 2.5 %collective-permute-start = (bf16[384,768]{1,0:T(8,128)(2,1)}, bf16[384,768]{1,0:T(8,128)(2,1)S(1)}, u32[]{:S(2)}, u32[]{:S(2)}) collective-permute-start(bf16[384,768]{1,0:T(8,128)(2,1)} %get-tuple-element.23.refs_0_), channel_id=1, source_target_pairs={{0,32},{32,64},{64,96},{96,128},{128,160},{160,192},{192,224},{224... | collective-permute-start | bytes 1769480 | tf_op jit(solution)/shard_map/ppermute | solution.py:427
  12.2 3.9 %collective-permute-start.1 = (bf16[384,768]{1,0:T(8,128)(2,1)}, bf16[384,768]{1,0:T(8,128)(2,1)S(1)}, u32[]{:S(2)}, u32[]{:S(2)}) collective-permute-start(bf16[384,768]{1,0:T(8,128)(2,1)} %get-tuple-element.23.refs_0_), channel_id=1, source_target_pairs={{0,224},{32,0},{64,32},{96,64},{128,96},{160,128},{192,160},{224,1... | collective-permute-start | bytes 1769480 | tf_op jit(solution)/shard_map/ppermute | solution.py:428
  16.1 3.4 %shard_map.146 = (bf16[8,12416]{1,0:T(8,128)(2,1)}, bf16[8,8,1536]{2,1,0:T(8,128)(2,1)}, s32[1,128]{1,0:T(1,128)}) custom-call(s32[1]{0:T(128)} %bitcast.place_ref, s32[1,128]{1,0:T(1,128)} %bitcast.19, bf16[1,128]{1,0:T(2,128)(2,1)} %bitcast.20, bf16[128,6144]{1,0:T(8,128)(2,1)} %x_ref.1, f32[48,128]{1,0:T(8,128)} %bitcast.16, bf16[128,6144]{1,0:T(8,128)(2,1)} %dy_ref.1), custom_call_target="tpu_custom_call" | custom-call | tf_op jit(solution)/shard_map/pallas_call | solution.py:402
  19.6 14.1 %all_to_all.10.sides_ref = bf16[8,8,1536]{2,1,0:T(8,128)(2,1)} all-to-all(bf16[8,8,1536]{2,1,0:T(8,128)(2,1)} %get-tuple-element.22), channel_id=1, replica_groups=mesh['fsdp'=8,'x'=4,'y'=4,'core'=2] {'fsdp'}, dimensions={0} | all-to-all | bytes 393216 | tf_op jit(solution)/shard_map/all_to_all | solution.py:464
  33.6 2.2 %shard_map.148 = bf16[8,24704]{1,0:T(8,128)(2,1)} custom-call(bf16[8,12416]{1,0:T(8,128)(2,1)} %get-tuple-element.21.packed_ref, bf16[8,8,1536]{2,1,0:T(8,128)(2,1)} %all_to_all.10.sides_ref), custom_call_target="tpu_custom_call" | custom-call | tf_op jit(solution)/shard_map/pallas_call | solution.py:267
  35.9 1.5 collective-permute-start.7
  38.2 1.4 collective-permute-start.2
  39.6 8.7 %collective-permute-done.7.refs_9_.refs_15_ = bf16[384,768]{1,0:T(8,128)(2,1)S(1)} collective-permute-done((bf16[384,768]{1,0:T(8,128)(2,1)S(1)}, bf16[384,768]{1,0:T(8,128)(2,1)S(1)}, u32[]{:S(2)}, u32[]{:S(2)}) %collective-permute-start.7) | collective-permute-done | bytes 589856 | tf_op jit(solution)/shard_map/ppermute | solution.py:428
  48.2 2.7 %collective-permute-start.9 = (bf16[384,768]{1,0:T(8,128)(2,1)S(1)}, bf16[384,768]{1,0:T(8,128)(2,1)S(1)}, u32[]{:S(2)}, u32[]{:S(2)}) collective-permute-start(bf16[384,768]{1,0:T(8,128)(2,1)S(1)} %collective-permute-done.7.refs_9_.refs_15_), channel_id=1, source_target_pairs={{0,224},{32,0},{64,32},{96,64},{128,96},{160,128},{192,160},{224,1... | collective-permute-start | bytes 1769480 | tf_op jit(solution)/shard_map/ppermute | solution.py:428
  52.4 11.0 %collective-permute-done.2.refs_3_.refs_2_ = bf16[384,768]{1,0:T(8,128)(2,1)S(1)} collective-permute-done((bf16[384,768]{1,0:T(8,128)(2,1)S(1)}, bf16[384,768]{1,0:T(8,128)(2,1)S(1)}, u32[]{:S(2)}, u32[]{:S(2)}) %collective-permute-start.2) | collective-permute-done | bytes 589856 | tf_op jit(solution)/shard_map/ppermute | solution.py:427
  63.4 2.7 %collective-permute-start.11 = (bf16[384,768]{1,0:T(8,128)(2,1)S(1)}, bf16[384,768]{1,0:T(8,128)(2,1)}, u32[]{:S(2)}, u32[]{:S(2)}) collective-permute-start(bf16[384,768]{1,0:T(8,128)(2,1)S(1)} %collective-permute-done.9.refs_11_.refs_14_), channel_id=1, source_target_pairs={{0,224},{32,0},{64,32},{96,64},{128,96},{160,128},{192,160},{224,1... | collective-permute-start | bytes 1769480 | tf_op jit(solution)/shard_map/ppermute | solution.py:428
  66.1 6.7 %collective-permute-done.3.refs_4_.refs_6_ = bf16[384,768]{1,0:T(8,128)(2,1)S(1)} collective-permute-done((bf16[384,768]{1,0:T(8,128)(2,1)S(1)}, bf16[384,768]{1,0:T(8,128)(2,1)S(1)}, u32[]{:S(2)}, u32[]{:S(2)}) %collective-permute-start.3) | collective-permute-done | bytes 589856 | tf_op jit(solution)/shard_map/ppermute | solution.py:428
  72.7 3.4 %collective-permute-start.5 = (bf16[384,768]{1,0:T(8,128)(2,1)S(1)}, bf16[384,768]{1,0:T(8,128)(2,1)S(1)}, u32[]{:S(2)}, u32[]{:S(2)}) collective-permute-start(bf16[384,768]{1,0:T(8,128)(2,1)S(1)} %collective-permute-done.3.refs_4_.refs_6_), channel_id=1, source_target_pairs={{0,224},{32,0},{64,32},{96,64},{128,96},{160,128},{192,160},{224,1... | collective-permute-start | bytes 1769480 | tf_op jit(solution)/shard_map/ppermute | solution.py:428
  76.2 12.5 %collective-permute-done.4.refs_5_.refs_3_ = bf16[384,768]{1,0:T(8,128)(2,1)} collective-permute-done((bf16[384,768]{1,0:T(8,128)(2,1)S(1)}, bf16[384,768]{1,0:T(8,128)(2,1)}, u32[]{:S(2)}, u32[]{:S(2)}) %collective-permute-start.4) | collective-permute-done | bytes 589856 | tf_op jit(solution)/shard_map/ppermute | solution.py:427
  88.7 2.7 %collective-permute-start.13 = (bf16[384,768]{1,0:T(8,128)(2,1)}, bf16[384,768]{1,0:T(8,128)(2,1)}, u32[]{:S(2)}, u32[]{:S(2)}) collective-permute-start(bf16[384,768]{1,0:T(8,128)(2,1)} %collective-permute-done.11.refs_13_), channel_id=1, source_target_pairs={{0,224},{32,0},{64,32},{96,64},{128,96},{160,128},{192,160},{224,1... | collective-permute-start | bytes 1769480 | tf_op jit(solution)/shard_map/ppermute | solution.py:430
  91.3 6.7 %collective-permute-done.5.refs_6_.refs_5_ = bf16[384,768]{1,0:T(8,128)(2,1)S(1)} collective-permute-done((bf16[384,768]{1,0:T(8,128)(2,1)S(1)}, bf16[384,768]{1,0:T(8,128)(2,1)S(1)}, u32[]{:S(2)}, u32[]{:S(2)}) %collective-permute-start.5) | collective-permute-done | bytes 589856 | tf_op jit(solution)/shard_map/ppermute | solution.py:428
  98.9 2.4 %collective-permute-done.10.refs_12_.refs_11_ = bf16[384,768]{1,0:T(8,128)(2,1)} collective-permute-done((bf16[384,768]{1,0:T(8,128)(2,1)S(1)}, bf16[384,768]{1,0:T(8,128)(2,1)}, u32[]{:S(2)}, u32[]{:S(2)}) %collective-permute-start.10) | collective-permute-done | bytes 589856 | tf_op jit(solution)/shard_map/ppermute | solution.py:427
  101.3 4.3 %all-gather.3.cloned.1.call-done.rows_ref.x_ref.dy_ref.prob_ref = bf16[256,24704]{1,0:T(8,128)(2,1)} async-done(((bf16[8,24704]{1,0:T(8,128)(2,1)}), bf16[256,24704]{1,0:T(8,128)(2,1)}) %all-gather.3.cloned.1.call-update) | async-done | bytes 12648464 | tf_op jit(solution)/shard_map/all_gather | solution.py:466
  105.6 6.8 %shard_map.149.sums_ref = f32[256,768]{1,0:T(8,128)} custom-call(bf16[256,24704]{1,0:T(8,128)(2,1)} %all-gather.3.cloned.1.call-done.rows_ref.x_ref.dy_ref.prob_ref, bf16[384,768]{1,0:T(8,128)(2,1)} %get-tuple-element.23.refs_0_, bf16[384,768]{1,0:T(8,128)(2,1)} %copy-done.2, bf16[384,768]{1,0:T(8,128)(2,1)} %copy-done.3, bf16[384,768]{1,0:T(8,128)(2,1)} %copy-done.6, ...), custom_call_target="tpu_custom_call" | custom-call | tf_op jit(solution)/shard_map/pallas_call | solution.py:124
  112.5 1.5 collective-permute-done.12.first_ref.refs_4_
  113.9 3.2 %shard_map.150 = (bf16[256,768]{1,0:T(8,128)(2,1)}, bf16[256,128]{1,0:T(8,128)(2,1)}) custom-call(bf16[256,24704]{1,0:T(8,128)(2,1)} %all-gather.3.cloned.1.call-done.rows_ref.x_ref.dy_ref.prob_ref, bf16[256,24704]{1,0:T(8,128)(2,1)} %all-gather.3.cloned.1.call-done.rows_ref.x_ref.dy_ref.prob_ref, ...), custom_call_target="tpu_custom_call" | custom-call | tf_op jit(solution)/shard_map/pallas_call | solution.py:165
  117.2 7.3 %shard_map.151 = (bf16[128,6272]{1,0:T(8,128)(2,1)}, bf16[128,6272]{1,0:T(8,128)(2,1)}) custom-call(s32[1]{0:T(128)} %bitcast.5.core_ref, bf16[256,768]{1,0:T(8,128)(2,1)} %get-tuple-element.26.acts_ref, bf16[256,128]{1,0:T(8,128)(2,1)} %get-tuple-element.27.prob_ref, bf16[384,768]{1,0:T(8,128)(2,1)} %get-tuple-element.23.refs_0_, ...), custom_call_target="tpu_custom_call" | custom-call | tf_op jit(solution)/shard_map/pallas_call | solution.py:224
  124.6 3.8 %collective-permute-start.14 = (bf16[128,6272]{1,0:T(8,128)(2,1)}, bf16[128,6272]{1,0:T(8,128)(2,1)S(1)}, u32[]{:S(2)}, u32[]{:S(2)}) collective-permute-start(bf16[128,6272]{1,0:T(8,128)(2,1)} %get-tuple-element.29), channel_id=1, source_target_pairs={{0,1},{1,0},{2,3},{3,2},{4,5},{5,4},{6,7},{7,6},{8,9},{9,8},{10,11... | collective-permute-start | bytes 4816904 | tf_op jit(solution)/shard_map/ppermute | solution.py:475
  128.4 3.3 %collective-permute-done.14.b_ref = bf16[128,6272]{1,0:T(8,128)(2,1)S(1)} collective-permute-done((bf16[128,6272]{1,0:T(8,128)(2,1)}, bf16[128,6272]{1,0:T(8,128)(2,1)S(1)}, u32[]{:S(2)}, u32[]{:S(2)}) %collective-permute-start.14) | collective-permute-done | bytes 1605664 | tf_op jit(solution)/shard_map/ppermute | solution.py:475
  131.7 1.4 copy-done
  133.1 1.9 %shard_map.152 = bf16[128,6272]{1,0:T(8,128)(2,1)} custom-call(bf16[128,6272]{1,0:T(8,128)(2,1)S(1)} %copy-done, bf16[128,6272]{1,0:T(8,128)(2,1)S(1)} %collective-permute-done.14.b_ref), custom_call_target="tpu_custom_call" | custom-call | tf_op jit(solution)/shard_map/pallas_call | solution.py:248
  135.0 6.7 %all-to-all-start.1 = ((bf16[16,8,6272]{2,1,0:T(8,128)(2,1)}), bf16[16,8,6272]{2,1,0:T(8,128)(2,1)S(1)}, u32[]{:S(2)}, u32[]{:S(2)}) async-start(bf16[16,8,6272]{2,1,0:T(8,128)(2,1)} %bitcast.8), calls=%async_computation.1 | async-start | bytes 3211264 | tf_op jit(solution)/shard_map/all_to_all | solution.py:477
  141.7 6.2 %shard_map.153.columns_ref = bf16[1536,2048]{1,0:T(8,128)(2,1)} custom-call(bf16[256,24704]{1,0:T(8,128)(2,1)} %all-gather.3.cloned.1.call-done.rows_ref.x_ref.dy_ref.prob_ref), custom_call_target="tpu_custom_call" | custom-call | tf_op jit(solution)/shard_map/pallas_call | solution.py:293
  147.9 16.9 %all-gather.5.cloned.1.call-done.acts_ref = bf16[2048,768]{1,0:T(8,128)(2,1)} async-done(((bf16[256,768]{1,0:T(8,128)(2,1)}), bf16[2048,768]{1,0:T(8,128)(2,1)}) %all-gather.5.cloned.1.call-update) | async-done | bytes 3145744 | tf_op jit(solution)/shard_map/all_gather | solution.py:470
  164.8 6.5 %shard_map.154 = (f32[768,256]{1,0:T(8,128)}, f32[768,256]{1,0:T(8,128)}, f32[256,768]{1,0:T(8,128)}) custom-call(bf16[1536,2048]{1,0:T(8,128)(2,1)} %shard_map.153.columns_ref, bf16[2048,768]{1,0:T(8,128)(2,1)} %all-gather.5.cloned.1.call-done.acts_ref), custom_call_target="tpu_custom_call" | custom-call | tf_op jit(solution)/shard_map/pallas_call | solution.py:343
  172.1 1.8 convolution_convert_fusion
  (49 shorter events, 4.6 us)
Async XLA Ops:
  7.2 98.4 %all-gather.3.cloned.1.call-start = ((), (), s32[]{:S(2)}) async-start(), calls=%async_computation.2 | async-start | bytes 13043712 | tf_op jit(solution)/shard_map/all_gather | solution.py:466
  9.7 23.9 %collective-permute-start = (bf16[384,768]{1,0:T(8,128)(2,1)}, bf16[384,768]{1,0:T(8,128)(2,1)S(1)}, u32[]{:S(2)}, u32[]{:S(2)}) collective-permute-start(bf16[384,768]{1,0:T(8,128)(2,1)} %get-tuple-element.23.refs_0_), channel_id=1, source_target_pairs={{0,32},{32,64},{64,96},{96,128},{128,160},{160,192},{192,224},{224... | collective-permute-start | bytes 1769480 | tf_op jit(solution)/shard_map/ppermute | solution.py:427
  12.2 21.4 %collective-permute-start.1 = (bf16[384,768]{1,0:T(8,128)(2,1)}, bf16[384,768]{1,0:T(8,128)(2,1)S(1)}, u32[]{:S(2)}, u32[]{:S(2)}) collective-permute-start(bf16[384,768]{1,0:T(8,128)(2,1)} %get-tuple-element.23.refs_0_), channel_id=1, source_target_pairs={{0,224},{32,0},{64,32},{96,64},{128,96},{160,128},{192,160},{224,1... | collective-permute-start | bytes 1769480 | tf_op jit(solution)/shard_map/ppermute | solution.py:428
  16.1 19.8 %copy-start.1 = (bf16[384,768]{1,0:T(8,128)(2,1)S(1)}, bf16[384,768]{1,0:T(8,128)(2,1)}, u32[]{:S(2)}) copy-start(bf16[384,768]{1,0:T(8,128)(2,1)} %get-tuple-element.25.refs_7_.refs_8_) | copy-start | bytes 1769476
  33.6 72.0 %copy-start.2 = (bf16[384,768]{1,0:T(8,128)(2,1)}, bf16[384,768]{1,0:T(8,128)(2,1)S(1)}, u32[]{:S(2)}) copy-start(bf16[384,768]{1,0:T(8,128)(2,1)S(1)} %collective-permute-done.refs_1_) | copy-start | bytes 1769476
  33.6 72.0 %copy-start.3 = (bf16[384,768]{1,0:T(8,128)(2,1)}, bf16[384,768]{1,0:T(8,128)(2,1)S(1)}, u32[]{:S(2)}) copy-start(bf16[384,768]{1,0:T(8,128)(2,1)S(1)} %collective-permute-done.1.refs_2_.refs_7_) | copy-start | bytes 1769476
  35.9 129.0 %all-gather.5.cloned.1.call-start = ((), (), s32[]{:S(2)}) async-start(), calls=%async_computation.3 | async-start | bytes 3538944 | tf_op jit(solution)/shard_map/all_gather | solution.py:470
  35.9 12.3 %collective-permute-start.7 = (bf16[384,768]{1,0:T(8,128)(2,1)S(1)}, bf16[384,768]{1,0:T(8,128)(2,1)S(1)}, u32[]{:S(2)}, u32[]{:S(2)}) collective-permute-start(bf16[384,768]{1,0:T(8,128)(2,1)S(1)} %copy-done.1), channel_id=1, source_target_pairs={{0,224},{32,0},{64,32},{96,64},{128,96},{160,128},{192,160},{224,1... | collective-permute-start | bytes 1769480 | tf_op jit(solution)/shard_map/ppermute | solution.py:428
  37.4 13.9 %collective-permute-start.6 = (bf16[384,768]{1,0:T(8,128)(2,1)S(1)}, bf16[384,768]{1,0:T(8,128)(2,1)S(1)}, u32[]{:S(2)}, u32[]{:S(2)}) collective-permute-start(bf16[384,768]{1,0:T(8,128)(2,1)S(1)} %copy-done.1), channel_id=1, source_target_pairs={{0,32},{32,64},{64,96},{96,128},{128,160},{160,192},{192,224},{224... | collective-permute-start | bytes 1769480 | tf_op jit(solution)/shard_map/ppermute | solution.py:427
  38.2 25.2 %collective-permute-start.2 = (bf16[384,768]{1,0:T(8,128)(2,1)S(1)}, bf16[384,768]{1,0:T(8,128)(2,1)S(1)}, u32[]{:S(2)}, u32[]{:S(2)}) collective-permute-start(bf16[384,768]{1,0:T(8,128)(2,1)S(1)} %collective-permute-done.refs_1_), channel_id=1, source_target_pairs={{0,32},{32,64},{64,96},{96,128},{128,160},{160,192},{192,224},{224... | collective-permute-start | bytes 1769480 | tf_op jit(solution)/shard_map/ppermute | solution.py:427
  48.2 57.4 %copy-start.4 = (bf16[384,768]{1,0:T(8,128)(2,1)}, bf16[384,768]{1,0:T(8,128)(2,1)S(1)}, u32[]{:S(2)}) copy-start(bf16[384,768]{1,0:T(8,128)(2,1)S(1)} %collective-permute-done.7.refs_9_.refs_15_) | copy-start | bytes 1769476
  48.2 15.2 %collective-permute-start.9 = (bf16[384,768]{1,0:T(8,128)(2,1)S(1)}, bf16[384,768]{1,0:T(8,128)(2,1)S(1)}, u32[]{:S(2)}, u32[]{:S(2)}) collective-permute-start(bf16[384,768]{1,0:T(8,128)(2,1)S(1)} %collective-permute-done.7.refs_9_.refs_15_), channel_id=1, source_target_pairs={{0,224},{32,0},{64,32},{96,64},{128,96},{160,128},{192,160},{224,1... | collective-permute-start | bytes 1769480 | tf_op jit(solution)/shard_map/ppermute | solution.py:428
  50.9 21.8 %collective-permute-start.3 = (bf16[384,768]{1,0:T(8,128)(2,1)S(1)}, bf16[384,768]{1,0:T(8,128)(2,1)S(1)}, u32[]{:S(2)}, u32[]{:S(2)}) collective-permute-start(bf16[384,768]{1,0:T(8,128)(2,1)S(1)} %collective-permute-done.1.refs_2_.refs_7_), channel_id=1, source_target_pairs={{0,224},{32,0},{64,32},{96,64},{128,96},{160,128},{192,160},{224,1... | collective-permute-start | bytes 1769480 | tf_op jit(solution)/shard_map/ppermute | solution.py:428
  51.3 54.3 %copy-start.5 = (bf16[384,768]{1,0:T(8,128)(2,1)}, bf16[384,768]{1,0:T(8,128)(2,1)S(1)}, u32[]{:S(2)}) copy-start(bf16[384,768]{1,0:T(8,128)(2,1)S(1)} %collective-permute-done.6.refs_8_.refs_9_) | copy-start | bytes 1769476
  51.3 24.8 %collective-permute-start.8 = (bf16[384,768]{1,0:T(8,128)(2,1)S(1)}, bf16[384,768]{1,0:T(8,128)(2,1)S(1)}, u32[]{:S(2)}, u32[]{:S(2)}) collective-permute-start(bf16[384,768]{1,0:T(8,128)(2,1)S(1)} %collective-permute-done.6.refs_8_.refs_9_), channel_id=1, source_target_pairs={{0,32},{32,64},{64,96},{96,128},{128,160},{160,192},{192,224},{224... | collective-permute-start | bytes 1769480 | tf_op jit(solution)/shard_map/ppermute | solution.py:427
  63.4 42.2 %copy-start.6 = (bf16[384,768]{1,0:T(8,128)(2,1)}, bf16[384,768]{1,0:T(8,128)(2,1)S(1)}, u32[]{:S(2)}) copy-start(bf16[384,768]{1,0:T(8,128)(2,1)S(1)} %collective-permute-done.2.refs_3_.refs_2_) | copy-start | bytes 1769476
  63.4 25.3 %collective-permute-start.4 = (bf16[384,768]{1,0:T(8,128)(2,1)S(1)}, bf16[384,768]{1,0:T(8,128)(2,1)}, u32[]{:S(2)}, u32[]{:S(2)}) collective-permute-start(bf16[384,768]{1,0:T(8,128)(2,1)S(1)} %collective-permute-done.2.refs_3_.refs_2_), channel_id=1, source_target_pairs={{0,32},{32,64},{64,96},{96,128},{128,160},{160,192},{192,224},{224... | collective-permute-start | bytes 1769480 | tf_op jit(solution)/shard_map/ppermute | solution.py:427
  63.4 25.3 %copy-start.7 = (bf16[384,768]{1,0:T(8,128)(2,1)}, bf16[384,768]{1,0:T(8,128)(2,1)S(1)}, u32[]{:S(2)}) copy-start(bf16[384,768]{1,0:T(8,128)(2,1)S(1)} %collective-permute-done.9.refs_11_.refs_14_) | copy-start | bytes 1769476
  63.4 25.3 %collective-permute-start.11 = (bf16[384,768]{1,0:T(8,128)(2,1)S(1)}, bf16[384,768]{1,0:T(8,128)(2,1)}, u32[]{:S(2)}, u32[]{:S(2)}) collective-permute-start(bf16[384,768]{1,0:T(8,128)(2,1)S(1)} %collective-permute-done.9.refs_11_.refs_14_), channel_id=1, source_target_pairs={{0,224},{32,0},{64,32},{96,64},{128,96},{160,128},{192,160},{224,1... | collective-permute-start | bytes 1769480 | tf_op jit(solution)/shard_map/ppermute | solution.py:428
  72.7 16.0 %copy-start.8 = (bf16[384,768]{1,0:T(8,128)(2,1)}, bf16[384,768]{1,0:T(8,128)(2,1)S(1)}, u32[]{:S(2)}) copy-start(bf16[384,768]{1,0:T(8,128)(2,1)S(1)} %collective-permute-done.3.refs_4_.refs_6_) | copy-start | bytes 1769476
  72.7 25.3 %collective-permute-start.5 = (bf16[384,768]{1,0:T(8,128)(2,1)S(1)}, bf16[384,768]{1,0:T(8,128)(2,1)S(1)}, u32[]{:S(2)}, u32[]{:S(2)}) collective-permute-start(bf16[384,768]{1,0:T(8,128)(2,1)S(1)} %collective-permute-done.3.refs_4_.refs_6_), channel_id=1, source_target_pairs={{0,224},{32,0},{64,32},{96,64},{128,96},{160,128},{192,160},{224,1... | collective-permute-start | bytes 1769480 | tf_op jit(solution)/shard_map/ppermute | solution.py:428
  76.1 29.5 %copy-start.9 = (bf16[384,768]{1,0:T(8,128)(2,1)}, bf16[384,768]{1,0:T(8,128)(2,1)S(1)}, u32[]{:S(2)}) copy-start(bf16[384,768]{1,0:T(8,128)(2,1)S(1)} %collective-permute-done.8.refs_10_) | copy-start | bytes 1769476
  76.1 25.2 %collective-permute-start.10 = (bf16[384,768]{1,0:T(8,128)(2,1)S(1)}, bf16[384,768]{1,0:T(8,128)(2,1)}, u32[]{:S(2)}, u32[]{:S(2)}) collective-permute-start(bf16[384,768]{1,0:T(8,128)(2,1)S(1)} %collective-permute-done.8.refs_10_), channel_id=1, source_target_pairs={{0,32},{32,64},{64,96},{96,128},{128,160},{160,192},{192,224},{224... | collective-permute-start | bytes 1769480 | tf_op jit(solution)/shard_map/ppermute | solution.py:427
  88.7 25.3 %collective-permute-start.12 = (bf16[384,768]{1,0:T(8,128)(2,1)}, bf16[384,768]{1,0:T(8,128)(2,1)}, u32[]{:S(2)}, u32[]{:S(2)}) collective-permute-start(bf16[384,768]{1,0:T(8,128)(2,1)} %collective-permute-done.4.refs_5_.refs_3_), channel_id=1, source_target_pairs={{0,32},{32,64},{64,96},{96,128},{128,160},{160,192},{192,224},{224... | collective-permute-start | bytes 1769480 | tf_op jit(solution)/shard_map/ppermute | solution.py:430
  88.7 25.3 %collective-permute-start.13 = (bf16[384,768]{1,0:T(8,128)(2,1)}, bf16[384,768]{1,0:T(8,128)(2,1)}, u32[]{:S(2)}, u32[]{:S(2)}) collective-permute-start(bf16[384,768]{1,0:T(8,128)(2,1)} %collective-permute-done.11.refs_13_), channel_id=1, source_target_pairs={{0,224},{32,0},{64,32},{96,64},{128,96},{160,128},{192,160},{224,1... | collective-permute-start | bytes 1769480 | tf_op jit(solution)/shard_map/ppermute | solution.py:430
  98.0 0.8 copy-start.10
  124.6 7.1 %collective-permute-start.14 = (bf16[128,6272]{1,0:T(8,128)(2,1)}, bf16[128,6272]{1,0:T(8,128)(2,1)S(1)}, u32[]{:S(2)}, u32[]{:S(2)}) collective-permute-start(bf16[128,6272]{1,0:T(8,128)(2,1)} %get-tuple-element.29), channel_id=1, source_target_pairs={{0,1},{1,0},{2,3},{3,2},{4,5},{5,4},{6,7},{7,6},{8,9},{9,8},{10,11... | collective-permute-start | bytes 4816904 | tf_op jit(solution)/shard_map/ppermute | solution.py:475
  131.7 1.4 copy-start
  135.0 36.3 %all-to-all-start.1 = ((bf16[16,8,6272]{2,1,0:T(8,128)(2,1)}), bf16[16,8,6272]{2,1,0:T(8,128)(2,1)S(1)}, u32[]{:S(2)}, u32[]{:S(2)}) async-start(bf16[16,8,6272]{2,1,0:T(8,128)(2,1)} %bitcast.8), calls=%async_computation.1 | async-start | bytes 3211264 | tf_op jit(solution)/shard_map/all_to_all | solution.py:477
  171.3 0.8 copy-start.11
Sparse Core Ops, SparseCore 0:
  36.0 69.5 all-gather.2
  117.3 47.4 all-gather.4

commit v8 on v7

--- a/solution.py
+++ b/solution.py
@@ -178,7 +178,7 @@
     )(rows, rows, rows, sums, first, second)
 
 
-def slot_sums(core, acts, prob_lanes, first_parts, second_parts):
+def slot_sums(whose, acts, prob_lanes, first_parts, second_parts):
     rows_half = acts.shape[0] // 2
     count = len(first_parts)
     half, wide = first_parts[0][1].shape
@@ -187,8 +187,8 @@
     first_parts = sorted(first_parts, key=lambda p: p[0])
     second_parts = sorted(second_parts, key=lambda p: p[0])
 
-    def body(core_ref, acts_ref, prob_ref, *refs):
-        weights, give, keep, weights_in, sems = refs[: 2 * count], *refs[2 * count :]
+    def body(whose_ref, acts_ref, prob_ref, *refs):
+        weights, out, weights_in, sems = refs[: 2 * count], *refs[2 * count :]
         copies = []
         for i in range(count):
             for k in range(2):
@@ -199,40 +199,36 @@
                 )
                 copy.start()
                 copies.append(copy)
-        theirs = pl.ds(pl.multiple_of((1 - core_ref[0]) * rows_half, rows_half), rows_half)
-        mine = pl.ds(pl.multiple_of(core_ref[0] * rows_half, rows_half), rows_half)
-        acts = jnp.concatenate([acts_ref[theirs, :both], acts_ref[mine, :both]], axis=0)
+        rows = pl.ds(pl.multiple_of(whose_ref[0] * rows_half, rows_half), rows_half)
+        acts = acts_ref[rows, :both]
 
         def step(i, carry):
             for k in range(2):
-                rows = pl.ds(k * half, half)
+                piece = pl.ds(k * half, half)
                 pltpu.make_async_copy(
-                    weights[0].at[:, pl.ds(0, both)], weights_in.at[i, rows], sems.at[k, i]
+                    weights[0].at[:, pl.ds(0, both)], weights_in.at[i, piece], sems.at[k, i]
                 ).wait()
-            sums = contract(acts, weights_in[i], 1, 1).astype(BF16)
             cols = pl.ds(pl.multiple_of(i * part, BLOCK), part)
-            give[:, cols] = sums[:rows_half]
-            keep[:, cols] = sums[rows_half:]
+            out[:, cols] = contract(acts, weights_in[i], 1, 1).astype(BF16)
             return carry
 
         lax.fori_loop(0, count, step, 0)
-        give[:, width:] = prob_ref[theirs, :]
-        keep[:, width:] = prob_ref[mine, :]
+        out[:, width:] = prob_ref[rows, :]
 
     weights = [w for _, w in first_parts] + [w for _, w in second_parts]
     shape = (rows_half, width + LANES)
     return kernel_call(
         body,
-        (jax.ShapeDtypeStruct(shape, BF16),) * 2,
+        jax.ShapeDtypeStruct(shape, BF16),
         60,
         scalars=1,
         in_specs=[whole(acts.shape), whole(prob_lanes.shape)] + [far_memory()] * (2 * count),
-        out_specs=(whole(shape),) * 2,
+        out_specs=whole(shape),
         scratch_shapes=[
             pltpu.VMEM((count, part, both), BF16),
             pltpu.SemaphoreType.DMA((2, count)),
         ],
-    )(core, acts, prob_lanes, *weights)
+    )(whose, acts, prob_lanes, *weights)
 
 
 def pair_sum(mine, other):
@@ -248,7 +244,7 @@
     return kernel_call(
         body,
         jax.ShapeDtypeStruct(mine.shape, BF16),
-        16,
+        60,
         in_specs=[whole(mine.shape)] * 2,
         out_specs=whole(mine.shape),
     )(mine, other)
@@ -469,16 +465,15 @@
         acts, prob_lanes = activations(rows, width, sums, first_far, second_far)
         all_acts = lax.all_gather(acts, "fsdp", axis=0, tiled=True)
 
-        give, keep = slot_sums(
-            core[None], acts, prob_lanes, [*first_near, first_far], [*second_near, second_far]
-        )
+        sources = (acts, prob_lanes, [*first_near, first_far], [*second_near, second_far])
+        give = slot_sums(1 - core[None], *sources)
         got = lax.ppermute(give, "core", [(0, 1), (1, 0)])
+        keep = slot_sums(core[None], *sources)
         both = pair_sum(keep, got).reshape(-1, CAP, width + LANES)
         shares = lax.all_to_all(both, PLANE, split_axis=0, concat_axis=0, tiled=True)
         grad_gate, grad_up, grad_down = weight_sums(
             turned_columns(rows, 2 * width + LANES, part, ring), all_acts
         )
-        shares, grad_up = lax.optimization_barrier((shares, grad_up))
         table = token_slot == jnp.arange(CAP, dtype=jnp.int32)[:, None]
         mine = jnp.sum(shares.astype(F32), axis=0)
         mine_grad = mine[:, :width].astype(BF16).reshape(CAP, ring, part)

time: 182 us -> 187 us (1.027)
  Pallas kernels: 40.1 us -> 47.8 us
  waiting for transfers between devices: 74 us -> 71.7 us
    all_to_all x1, waiting for transfers between devices: 0.01 us -> 17.9 us  [on_device(): lax.all_to_all(both, PLANE, split_axis=0, concat_axis=0, tiled=True)]
    all_gather x1, waiting for transfers between devices: 16.9 us -> 0.01 us  [on_device(): all_acts = lax.all_gather(acts, 'fsdp', axis=0, tiled=True)]
    pallas_call x2 -> x3, Pallas kernels: 9.21 us -> 16.9 us  [the longest x2 13.2 us: slot_sums(): kernel_call(body, jax.ShapeDtypeStruct(shape, BF16), 60, scalars=1, in_sp...]
    ppermute x1, waiting for transfers between devices: 3.29 us -> 0.01 us  [on_device(): got = lax.ppermute(give, 'core', [(0, 1), (1, 0)])]
  transfers between devices with their start and end apart: 18 -> 18, of which waited for: 10 -> 9; matrix products, arithmetic and copies ran while one was open for 0% -> 2% of each run, Pallas kernels for 18% -> 18%
where the time goes in v8:
time: 187 us
  waiting for transfers between devices  71.7 us (38%)
  Pallas kernels  47.8 us (26%)
  starting transfers between devices  33.6 us (18%)
  between operations  14.3 us (8%)
  blocking collectives  14.1 us (8%)
  local copies, waits for them, and re-layouts  2.27 us (1%)
    ppermute x6, waiting for transfers between devices, ring_gather(): ahead = lax.ppermute(ahead, axis, up)  25.9 us
    ppermute x6, waiting for transfers between devices, ring_gather(): behind = lax.ppermute(behind, axis, down)  22 us
    all_to_all x1, waiting for transfers between devices, on_device(): lax.all_to_all(both, PLANE, split_axis=0, concat_axis=0, tiled=True)  17.9 us
    ppermute x6, starting transfers between devices, ring_gather(): behind = lax.ppermute(behind, axis, down)  14.6 us
    all_to_all x1, blocking collectives, on_device(): lax.all_to_all(sides, 'fsdp', split_axis=0, concat_axis=0, tiled=True)  14.1 us
    pallas_call x2, Pallas kernels, slot_sums(): kernel_call(body, jax.ShapeDtypeStruct(shape, BF16), 60, scalars=1, in_sp...  13.2 us
    pallas_call x1, Pallas kernels, pre_sums(): kernel_call(body, jax.ShapeDtypeStruct(shape, F32), 60, in_specs=[far_mem...  6.83 us
    all_to_all x1, starting transfers between devices, on_device(): lax.all_to_all(both, PLANE, split_axis=0, concat_axis=0, tiled=True)  6.77 us
  transfers between devices with their start and end apart: 18, of which 9 were waited for; matrix products, arithmetic and copies ran while one was open for 2% of the time, Pallas kernels for 18%

profile of v8, /device:TPU:1, one launch (start us, length us, event | category | flops | bytes accessed | tf_op | source)
XLA Modules:
  0.0 186.5 jit_solution(1031750653029635542)
XLA Ops:
  7.2 2.5 %shard_map.147 = (bf16[384,768]{1,0:T(8,128)(2,1)}, bf16[384,768]{1,0:T(8,128)(2,1)}) custom-call(bf16[768,256]{1,0:T(8,128)(2,1)} %gate.1, bf16[768,256]{1,0:T(8,128)(2,1)} %up.1, bf16[256,768]{1,0:T(8,128)(2,1)} %down.1, f32[2,6]{1,0:T(2,128)} %bitcast.18, f32[2,6]{1,0:T(2,128)} %bitcast.19, f32[2,6]{1,0:T(2,128)} %down_s.1), custom_call_target="tpu_custom_call" | custom-call | tf_op jit(solution)/shard_map/pallas_call | solution.py:75
  9.7 2.5 %collective-permute-start = (bf16[384,768]{1,0:T(8,128)(2,1)}, bf16[384,768]{1,0:T(8,128)(2,1)S(1)}, u32[]{:S(2)}, u32[]{:S(2)}) collective-permute-start(bf16[384,768]{1,0:T(8,128)(2,1)} %get-tuple-element.19.refs_0_), channel_id=1, source_target_pairs={{0,32},{32,64},{64,96},{96,128},{128,160},{160,192},{192,224},{224... | collective-permute-start | bytes 1769480 | tf_op jit(solution)/shard_map/ppermute | solution.py:423
  12.2 3.9 %collective-permute-start.1 = (bf16[384,768]{1,0:T(8,128)(2,1)}, bf16[384,768]{1,0:T(8,128)(2,1)S(1)}, u32[]{:S(2)}, u32[]{:S(2)}) collective-permute-start(bf16[384,768]{1,0:T(8,128)(2,1)} %get-tuple-element.19.refs_0_), channel_id=1, source_target_pairs={{0,224},{32,0},{64,32},{96,64},{128,96},{160,128},{192,160},{224,1... | collective-permute-start | bytes 1769480 | tf_op jit(solution)/shard_map/ppermute | solution.py:424
  16.1 3.4 %shard_map.146 = (bf16[8,12416]{1,0:T(8,128)(2,1)}, bf16[8,8,1536]{2,1,0:T(8,128)(2,1)}, s32[1,128]{1,0:T(1,128)}) custom-call(s32[1]{0:T(128)} %bitcast.place_ref, s32[1,128]{1,0:T(1,128)} %bitcast.20, bf16[1,128]{1,0:T(2,128)(2,1)} %bitcast.21, bf16[128,6144]{1,0:T(8,128)(2,1)} %x_ref.1, f32[48,128]{1,0:T(8,128)} %bitcast.17, bf16[128,6144]{1,0:T(8,128)(2,1)} %dy_ref.1), custom_call_target="tpu_custom_call" | custom-call | tf_op jit(solution)/shard_map/pallas_call | solution.py:398
  19.6 14.1 %all_to_all.10.sides_ref = bf16[8,8,1536]{2,1,0:T(8,128)(2,1)} all-to-all(bf16[8,8,1536]{2,1,0:T(8,128)(2,1)} %get-tuple-element.18), channel_id=1, replica_groups=mesh['fsdp'=8,'x'=4,'y'=4,'core'=2] {'fsdp'}, dimensions={0} | all-to-all | bytes 393216 | tf_op jit(solution)/shard_map/all_to_all | solution.py:460
  33.6 2.2 %shard_map.148 = bf16[8,24704]{1,0:T(8,128)(2,1)} custom-call(bf16[8,12416]{1,0:T(8,128)(2,1)} %get-tuple-element.17.packed_ref, bf16[8,8,1536]{2,1,0:T(8,128)(2,1)} %all_to_all.10.sides_ref), custom_call_target="tpu_custom_call" | custom-call | tf_op jit(solution)/shard_map/pallas_call | solution.py:263
  35.9 1.5 collective-permute-start.7
  38.2 1.4 collective-permute-start.2
  39.6 8.7 %collective-permute-done.7.refs_9_.refs_15_ = bf16[384,768]{1,0:T(8,128)(2,1)S(1)} collective-permute-done((bf16[384,768]{1,0:T(8,128)(2,1)S(1)}, bf16[384,768]{1,0:T(8,128)(2,1)S(1)}, u32[]{:S(2)}, u32[]{:S(2)}) %collective-permute-start.7) | collective-permute-done | bytes 589856 | tf_op jit(solution)/shard_map/ppermute | solution.py:424
  48.2 2.7 %collective-permute-start.9 = (bf16[384,768]{1,0:T(8,128)(2,1)S(1)}, bf16[384,768]{1,0:T(8,128)(2,1)S(1)}, u32[]{:S(2)}, u32[]{:S(2)}) collective-permute-start(bf16[384,768]{1,0:T(8,128)(2,1)S(1)} %collective-permute-done.7.refs_9_.refs_15_), channel_id=1, source_target_pairs={{0,224},{32,0},{64,32},{96,64},{128,96},{160,128},{192,160},{224,1... | collective-permute-start | bytes 1769480 | tf_op jit(solution)/shard_map/ppermute | solution.py:424
  52.4 11.0 %collective-permute-done.2.refs_3_.refs_2_ = bf16[384,768]{1,0:T(8,128)(2,1)S(1)} collective-permute-done((bf16[384,768]{1,0:T(8,128)(2,1)S(1)}, bf16[384,768]{1,0:T(8,128)(2,1)S(1)}, u32[]{:S(2)}, u32[]{:S(2)}) %collective-permute-start.2) | collective-permute-done | bytes 589856 | tf_op jit(solution)/shard_map/ppermute | solution.py:423
  63.4 2.7 %collective-permute-start.11 = (bf16[384,768]{1,0:T(8,128)(2,1)S(1)}, bf16[384,768]{1,0:T(8,128)(2,1)}, u32[]{:S(2)}, u32[]{:S(2)}) collective-permute-start(bf16[384,768]{1,0:T(8,128)(2,1)S(1)} %collective-permute-done.9.refs_11_.refs_14_), channel_id=1, source_target_pairs={{0,224},{32,0},{64,32},{96,64},{128,96},{160,128},{192,160},{224,1... | collective-permute-start | bytes 1769480 | tf_op jit(solution)/shard_map/ppermute | solution.py:424
  66.1 6.7 %collective-permute-done.3.refs_4_.refs_6_ = bf16[384,768]{1,0:T(8,128)(2,1)S(1)} collective-permute-done((bf16[384,768]{1,0:T(8,128)(2,1)S(1)}, bf16[384,768]{1,0:T(8,128)(2,1)S(1)}, u32[]{:S(2)}, u32[]{:S(2)}) %collective-permute-start.3) | collective-permute-done | bytes 589856 | tf_op jit(solution)/shard_map/ppermute | solution.py:424
  72.7 3.4 %collective-permute-start.5 = (bf16[384,768]{1,0:T(8,128)(2,1)S(1)}, bf16[384,768]{1,0:T(8,128)(2,1)S(1)}, u32[]{:S(2)}, u32[]{:S(2)}) collective-permute-start(bf16[384,768]{1,0:T(8,128)(2,1)S(1)} %collective-permute-done.3.refs_4_.refs_6_), channel_id=1, source_target_pairs={{0,224},{32,0},{64,32},{96,64},{128,96},{160,128},{192,160},{224,1... | collective-permute-start | bytes 1769480 | tf_op jit(solution)/shard_map/ppermute | solution.py:424
  76.2 12.5 %collective-permute-done.4.refs_5_.refs_3_ = bf16[384,768]{1,0:T(8,128)(2,1)} collective-permute-done((bf16[384,768]{1,0:T(8,128)(2,1)S(1)}, bf16[384,768]{1,0:T(8,128)(2,1)}, u32[]{:S(2)}, u32[]{:S(2)}) %collective-permute-start.4) | collective-permute-done | bytes 589856 | tf_op jit(solution)/shard_map/ppermute | solution.py:423
  88.7 2.7 %collective-permute-start.13 = (bf16[384,768]{1,0:T(8,128)(2,1)}, bf16[384,768]{1,0:T(8,128)(2,1)}, u32[]{:S(2)}, u32[]{:S(2)}) collective-permute-start(bf16[384,768]{1,0:T(8,128)(2,1)} %collective-permute-done.11.refs_13_), channel_id=1, source_target_pairs={{0,224},{32,0},{64,32},{96,64},{128,96},{160,128},{192,160},{224,1... | collective-permute-start | bytes 1769480 | tf_op jit(solution)/shard_map/ppermute | solution.py:426
  91.3 6.7 %collective-permute-done.5.refs_6_.refs_5_ = bf16[384,768]{1,0:T(8,128)(2,1)S(1)} collective-permute-done((bf16[384,768]{1,0:T(8,128)(2,1)S(1)}, bf16[384,768]{1,0:T(8,128)(2,1)S(1)}, u32[]{:S(2)}, u32[]{:S(2)}) %collective-permute-start.5) | collective-permute-done | bytes 589856 | tf_op jit(solution)/shard_map/ppermute | solution.py:424
  98.9 2.4 %collective-permute-done.10.refs_12_.refs_11_ = bf16[384,768]{1,0:T(8,128)(2,1)} collective-permute-done((bf16[384,768]{1,0:T(8,128)(2,1)S(1)}, bf16[384,768]{1,0:T(8,128)(2,1)}, u32[]{:S(2)}, u32[]{:S(2)}) %collective-permute-start.10) | collective-permute-done | bytes 589856 | tf_op jit(solution)/shard_map/ppermute | solution.py:423
  101.3 4.3 %all-gather.3.cloned.1.call-done.rows_ref.x_ref.dy_ref.prob_ref = bf16[256,24704]{1,0:T(8,128)(2,1)} async-done(((bf16[8,24704]{1,0:T(8,128)(2,1)}), bf16[256,24704]{1,0:T(8,128)(2,1)}) %all-gather.3.cloned.1.call-update) | async-done | bytes 12648464 | tf_op jit(solution)/shard_map/all_gather | solution.py:462
  105.6 6.8 %shard_map.149.sums_ref = f32[256,768]{1,0:T(8,128)} custom-call(bf16[256,24704]{1,0:T(8,128)(2,1)} %all-gather.3.cloned.1.call-done.rows_ref.x_ref.dy_ref.prob_ref, bf16[384,768]{1,0:T(8,128)(2,1)} %get-tuple-element.19.refs_0_, bf16[384,768]{1,0:T(8,128)(2,1)} %copy-done.1, bf16[384,768]{1,0:T(8,128)(2,1)} %copy-done.2, bf16[384,768]{1,0:T(8,128)(2,1)} %copy-done.5, ...), custom_call_target="tpu_custom_call" | custom-call | tf_op jit(solution)/shard_map/pallas_call | solution.py:124
  112.5 1.5 collective-permute-done.12.first_ref.refs_4_
  113.9 3.2 %shard_map.150 = (bf16[256,768]{1,0:T(8,128)(2,1)}, bf16[256,128]{1,0:T(8,128)(2,1)}) custom-call(bf16[256,24704]{1,0:T(8,128)(2,1)} %all-gather.3.cloned.1.call-done.rows_ref.x_ref.dy_ref.prob_ref, bf16[256,24704]{1,0:T(8,128)(2,1)} %all-gather.3.cloned.1.call-done.rows_ref.x_ref.dy_ref.prob_ref, ...), custom_call_target="tpu_custom_call" | custom-call | tf_op jit(solution)/shard_map/pallas_call | solution.py:165
  117.2 6.6 %shard_map.152 = bf16[128,6272]{1,0:T(8,128)(2,1)} custom-call(s32[1]{0:T(128)S(6)} %sub.6.whose_ref, bf16[256,768]{1,0:T(8,128)(2,1)} %get-tuple-element.22.acts_ref, bf16[256,128]{1,0:T(8,128)(2,1)} %get-tuple-element.23.prob_ref, bf16[384,768]{1,0:T(8,128)(2,1)} %get-tuple-element.19.refs_0_, bf16[384,768]{1,0:T(8,128)(2,1)} %copy-done.1, ...), custom_call_target="tpu_custom_call" | custom-call | tf_op jit(solution)/shard_map/pallas_call | solution.py:220
  123.8 3.8 %collective-permute-start.14 = (bf16[128,6272]{1,0:T(8,128)(2,1)}, bf16[128,6272]{1,0:T(8,128)(2,1)S(1)}, u32[]{:S(2)}, u32[]{:S(2)}) collective-permute-start(bf16[128,6272]{1,0:T(8,128)(2,1)} %shard_map.152), channel_id=1, source_target_pairs={{0,1},{1,0},{2,3},{3,2},{4,5},{5,4},{6,7},{7,6},{8,9},{9,8},{10,11... | collective-permute-start | bytes 4816904 | tf_op jit(solution)/shard_map/ppermute | solution.py:470
  127.6 6.6 %shard_map.151.a_ref = bf16[128,6272]{1,0:T(8,128)(2,1)} custom-call(s32[1]{0:T(128)} %bitcast.5.whose_ref, bf16[256,768]{1,0:T(8,128)(2,1)} %get-tuple-element.22.acts_ref, bf16[256,128]{1,0:T(8,128)(2,1)} %get-tuple-element.23.prob_ref, bf16[384,768]{1,0:T(8,128)(2,1)} %get-tuple-element.19.refs_0_, bf16[384,768]{1,0:T(8,128)(2,1)} %copy-done.1, ...), custom_call_target="tpu_custom_call" | custom-call | tf_op jit(solution)/shard_map/pallas_call | solution.py:220
  134.2 1.2 copy-done.10
  135.4 3.8 %shard_map.153 = bf16[128,6272]{1,0:T(8,128)(2,1)} custom-call(bf16[128,6272]{1,0:T(8,128)(2,1)} %shard_map.151.a_ref, bf16[128,6272]{1,0:T(8,128)(2,1)} %copy-done.10), custom_call_target="tpu_custom_call" | custom-call | tf_op jit(solution)/shard_map/pallas_call | solution.py:244
  139.2 6.8 %all-to-all-start.1 = ((bf16[16,8,6272]{2,1,0:T(8,128)(2,1)}), bf16[16,8,6272]{2,1,0:T(8,128)(2,1)S(1)}, u32[]{:S(2)}, u32[]{:S(2)}) async-start(bf16[16,8,6272]{2,1,0:T(8,128)(2,1)} %bitcast.14), calls=%async_computation.1 | async-start | bytes 3211264 | tf_op jit(solution)/shard_map/all_to_all | solution.py:473
  145.9 6.2 %shard_map.154.columns_ref = bf16[1536,2048]{1,0:T(8,128)(2,1)} custom-call(bf16[256,24704]{1,0:T(8,128)(2,1)} %all-gather.3.cloned.1.call-done.rows_ref.x_ref.dy_ref.prob_ref), custom_call_target="tpu_custom_call" | custom-call | tf_op jit(solution)/shard_map/pallas_call | solution.py:289
  152.2 17.9 %all-to-all-done.1 = bf16[16,8,6272]{2,1,0:T(8,128)(2,1)S(1)} async-done(((bf16[16,8,6272]{2,1,0:T(8,128)(2,1)}), bf16[16,8,6272]{2,1,0:T(8,128)(2,1)S(1)}, u32[]{:S(2)}, u32[]{:S(2)}) %all-to-all-start.1) | async-done | bytes 1605664 | tf_op jit(solution)/shard_map/all_to_all | solution.py:473
  171.4 1.8 convolution_convert_fusion
  173.2 6.5 %shard_map.155 = (f32[768,256]{1,0:T(8,128)}, f32[768,256]{1,0:T(8,128)}, f32[256,768]{1,0:T(8,128)}) custom-call(bf16[1536,2048]{1,0:T(8,128)(2,1)} %shard_map.154.columns_ref, bf16[2048,768]{1,0:T(8,128)(2,1)} %all-gather.5.cloned.1.call-done.acts_ref), custom_call_target="tpu_custom_call" | custom-call | tf_op jit(solution)/shard_map/pallas_call | solution.py:339
  (50 shorter events, 4.6 us)
Async XLA Ops:
  7.2 98.4 %all-gather.3.cloned.1.call-start = ((), (), s32[]{:S(2)}) async-start(), calls=%async_computation.2 | async-start | bytes 13043712 | tf_op jit(solution)/shard_map/all_gather | solution.py:462
  9.7 23.9 %collective-permute-start = (bf16[384,768]{1,0:T(8,128)(2,1)}, bf16[384,768]{1,0:T(8,128)(2,1)S(1)}, u32[]{:S(2)}, u32[]{:S(2)}) collective-permute-start(bf16[384,768]{1,0:T(8,128)(2,1)} %get-tuple-element.19.refs_0_), channel_id=1, source_target_pairs={{0,32},{32,64},{64,96},{96,128},{128,160},{160,192},{192,224},{224... | collective-permute-start | bytes 1769480 | tf_op jit(solution)/shard_map/ppermute | solution.py:423
  12.2 21.4 %collective-permute-start.1 = (bf16[384,768]{1,0:T(8,128)(2,1)}, bf16[384,768]{1,0:T(8,128)(2,1)S(1)}, u32[]{:S(2)}, u32[]{:S(2)}) collective-permute-start(bf16[384,768]{1,0:T(8,128)(2,1)} %get-tuple-element.19.refs_0_), channel_id=1, source_target_pairs={{0,224},{32,0},{64,32},{96,64},{128,96},{160,128},{192,160},{224,1... | collective-permute-start | bytes 1769480 | tf_op jit(solution)/shard_map/ppermute | solution.py:424
  16.1 19.8 %copy-start = (bf16[384,768]{1,0:T(8,128)(2,1)S(1)}, bf16[384,768]{1,0:T(8,128)(2,1)}, u32[]{:S(2)}) copy-start(bf16[384,768]{1,0:T(8,128)(2,1)} %get-tuple-element.21.refs_7_.refs_8_) | copy-start | bytes 1769476
  33.6 72.0 %copy-start.1 = (bf16[384,768]{1,0:T(8,128)(2,1)}, bf16[384,768]{1,0:T(8,128)(2,1)S(1)}, u32[]{:S(2)}) copy-start(bf16[384,768]{1,0:T(8,128)(2,1)S(1)} %collective-permute-done.refs_1_) | copy-start | bytes 1769476
  33.6 72.0 %copy-start.2 = (bf16[384,768]{1,0:T(8,128)(2,1)}, bf16[384,768]{1,0:T(8,128)(2,1)S(1)}, u32[]{:S(2)}) copy-start(bf16[384,768]{1,0:T(8,128)(2,1)S(1)} %collective-permute-done.1.refs_2_.refs_7_) | copy-start | bytes 1769476
  35.9 137.3 %all-gather.5.cloned.1.call-start = ((), (), s32[]{:S(2)}) async-start(), calls=%async_computation.3 | async-start | bytes 3538944 | tf_op jit(solution)/shard_map/all_gather | solution.py:466
  35.9 12.3 %collective-permute-start.7 = (bf16[384,768]{1,0:T(8,128)(2,1)S(1)}, bf16[384,768]{1,0:T(8,128)(2,1)S(1)}, u32[]{:S(2)}, u32[]{:S(2)}) collective-permute-start(bf16[384,768]{1,0:T(8,128)(2,1)S(1)} %copy-done), channel_id=1, source_target_pairs={{0,224},{32,0},{64,32},{96,64},{128,96},{160,128},{192,160},{224,1... | collective-permute-start | bytes 1769480 | tf_op jit(solution)/shard_map/ppermute | solution.py:424
  37.4 13.9 %collective-permute-start.6 = (bf16[384,768]{1,0:T(8,128)(2,1)S(1)}, bf16[384,768]{1,0:T(8,128)(2,1)S(1)}, u32[]{:S(2)}, u32[]{:S(2)}) collective-permute-start(bf16[384,768]{1,0:T(8,128)(2,1)S(1)} %copy-done), channel_id=1, source_target_pairs={{0,32},{32,64},{64,96},{96,128},{128,160},{160,192},{192,224},{224... | collective-permute-start | bytes 1769480 | tf_op jit(solution)/shard_map/ppermute | solution.py:423
  38.2 25.2 %collective-permute-start.2 = (bf16[384,768]{1,0:T(8,128)(2,1)S(1)}, bf16[384,768]{1,0:T(8,128)(2,1)S(1)}, u32[]{:S(2)}, u32[]{:S(2)}) collective-permute-start(bf16[384,768]{1,0:T(8,128)(2,1)S(1)} %collective-permute-done.refs_1_), channel_id=1, source_target_pairs={{0,32},{32,64},{64,96},{96,128},{128,160},{160,192},{192,224},{224... | collective-permute-start | bytes 1769480 | tf_op jit(solution)/shard_map/ppermute | solution.py:423
  48.2 57.4 %copy-start.3 = (bf16[384,768]{1,0:T(8,128)(2,1)}, bf16[384,768]{1,0:T(8,128)(2,1)S(1)}, u32[]{:S(2)}) copy-start(bf16[384,768]{1,0:T(8,128)(2,1)S(1)} %collective-permute-done.7.refs_9_.refs_15_) | copy-start | bytes 1769476
  48.2 15.2 %collective-permute-start.9 = (bf16[384,768]{1,0:T(8,128)(2,1)S(1)}, bf16[384,768]{1,0:T(8,128)(2,1)S(1)}, u32[]{:S(2)}, u32[]{:S(2)}) collective-permute-start(bf16[384,768]{1,0:T(8,128)(2,1)S(1)} %collective-permute-done.7.refs_9_.refs_15_), channel_id=1, source_target_pairs={{0,224},{32,0},{64,32},{96,64},{128,96},{160,128},{192,160},{224,1... | collective-permute-start | bytes 1769480 | tf_op jit(solution)/shard_map/ppermute | solution.py:424
  50.9 21.8 %collective-permute-start.3 = (bf16[384,768]{1,0:T(8,128)(2,1)S(1)}, bf16[384,768]{1,0:T(8,128)(2,1)S(1)}, u32[]{:S(2)}, u32[]{:S(2)}) collective-permute-start(bf16[384,768]{1,0:T(8,128)(2,1)S(1)} %collective-permute-done.1.refs_2_.refs_7_), channel_id=1, source_target_pairs={{0,224},{32,0},{64,32},{96,64},{128,96},{160,128},{192,160},{224,1... | collective-permute-start | bytes 1769480 | tf_op jit(solution)/shard_map/ppermute | solution.py:424
  51.3 54.3 %copy-start.4 = (bf16[384,768]{1,0:T(8,128)(2,1)}, bf16[384,768]{1,0:T(8,128)(2,1)S(1)}, u32[]{:S(2)}) copy-start(bf16[384,768]{1,0:T(8,128)(2,1)S(1)} %collective-permute-done.6.refs_8_.refs_9_) | copy-start | bytes 1769476
  51.3 24.8 %collective-permute-start.8 = (bf16[384,768]{1,0:T(8,128)(2,1)S(1)}, bf16[384,768]{1,0:T(8,128)(2,1)S(1)}, u32[]{:S(2)}, u32[]{:S(2)}) collective-permute-start(bf16[384,768]{1,0:T(8,128)(2,1)S(1)} %collective-permute-done.6.refs_8_.refs_9_), channel_id=1, source_target_pairs={{0,32},{32,64},{64,96},{96,128},{128,160},{160,192},{192,224},{224... | collective-permute-start | bytes 1769480 | tf_op jit(solution)/shard_map/ppermute | solution.py:423
  63.4 42.2 %copy-start.5 = (bf16[384,768]{1,0:T(8,128)(2,1)}, bf16[384,768]{1,0:T(8,128)(2,1)S(1)}, u32[]{:S(2)}) copy-start(bf16[384,768]{1,0:T(8,128)(2,1)S(1)} %collective-permute-done.2.refs_3_.refs_2_) | copy-start | bytes 1769476
  63.4 25.3 %collective-permute-start.4 = (bf16[384,768]{1,0:T(8,128)(2,1)S(1)}, bf16[384,768]{1,0:T(8,128)(2,1)}, u32[]{:S(2)}, u32[]{:S(2)}) collective-permute-start(bf16[384,768]{1,0:T(8,128)(2,1)S(1)} %collective-permute-done.2.refs_3_.refs_2_), channel_id=1, source_target_pairs={{0,32},{32,64},{64,96},{96,128},{128,160},{160,192},{192,224},{224... | collective-permute-start | bytes 1769480 | tf_op jit(solution)/shard_map/ppermute | solution.py:423
  63.4 25.3 %copy-start.6 = (bf16[384,768]{1,0:T(8,128)(2,1)}, bf16[384,768]{1,0:T(8,128)(2,1)S(1)}, u32[]{:S(2)}) copy-start(bf16[384,768]{1,0:T(8,128)(2,1)S(1)} %collective-permute-done.9.refs_11_.refs_14_) | copy-start | bytes 1769476
  63.4 25.3 %collective-permute-start.11 = (bf16[384,768]{1,0:T(8,128)(2,1)S(1)}, bf16[384,768]{1,0:T(8,128)(2,1)}, u32[]{:S(2)}, u32[]{:S(2)}) collective-permute-start(bf16[384,768]{1,0:T(8,128)(2,1)S(1)} %collective-permute-done.9.refs_11_.refs_14_), channel_id=1, source_target_pairs={{0,224},{32,0},{64,32},{96,64},{128,96},{160,128},{192,160},{224,1... | collective-permute-start | bytes 1769480 | tf_op jit(solution)/shard_map/ppermute | solution.py:424
  72.7 16.0 %copy-start.7 = (bf16[384,768]{1,0:T(8,128)(2,1)}, bf16[384,768]{1,0:T(8,128)(2,1)S(1)}, u32[]{:S(2)}) copy-start(bf16[384,768]{1,0:T(8,128)(2,1)S(1)} %collective-permute-done.3.refs_4_.refs_6_) | copy-start | bytes 1769476
  72.7 25.3 %collective-permute-start.5 = (bf16[384,768]{1,0:T(8,128)(2,1)S(1)}, bf16[384,768]{1,0:T(8,128)(2,1)S(1)}, u32[]{:S(2)}, u32[]{:S(2)}) collective-permute-start(bf16[384,768]{1,0:T(8,128)(2,1)S(1)} %collective-permute-done.3.refs_4_.refs_6_), channel_id=1, source_target_pairs={{0,224},{32,0},{64,32},{96,64},{128,96},{160,128},{192,160},{224,1... | collective-permute-start | bytes 1769480 | tf_op jit(solution)/shard_map/ppermute | solution.py:424
  76.1 29.5 %copy-start.8 = (bf16[384,768]{1,0:T(8,128)(2,1)}, bf16[384,768]{1,0:T(8,128)(2,1)S(1)}, u32[]{:S(2)}) copy-start(bf16[384,768]{1,0:T(8,128)(2,1)S(1)} %collective-permute-done.8.refs_10_) | copy-start | bytes 1769476
  76.1 25.2 %collective-permute-start.10 = (bf16[384,768]{1,0:T(8,128)(2,1)S(1)}, bf16[384,768]{1,0:T(8,128)(2,1)}, u32[]{:S(2)}, u32[]{:S(2)}) collective-permute-start(bf16[384,768]{1,0:T(8,128)(2,1)S(1)} %collective-permute-done.8.refs_10_), channel_id=1, source_target_pairs={{0,32},{32,64},{64,96},{96,128},{128,160},{160,192},{192,224},{224... | collective-permute-start | bytes 1769480 | tf_op jit(solution)/shard_map/ppermute | solution.py:423
  88.7 25.3 %collective-permute-start.12 = (bf16[384,768]{1,0:T(8,128)(2,1)}, bf16[384,768]{1,0:T(8,128)(2,1)}, u32[]{:S(2)}, u32[]{:S(2)}) collective-permute-start(bf16[384,768]{1,0:T(8,128)(2,1)} %collective-permute-done.4.refs_5_.refs_3_), channel_id=1, source_target_pairs={{0,32},{32,64},{64,96},{96,128},{128,160},{160,192},{192,224},{224... | collective-permute-start | bytes 1769480 | tf_op jit(solution)/shard_map/ppermute | solution.py:426
  88.7 25.3 %collective-permute-start.13 = (bf16[384,768]{1,0:T(8,128)(2,1)}, bf16[384,768]{1,0:T(8,128)(2,1)}, u32[]{:S(2)}, u32[]{:S(2)}) collective-permute-start(bf16[384,768]{1,0:T(8,128)(2,1)} %collective-permute-done.11.refs_13_), channel_id=1, source_target_pairs={{0,224},{32,0},{64,32},{96,64},{128,96},{160,128},{192,160},{224,1... | collective-permute-start | bytes 1769480 | tf_op jit(solution)/shard_map/ppermute | solution.py:426
  98.0 0.8 copy-start.9
  123.8 10.4 %collective-permute-start.14 = (bf16[128,6272]{1,0:T(8,128)(2,1)}, bf16[128,6272]{1,0:T(8,128)(2,1)S(1)}, u32[]{:S(2)}, u32[]{:S(2)}) collective-permute-start(bf16[128,6272]{1,0:T(8,128)(2,1)} %shard_map.152), channel_id=1, source_target_pairs={{0,1},{1,0},{2,3},{3,2},{4,5},{5,4},{6,7},{7,6},{8,9},{9,8},{10,11... | collective-permute-start | bytes 4816904 | tf_op jit(solution)/shard_map/ppermute | solution.py:470
  134.2 1.2 copy-start.10
  139.2 30.9 %all-to-all-start.1 = ((bf16[16,8,6272]{2,1,0:T(8,128)(2,1)}), bf16[16,8,6272]{2,1,0:T(8,128)(2,1)S(1)}, u32[]{:S(2)}, u32[]{:S(2)}) async-start(bf16[16,8,6272]{2,1,0:T(8,128)(2,1)} %bitcast.14), calls=%async_computation.1 | async-start | bytes 3211264 | tf_op jit(solution)/shard_map/all_to_all | solution.py:473
  152.2 18.7 %copy-start.11 = (s32[1,128]{1,0:T(1,128)S(1)}, s32[1,128]{1,0:T(1,128)}, u32[]{:S(2)}) copy-start(s32[1,128]{1,0:T(1,128)} %get-tuple-element.16) | copy-start | bytes 1540
Sparse Core Ops, SparseCore 0:
  36.0 69.5 all-gather.2
  117.3 47.4 all-gather.4
